TPU v7x, 512 devices: a whole 4x4x16 slice. The times are simulated.
512 devices in a mesh: section: 8 (over z_lo, core), tensor: 16 (over y, z_hi), dp: 4 (over x).
Axes of the slice: x: 4, y: 4, z: 16 (z_hi: 4, z_lo: 4; z = z_hi * 4 + z_lo), core: 2. Of those that a mesh axis runs over, the one named last changes fastest.
Arguments:
- plan: int32 [8, 2], P('section'), may hold values from 0 to 1, each once within a row
- stashed: bfloat16 [8, 2, 1024, 8192], P('section', None, 'dp', 'tensor'), may hold values from -400 to 400
- norm_gain: bfloat16 [8, 8192], P('section', 'tensor'), may hold values from 0.099609375 to 1.8984375
- kv_weight: bfloat16 [8, 8192, 2048], P('section', 'tensor'), may hold values from -0.0625 to 0.0625
- kv_grad: bfloat16 [8, 2, 1024, 2048], P('section', None, ('dp', 'tensor')), may hold values from -4 to 4
- top_grad: bfloat16 [2, 1024, 8192], P(None, 'dp', 'tensor'), may hold values from -1.5 to 1.5
Outputs:
- input_grads: bfloat16 [8, 2, 1024, 8192], P('section', None, 'dp', 'tensor')
- weight_grads: bfloat16 [8, 8192, 2048], P('section', 'tensor', 'dp')
Inputs may be any that keep to these rules, and one draw needn't show every extreme that they name: Each row of plan is a permutation of the micro-batch numbers.
All inputs are finite; a program needn't handle non-finite values.
Results may differ from a plain program's by a relative error of at most 0.0049.
Values may be sent and summed in bfloat16 or wider, within the bound.
No kernel may reach another device: no remote copies, remote signals or barrier semaphores. Data moves between devices by JAX's collectives and lax.ppermute only.
A program may use at most 64 MiB of HBM per device.

v0:
```python
import jax
import jax.numpy as jnp
from jax import lax
from jax.sharding import PartitionSpec as P

EPSILON = 1e-06


def carried_in(value, axis, combine, identity):
    size, index = (lax.axis_size(axis), lax.axis_index(axis))
    everything = lax.all_gather(value, axis)
    start = jnp.broadcast_to(jnp.asarray(identity, value.dtype), value.shape)

    def hop(k, before):
        at = size - 1 - k
        reached = at > index
        new = combine(before, everything[at])
        return jnp.where(reached, new, before)

    return lax.fori_loop(0, size, hop, start)


def add_terms(earlier, later_part):
    return earlier + later_part


def shards(plan, stashed, norm_gain, kv_weight, kv_grad, top_grad):
    micro_count = plan.shape[1]
    slot_ids = jnp.arange(micro_count, dtype=jnp.int32)
    matches = plan[0][None, :] == slot_ids[:, None]
    where_slot = jnp.sum(jnp.where(matches, slot_ids[None, :], 0), axis=1)
    hidden_in = jnp.take(stashed[0], where_slot, axis=0).astype(jnp.float32)
    gains = norm_gain[0].astype(jnp.float32)
    model_width = lax.axis_size("tensor") * hidden_in.shape[-1]
    data_count = lax.axis_size("dp")
    kv_rows = lax.all_gather(kv_grad[0], "tensor", axis=1, tiled=True)
    flat_grads = kv_rows.reshape(-1, kv_rows.shape[-1])
    weight = kv_weight[0]
    squares_part = jnp.sum(hidden_in * hidden_in, -1)
    total_squares = lax.psum(squares_part, "tensor")
    row_rms = jnp.sqrt(total_squares / model_width + EPSILON)
    normed = (gains * hidden_in / row_rms[..., None]).astype(jnp.bfloat16)
    flat_normed = normed.reshape(-1, normed.shape[-1])
    local_weight = lax.dot_general(
        flat_normed, flat_grads, (((0,), (0,)), ((), ())), preferred_element_type=jnp.float32
    )
    summed = lax.psum_scatter(local_weight, "dp", scatter_dimension=1, tiled=True)
    weight_grads = (summed / (micro_count * data_count)).astype(jnp.bfloat16)[None]
    product = lax.dot_general(
        flat_grads, weight, (((1,), (1,)), ((), ())), preferred_element_type=jnp.float32
    )
    normed_grad = product.reshape(hidden_in.shape)
    aligned = lax.psum(jnp.sum(gains * normed_grad * hidden_in, -1), "tensor")
    contrib = (
        gains * normed_grad / row_rms[..., None]
        - hidden_in * (aligned / (model_width * row_rms**3))[..., None]
    )
    from_above = carried_in(contrib, "section", add_terms, jnp.zeros_like(contrib))
    summed_above = from_above + contrib
    input_grads = (top_grad.astype(jnp.float32) + summed_above).astype(jnp.bfloat16)[None]
    return (input_grads, weight_grads)


def solution(mesh):
    in_specs = (
        P("section", None),
        P("section", None, "dp", "tensor"),
        P("section", "tensor"),
        P("section", "tensor", None),
        P("section", None, ("dp", "tensor"), None),
        P(None, "dp", "tensor"),
    )
    out_specs = (P("section", None, "dp", "tensor"), P("section", "tensor", "dp"))
    return jax.shard_map(shards, mesh=mesh, in_specs=in_specs, out_specs=out_specs, check_vma=False)
```

profile of v0, /device:TPU:1, one launch (start us, length us, event | category | flops | bytes accessed | tf_op | source)
XLA Modules:
  0.0 337.1 jit_solution(9317897947338051104)
XLA Ops:
  7.2 0.0 copy-start
  7.2 0.0 all-gather.5.cloned.1.call-start
  7.2 0.7 all-gather.5.cloned.1.call-update
  7.9 0.0 reduce-scatter.2.cloned.1.call-start
  8.0 0.7 convert_element_type.32
  8.6 0.8 fusion.21
  9.4 1.6 gather_fusion
  11.1 99.7 %all-gather.5.cloned.1.call-done = bf16[1,2,256,2048]{3,2,1,0:T(8,128)(2,1)} async-done(((bf16[1,2,16,2048]{3,2,1,0:T(8,128)(2,1)}), bf16[1,2,256,2048]{3,2,1,0:T(8,128)(2,1)}) %all-gather.5.cloned.1.call-update) | async-done | bytes 2097168 | tf_op jit(solution)/shard_map/all_gather | solution.py:36
  110.8 0.0 copy-done
  110.8 3.9 %fusion.9 = (f32[2,256]{1,0:T(2,128)S(1)}, f32[2,256]{1,0:T(2,128)S(1)}, f32[2,256,512]{2,1,0:T(8,128)}) fusion(bf16[2,256,512]{2,1,0:T(8,128)(2,1)S(1)} %gather_fusion, pred[2]{0:T(512)(128)(4,1)S(1)} %compare_and_fusion, bf16[1,512,2048]{2,1,0:T(8,128)(2,1)S(1)} %copy-done, bf16[1,2,256,2048]{3,2,1,0:T(8,128)(2,1)} %all-gather.5.cloned.1.call-done, ...), kind=kOutput, calls=%fused_computation.12 | convolution fusion | flops 1075575808 | bytes 5773314 | tf_op jit(solution)/shard_map/dot_general | solution.py:49
  114.7 43.8 %all-reduce = (f32[2,256]{1,0:T(2,128)S(1)}, f32[2,256]{1,0:T(2,128)S(1)}) all-reduce(f32[2,256]{1,0:T(2,128)S(1)} %get-tuple-element.129, f32[2,256]{1,0:T(2,128)S(1)} %get-tuple-element.128), channel_id=1, replica_groups=mesh['section'=8,'tensor'=16,'dp'=4] {'tensor'}, use_global_device_ids=true, to_apply=%region_4.5 | all-reduce | flops 1024 | bytes 8192 | tf_op jit(solution)/shard_map/psum | solution.py:53
  158.5 5.0 %convolution_bitcast_fusion = f32[512,2048]{1,0:T(8,128)} fusion(bf16[1,2,256,2048]{3,2,1,0:T(8,128)(2,1)} %all-gather.5.cloned.1.call-done, f32[2,256]{1,0:T(2,128)S(1)} %get-tuple-element.140, f32[512]{0:T(512)S(1)} %bitcast.38, bf16[2,256,512]{2,1,0:T(8,128)(2,1)S(1)} %gather_fusion, pred[2]{0:T(512)(128)(4,1)S(1)} %compare_and_fusion), kind=kOutput, calls=%fused_computation.2 | convolution fusion | flops 1075052544 | bytes 6819842 | tf_op jit(solution)/shard_map/dot_general | solution.py:44
  163.5 0.0 reduce-scatter.2.cloned.1.call-update
  163.5 0.0 all-gather.7.cloned.1.call-start
  163.5 2.5 fusion.11
  166.1 0.0 all-gather.7.cloned.1.call-update
  166.1 50.2 %reduce-scatter.2.cloned.1.call-done = f32[512,512]{1,0:T(8,128)} async-done(((f32[512,2048]{1,0:T(8,128)}), f32[512,512]{1,0:T(8,128)}) %reduce-scatter.2.cloned.1.call-update) | async-done | bytes 1048592 | tf_op jit(solution)/shard_map/reduce_scatter | solution.py:47
  216.3 2.1 fusion.16
  218.4 96.7 %all-gather.7.cloned.1.call-done = f32[16,256,512]{2,1,0:T(8,128)} async-done(((f32[2,256,512]{2,1,0:T(8,128)}), f32[16,256,512]{2,1,0:T(8,128)}) %all-gather.7.cloned.1.call-update) | async-done | bytes 8388624 | tf_op jit(solution)/shard_map/all_gather | solution.py:11
  315.2 13.0 %while.16 = (s32[]{:T(128)}, f32[2,256,512]{2,1,0:T(8,128)S(1)}, s32[]{:T(128)}, f32[8,2,256,512]{3,2,1,0:T(8,128)}, s32[]{:T(128)}, /*index=5*/s32[]{:T(128)}, s32[]{:T(128)}, s32[]{:T(128)}) while((s32[]{:T(128)}, f32[2,256,512]{2,1,0:T(8,128)S(1)}, s32[]{:T(128)}, f32[8,2,256,512]{3,2,1,0:T(8,128)}, s32[]{:T(128)}, ...), condition=%wide.region_6.7_spmd.clone, body=%wide.region_5.6_spmd.clone.sunk | while | flops 786440 | bytes 3145883 | solution.py:20
  315.2 1.6 add_select_fusion.2
  316.8 1.6 add_select_fusion.2
  318.4 1.6 add_select_fusion.2
  320.0 1.6 add_select_fusion.2
  321.7 1.6 add_select_fusion.2
  323.3 1.6 add_select_fusion.2
  324.9 1.6 add_select_fusion.2
  326.5 1.6 add_select_fusion.2
  328.1 2.4 fusion.15
  (5 shorter events, 0.0 us)
Async XLA Ops:
  7.2 103.6 %copy-start = (bf16[1,512,2048]{2,1,0:T(8,128)(2,1)S(1)}, bf16[1,512,2048]{2,1,0:T(8,128)(2,1)}, u32[]{:S(2)}) copy-start(bf16[1,512,2048]{2,1,0:T(8,128)(2,1)} %param.11) | copy-start | bytes 6291460
  7.2 103.6 %all-gather.5.cloned.1.call-start = ((), (), s32[]{:S(2)}) async-start(), calls=%async_computation.2 | async-start | bytes 2228224 | tf_op jit(solution)/shard_map/all_gather | solution.py:36
  7.9 208.4 %reduce-scatter.2.cloned.1.call-start = ((), (), s32[]{:S(2)}) async-start(), calls=%async_computation.1 | async-start | bytes 5242880 | tf_op jit(solution)/shard_map/reduce_scatter | solution.py:47
  163.5 151.7 %all-gather.7.cloned.1.call-start = ((), (), s32[]{:S(2)}) async-start(), calls=%async_computation.3 | async-start | bytes 9437184 | tf_op jit(solution)/shard_map/all_gather | solution.py:11
Sparse Core Ops, SparseCore 0:
  11.1 99.6 all-gather.4
  163.6 52.6 reduce-scatter.1
  218.6 96.5 all-gather.6
where the time goes:
time: 339 us; the launch traced here: 337 us
  waiting for transfers between devices  247 us (73%)
  blocking collectives  43.8 us (13%)
  other arithmetic  21.3 us (6%)
  between operations  13.8 us (4%)
  matrix products  8.82 us (3%)
    all_gather x1, waiting for transfers between devices, shards(): kv_rows = lax.all_gather(kv_grad[0], 'tensor', axis=1, tiled=True)  99.7 us
    all_gather x1, waiting for transfers between devices, carried_in(): everything = lax.all_gather(value, axis)  96.7 us
    reduce_scatter x1, waiting for transfers between devices, shards(): lax.psum_scatter(local_weight, 'dp', scatter_dimension=1, tiled=True)  50.2 us
    psum x1, blocking collectives, shards(): aligned = lax.psum(jnp.sum(gains * normed_grad * hidden_in, -1), 'tensor')  43.8 us
    select_n x8, other arithmetic, hop(): return jnp.where(reached, new, before)  12.7 us
  transfers between devices with their start and end apart: 3, of which 3 were waited for; matrix products, arithmetic and copies ran while one was open for 2% of the time, Pallas kernels for 0%

commit v1 on v0

v1 whole, which is shorter than its diff:
```python
import jax
import jax.numpy as jnp
from jax import lax
from jax.sharding import PartitionSpec as P

EPSILON = 1e-06
NY, NZ = 4, 4


def y_groups():
    return [[y * NZ + z for y in range(NY)] for z in range(NZ)]


def z_groups():
    return [[y * NZ + z for z in range(NZ)] for y in range(NY)]


def from_z(value, step):
    perm = [(y * NZ + (z + step) % NZ, y * NZ + z) for y in range(NY) for z in range(NZ)]
    return lax.ppermute(value, "tensor", perm)


def from_other_core(value):
    return lax.ppermute(value, "section", [(s, s ^ 1) for s in range(8)])


def from_chips_above(value, chips):
    return lax.ppermute(value, "section", [(s, s - 2 * chips) for s in range(2 * chips, 8)])


def to_all(value, axis, groups, count):
    spread = jnp.broadcast_to(value, (count,) + value.shape)
    return lax.all_to_all(spread, axis, 0, 0, axis_index_groups=groups)


def tensor_sum(value):
    value = jnp.sum(to_all(value, "tensor", y_groups(), NY), axis=0)
    return jnp.sum(to_all(value, "tensor", z_groups(), NZ), axis=0)


def shards(plan, stashed, norm_gain, kv_weight, kv_grad, top_grad):
    section = lax.axis_index("section")
    core = section % 2
    tz = lax.axis_index("tensor") % NZ
    width = stashed.shape[-1]
    model_width = lax.axis_size("tensor") * width
    data_count = lax.axis_size("dp")
    micro_count = plan.shape[1]
    rows = kv_grad.shape[2]
    tokens = micro_count * NY * NZ * rows

    def roll_z(value, by):
        return lax.dynamic_slice_in_dim(jnp.concatenate([value, value], axis=1), by % NZ, NZ, axis=1)

    def turned(value):
        value = value.reshape(micro_count, NY, NZ, rows, width).transpose(1, 2, 0, 3, 4)
        return roll_z(value, tz).reshape(tokens, width)

    def absolute(value):
        return roll_z(value.reshape(NY, NZ, -1), NZ - tz).reshape(-1, 128)

    def relative(value):
        return roll_z(value.reshape(NY, NZ, -1), tz).reshape(tokens)

    kv0 = kv_grad[0]
    z_parts = [from_z(kv0, d) for d in (1, 2, 3)]
    kv_own = to_all(kv0, "tensor", y_groups(), NY)
    kv_others = to_all(jnp.stack(z_parts), "tensor", y_groups(), NY)

    slots = jnp.where(plan[0, 0] == 0, stashed[0], stashed[0][::-1])
    hidden16 = turned(slots)
    hidden_all = lax.all_gather(hidden16, "section")
    hidden = hidden16.astype(jnp.float32)
    top = turned(top_grad)
    gains = norm_gain[0].astype(jnp.float32)
    squares = tensor_sum(absolute(jnp.sum(hidden * hidden, -1)))
    row_rms = jnp.sqrt(relative(squares) / model_width + EPSILON)
    normed = (gains * hidden / row_rms[:, None]).astype(jnp.bfloat16)

    def split(value):
        value = value.reshape((NY, NZ, micro_count * rows) + value.shape[1:])
        return value[:, :1], value[:, 1:]

    weight = kv_weight[0]
    flat_own = kv_own.reshape(-1, kv_own.shape[-1])
    flat_others = kv_others.reshape(-1, kv_own.shape[-1])

    def back(flat):
        product = lax.dot_general(
            flat, weight, (((1,), (1,)), ((), ())), preferred_element_type=jnp.float32
        )
        return product.reshape(NY, -1, micro_count * rows, width)

    normed_grad = jnp.concatenate([back(flat_own), back(flat_others)], axis=1).reshape(tokens, width)
    gained = gains * normed_grad
    aligned_part = jnp.sum(gained * hidden, -1)
    direct = gained / row_rms[:, None]
    direct16 = direct.astype(jnp.bfloat16)

    other = from_other_core(direct16).astype(jnp.float32)
    halves = (direct + other).reshape(2, tokens // 2, width)
    half = lax.dynamic_index_in_dim(halves, core, 0, keepdims=False).astype(jnp.bfloat16)
    above = sum(from_chips_above(half, d).astype(jnp.float32) for d in (1, 2, 3))
    above_other = from_other_core(above.astype(jnp.bfloat16)).astype(jnp.float32)
    first = core == 0
    above_all = jnp.concatenate([jnp.where(first, above, above_other), jnp.where(first, above_other, above)])

    aligned = relative(tensor_sum(absolute(aligned_part)))
    scale = (aligned / (model_width * row_rms**3)).reshape(-1, 128)
    scales = to_all(scale, "section", None, 8).reshape(8, tokens)
    later = jnp.arange(8)[:, None] >= section
    scales = jnp.where(later, scales, 0.0)
    correction = jnp.sum(hidden_all.astype(jnp.float32) * scales[:, :, None], axis=0)
    total = top.astype(jnp.float32) + direct + jnp.where(first, other, 0.0) + above_all - correction
    out = roll_z(total.astype(jnp.bfloat16).reshape(NY, NZ, micro_count, rows, width), NZ - tz)
    input_grads = out.transpose(2, 0, 1, 3, 4).reshape(1, micro_count, NY * NZ * rows, width)

    normed_own, normed_others = split(normed)

    def outer(left, right):
        return lax.dot_general(
            left.reshape(-1, width), right, (((0,), (0,)), ((), ())), preferred_element_type=jnp.float32
        )

    local_weight = outer(normed_own, flat_own) + outer(normed_others, flat_others)
    pieces = local_weight.astype(jnp.bfloat16).reshape(width, data_count, -1).transpose(1, 0, 2)
    got = lax.all_to_all(pieces, "dp", 0, 0)
    summed = jnp.sum(got.astype(jnp.float32), axis=0)
    weight_grads = (summed / (micro_count * data_count)).astype(jnp.bfloat16)[None]
    return (input_grads, weight_grads)


def solution(mesh):
    in_specs = (
        P("section", None),
        P("section", None, "dp", "tensor"),
        P("section", "tensor"),
        P("section", "tensor", None),
        P("section", None, ("dp", "tensor"), None),
        P(None, "dp", "tensor"),
    )
    out_specs = (P("section", None, "dp", "tensor"), P("section", "tensor", "dp"))
    return jax.shard_map(shards, mesh=mesh, in_specs=in_specs, out_specs=out_specs, check_vma=False)
```

time: 339 us -> 218 us (0.64)
  waiting for transfers between devices: 247 us -> 85.7 us
  starting transfers between devices: 0.12 us -> 75.7 us
  blocking collectives: 43.8 us -> 0 us
  local copies, waits for them, and re-layouts: 1.63 us -> 13.6 us
  other arithmetic: 21.3 us -> 17.9 us
    all_gather x2 -> x1, waiting for transfers between devices: 196 us -> 0.01 us  [shards(): hidden_all = lax.all_gather(hidden16, 'section')]
    reduce_scatter x1 -> x0, waiting for transfers between devices: 50.2 us -> none  [shards(): lax.psum_scatter(local_weight, 'dp', scatter_dimension=1, tiled=True)]
    all_to_all x0 -> x8, waiting for transfers between devices: none -> 48.5 us  [the longest x7 48.5 us: to_all(): return lax.all_to_all(spread, axis, 0, 0, axis_index_groups=groups)]
    psum x1 -> x0, blocking collectives: 43.8 us -> none  [shards(): aligned = lax.psum(jnp.sum(gains * normed_grad * hidden_in, -1), 'tensor')]
    all_to_all x0 -> x8, starting transfers between devices: none -> 42.8 us  [the longest x7 38.3 us: to_all(): return lax.all_to_all(spread, axis, 0, 0, axis_index_groups=groups)]
    ppermute x0 -> x8, waiting for transfers between devices: none -> 37.3 us  [the longest x3 19.1 us: from_z(): return lax.ppermute(value, 'tensor', perm)]
    ppermute x0 -> x8, starting transfers between devices: none -> 32.9 us  [the longest x3 24.6 us: from_z(): return lax.ppermute(value, 'tensor', perm)]
    select_n x9 -> x3, other arithmetic: 12.7 us -> 2.28 us  [the longest x1 2.11 us: shards(): jnp.where(first, above, above_other)]
  transfers between devices with their start and end apart: 3 -> 17, of which waited for: 3 -> 9; matrix products, arithmetic and copies ran while one was open for 2% -> 11% of each run, Pallas kernels for 0% -> 0%
where the time goes in v1:
time: 218 us; the launch traced here: 214 us
  waiting for transfers between devices  85.7 us (39%)
  starting transfers between devices  75.7 us (35%)
  other arithmetic  17.9 us (8%)
  between operations  14.6 us (7%)
  local copies, waits for them, and re-layouts  13.6 us (6%)
  matrix products  6.75 us (3%)
    all_to_all x7, waiting for transfers between devices, to_all(): return lax.all_to_all(spread, axis, 0, 0, axis_index_groups=groups)  48.5 us
    all_to_all x7, starting transfers between devices, to_all(): return lax.all_to_all(spread, axis, 0, 0, axis_index_groups=groups)  38.3 us
    ppermute x3, starting transfers between devices, from_z(): return lax.ppermute(value, 'tensor', perm)  24.6 us
    ppermute x3, waiting for transfers between devices, from_z(): return lax.ppermute(value, 'tensor', perm)  19.1 us
    ppermute x3, waiting for transfers between devices, from_chips_above(): lax.ppermute(value, 'section', [(s, s - 2 * chips) for s in range(2 * chi...  18.2 us
    broadcast_in_dim x7, local copies, waits for them, and re-layouts, to_all(): spread = jnp.broadcast_to(value, (count,) + value.shape)  6.28 us
    all_to_all x1, starting transfers between devices, shards(): got = lax.all_to_all(pieces, 'dp', 0, 0)  4.44 us
    ppermute x2, starting transfers between devices, from_other_core(): return lax.ppermute(value, 'section', [(s, s ^ 1) for s in range(8)])  4.36 us
  transfers between devices with their start and end apart: 17, of which 9 were waited for; matrix products, arithmetic and copies ran while one was open for 11% of the time, Pallas kernels for 0%

profile of v1, /device:TPU:1, one launch (start us, length us, event | category | flops | bytes accessed | tf_op | source)
XLA Modules:
  0.0 214.3 jit_solution(13526018152849407148)
XLA Ops:
  7.2 1.9 broadcast_in_dim.44
  9.1 5.0 %all-to-all-start = ((bf16[4,2,16,2048]{3,2,1,0:T(8,128)(2,1)}), bf16[4,2,16,2048]{3,2,1,0:T(8,128)(2,1)S(1)}, u32[]{:S(2)}, u32[]{:S(2)}) async-start(bf16[4,2,16,2048]{3,2,1,0:T(8,128)(2,1)} %broadcast_in_dim.44), calls=%async_computation | async-start | bytes 1048576 | tf_op jit(solution)/shard_map/all_to_all | solution.py:33
  14.1 8.8 %collective-permute-start.2 = (bf16[2,16,2048]{2,1,0:T(8,128)(2,1)}, bf16[2,16,2048]{2,1,0:T(8,128)(2,1)S(1)}, u32[]{:S(2)}, u32[]{:S(2)}) collective-permute-start(bf16[2,16,2048]{2,1,0:T(8,128)(2,1)} %bitcast.102), channel_id=1, source_target_pairs={{12,0},{0,4},{4,8},{8,12},{28,16},{16,20},{20,24},{24,28},{44,32},... | collective-permute-start | bytes 393224 | tf_op jit(solution)/shard_map/ppermute | solution.py:20
  22.9 10.6 %collective-permute-start.1 = (bf16[2,16,2048]{2,1,0:T(8,128)(2,1)}, bf16[2,16,2048]{2,1,0:T(8,128)(2,1)S(1)}, u32[]{:S(2)}, u32[]{:S(2)}) collective-permute-start(bf16[2,16,2048]{2,1,0:T(8,128)(2,1)} %bitcast.103), channel_id=1, source_target_pairs={{8,0},{12,4},{0,8},{4,12},{24,16},{28,20},{16,24},{20,28},{40,32},... | collective-permute-start | bytes 393224 | tf_op jit(solution)/shard_map/ppermute | solution.py:20
  33.6 5.2 %collective-permute-start = (bf16[2,16,2048]{2,1,0:T(8,128)(2,1)}, bf16[2,16,2048]{2,1,0:T(8,128)(2,1)S(1)}, u32[]{:S(2)}, u32[]{:S(2)}) collective-permute-start(bf16[2,16,2048]{2,1,0:T(8,128)(2,1)} %bitcast.104), channel_id=1, source_target_pairs={{4,0},{8,4},{12,8},{0,12},{20,16},{24,20},{28,24},{16,28},{36,32},... | collective-permute-start | bytes 393224 | tf_op jit(solution)/shard_map/ppermute | solution.py:20
  38.8 12.1 %collective-permute-done.1 = bf16[2,16,2048]{2,1,0:T(8,128)(2,1)S(1)} collective-permute-done((bf16[2,16,2048]{2,1,0:T(8,128)(2,1)}, bf16[2,16,2048]{2,1,0:T(8,128)(2,1)S(1)}, u32[]{:S(2)}, u32[]{:S(2)}) %collective-permute-start.1) | collective-permute-done | bytes 131104 | tf_op jit(solution)/shard_map/ppermute | solution.py:20
  50.8 7.0 %collective-permute-done = bf16[2,16,2048]{2,1,0:T(8,128)(2,1)S(1)} collective-permute-done((bf16[2,16,2048]{2,1,0:T(8,128)(2,1)}, bf16[2,16,2048]{2,1,0:T(8,128)(2,1)S(1)}, u32[]{:S(2)}, u32[]{:S(2)}) %collective-permute-start) | collective-permute-done | bytes 131104 | tf_op jit(solution)/shard_map/ppermute | solution.py:20
  57.9 1.4 broadcast_in_dim.45
  59.3 4.5 %all-to-all-start.1 = ((bf16[4,3,2,16,2048]{4,3,2,1,0:T(8,128)(2,1)}), bf16[4,3,2,16,2048]{4,3,2,1,0:T(8,128)(2,1)}, u32[]{:S(2)}, u32[]{:S(2)}) async-start(bf16[4,3,2,16,2048]{4,3,2,1,0:T(8,128)(2,1)} %broadcast_in_dim.45), calls=%async_computation.1 | async-start | bytes 3145728 | tf_op jit(solution)/shard_map/all_to_all | solution.py:33
  64.1 0.8 fusion.2
  64.9 18.9 %all-to-all-done.1 = bf16[4,3,2,16,2048]{4,3,2,1,0:T(8,128)(2,1)} async-done(((bf16[4,3,2,16,2048]{4,3,2,1,0:T(8,128)(2,1)}), bf16[4,3,2,16,2048]{4,3,2,1,0:T(8,128)(2,1)}, u32[]{:S(2)}, u32[]{:S(2)}) %all-to-all-start.1) | async-done | bytes 1572896 | tf_op jit(solution)/shard_map/all_to_all | solution.py:33
  83.8 2.4 %fusion = f32[4,3,32,512]{3,2,1,0:T(8,128)S(1)} fusion(bf16[4,3,32,2048]{3,2,1,0:T(8,128)(2,1)} %bitcast.13, bf16[1,512,2048]{2,1,0:T(8,128)(2,1)S(1)} %copy-done), kind=kOutput, calls=%fused_computation.4 | convolution fusion | flops 805306368 | bytes 4456448 | tf_op jit(solution)/shard_map/dot_general | solution.py:89
  86.3 0.9 copy-done.4
  87.2 1.2 multiply_reduce_fusion.1
  89.3 3.2 %all-to-all-start.2 = ((f32[4,4,128]{2,1,0:T(4,128)}), f32[4,4,128]{2,1,0:T(4,128)S(1)}, u32[]{:S(2)}, u32[]{:S(2)}) async-start(f32[4,4,128]{2,1,0:T(4,128)} %broadcast_in_dim.46), calls=%async_computation.2 | async-start | bytes 16384 | tf_op jit(solution)/shard_map/all_to_all | solution.py:33
  92.6 4.0 %all-to-all-done.2 = f32[4,4,128]{2,1,0:T(4,128)S(1)} async-done(((f32[4,4,128]{2,1,0:T(4,128)}), f32[4,4,128]{2,1,0:T(4,128)S(1)}, u32[]{:S(2)}, u32[]{:S(2)}) %all-to-all-start.2) | async-done | bytes 8224 | tf_op jit(solution)/shard_map/all_to_all | solution.py:33
  97.3 3.2 %all-to-all-start.4 = ((f32[4,4,128]{2,1,0:T(4,128)}), f32[4,4,128]{2,1,0:T(4,128)S(1)}, u32[]{:S(2)}, u32[]{:S(2)}) async-start(f32[4,4,128]{2,1,0:T(4,128)} %broadcast_in_dim.50), calls=%async_computation.4 | async-start | bytes 16384 | tf_op jit(solution)/shard_map/all_to_all | solution.py:33
  100.6 4.1 %all-to-all-done.4 = f32[4,4,128]{2,1,0:T(4,128)S(1)} async-done(((f32[4,4,128]{2,1,0:T(4,128)}), f32[4,4,128]{2,1,0:T(4,128)S(1)}, u32[]{:S(2)}, u32[]{:S(2)}) %all-to-all-start.4) | async-done | bytes 8224 | tf_op jit(solution)/shard_map/all_to_all | solution.py:33
  105.3 9.4 %all-to-all-start.3 = ((f32[4,4,128]{2,1,0:T(4,128)}), f32[4,4,128]{2,1,0:T(4,128)S(1)}, u32[]{:S(2)}, u32[]{:S(2)}) async-start(f32[4,4,128]{2,1,0:T(4,128)} %broadcast_in_dim.47), calls=%async_computation.3 | async-start | bytes 16384 | tf_op jit(solution)/shard_map/all_to_all | solution.py:33
  114.7 1.2 pad_maximum_fusion
  115.9 10.2 %all-to-all-done.3 = f32[4,4,128]{2,1,0:T(4,128)S(1)} async-done(((f32[4,4,128]{2,1,0:T(4,128)}), f32[4,4,128]{2,1,0:T(4,128)S(1)}, u32[]{:S(2)}, u32[]{:S(2)}) %all-to-all-start.3) | async-done | bytes 8224 | tf_op jit(solution)/shard_map/all_to_all | solution.py:33
  126.8 3.2 %all-to-all-start.5 = ((f32[4,4,128]{2,1,0:T(4,128)}), f32[4,4,128]{2,1,0:T(4,128)S(1)}, u32[]{:S(2)}, u32[]{:S(2)}) async-start(f32[4,4,128]{2,1,0:T(4,128)} %broadcast_in_dim.51), calls=%async_computation.5 | async-start | bytes 16384 | tf_op jit(solution)/shard_map/all_to_all | solution.py:33
  130.3 11.1 %all-to-all-done.5 = f32[4,4,128]{2,1,0:T(4,128)S(1)} async-done(((f32[4,4,128]{2,1,0:T(4,128)}), f32[4,4,128]{2,1,0:T(4,128)S(1)}, u32[]{:S(2)}, u32[]{:S(2)}) %all-to-all-start.5) | async-done | bytes 8224 | tf_op jit(solution)/shard_map/all_to_all | solution.py:33
  142.3 9.7 %all-to-all-start.6 = ((f32[8,4,128]{2,1,0:T(4,128)}), f32[8,4,128]{2,1,0:T(4,128)S(1)}, u32[]{:S(2)}, u32[]{:S(2)}) async-start(f32[8,4,128]{2,1,0:T(4,128)} %broadcast_in_dim.52), calls=%async_computation.6 | async-start | bytes 32768 | tf_op jit(solution)/shard_map/all_to_all | solution.py:33
  152.0 0.9 fusion.29
  152.9 2.0 collective-permute-start.3
  155.0 1.2 fusion.11
  156.2 0.7 fusion.31
  157.0 2.8 %add_convert_fusion = bf16[512,2048]{1,0:T(8,128)(2,1)S(1)} fusion(f32[512,2048]{1,0:T(8,128)S(1)} %fusion.31, bf16[384,512]{1,0:T(8,128)(2,1)S(1)} %bitcast.95, bf16[384,2048]{1,0:T(8,128)(2,1)} %bitcast.34), kind=kOutput, calls=%fused_computation.2 | convolution fusion | flops 807403520 | bytes 8257536 | tf_op jit(solution)/shard_map/dot_general | solution.py:121
  159.7 1.5 copy.36
  161.2 4.4 %all-to-all-start.7 = ((bf16[4,512,512]{2,1,0:T(8,128)(2,1)}), bf16[4,512,512]{2,1,0:T(8,128)(2,1)}, u32[]{:S(2)}, u32[]{:S(2)}) async-start(bf16[4,512,512]{2,1,0:T(8,128)(2,1)} %bitcast.84), calls=%async_computation.7 | async-start | bytes 4194304 | tf_op jit(solution)/shard_map/all_to_all | solution.py:127
  165.7 1.4 convert_add_fusion
  167.1 1.3 collective-permute-start.6
  168.4 1.3 collective-permute-start.5
  169.7 1.3 collective-permute-start.4
  171.0 1.2 fusion.17
  172.3 6.1 %collective-permute-done.6 = bf16[256,512]{1,0:T(8,128)(2,1)S(1)} collective-permute-done((bf16[256,512]{1,0:T(8,128)(2,1)S(1)}, bf16[256,512]{1,0:T(8,128)(2,1)S(1)}, u32[]{:S(2)}, u32[]{:S(2)}) %collective-permute-start.6) | collective-permute-done | bytes 262176 | tf_op jit(solution)/shard_map/ppermute | solution.py:28
  178.4 12.0 %collective-permute-done.5 = bf16[256,512]{1,0:T(8,128)(2,1)S(1)} collective-permute-done((bf16[256,512]{1,0:T(8,128)(2,1)S(1)}, bf16[256,512]{1,0:T(8,128)(2,1)S(1)}, u32[]{:S(2)}, u32[]{:S(2)}) %collective-permute-start.5) | collective-permute-done | bytes 262176 | tf_op jit(solution)/shard_map/ppermute | solution.py:28
  190.5 0.7 copy-done.7
  191.1 0.8 fusion.19
  192.0 2.3 %collective-permute-start.7 = (bf16[256,512]{1,0:T(8,128)(2,1)}, bf16[256,512]{1,0:T(8,128)(2,1)}, u32[]{:S(2)}, u32[]{:S(2)}) collective-permute-start(bf16[256,512]{1,0:T(8,128)(2,1)} %fusion.19), channel_id=1, source_target_pairs={{0,64},{64,0},{128,192},{192,128},{256,320},{320,256},{384,448},{4... | collective-permute-start | bytes 786440 | tf_op jit(solution)/shard_map/ppermute | solution.py:24
  194.4 2.5 %copy.21 = f32[4,4,2,16,512]{4,3,2,1,0:T(8,128)} copy(f32[4,4,2,16,512]{4,3,1,0,2:T(8,128)} %fusion.17) | data formatting | bytes 2097152 | tf_op jit(solution)/shard_map/convert_element_type | solution.py:114
  196.9 2.1 convert_select_fusion.2
  199.0 2.0 convert_reduce_fusion
  201.0 0.9 fusion.13
  202.0 2.9 %multiply_reduce_fusion = f32[512,512]{1,0:T(8,128)S(1)} fusion(bf16[8,512,512]{2,1,0:T(8,128)(2,1)} %all-gather.2.cloned.1.call-done, f32[8,512]{1,0:T(8,128)S(1)} %bitcast_select_fusion), kind=kLoop, calls=%fused_computation | loop fusion | flops 6029312 | bytes 5259264 | tf_op jit(solution)/shard_map/reduce_sum | solution.py:113
  204.9 1.5 fusion.7
  206.6 0.8 copy.30
  (70 shorter events, 4.6 us)
Async XLA Ops:
  7.2 56.9 %copy-start = (bf16[1,512,2048]{2,1,0:T(8,128)(2,1)S(1)}, bf16[1,512,2048]{2,1,0:T(8,128)(2,1)}, u32[]{:S(2)}) copy-start(bf16[1,512,2048]{2,1,0:T(8,128)(2,1)} %param.9) | copy-start | bytes 6291460
  9.1 48.8 %all-to-all-start = ((bf16[4,2,16,2048]{3,2,1,0:T(8,128)(2,1)}), bf16[4,2,16,2048]{3,2,1,0:T(8,128)(2,1)S(1)}, u32[]{:S(2)}, u32[]{:S(2)}) async-start(bf16[4,2,16,2048]{3,2,1,0:T(8,128)(2,1)} %broadcast_in_dim.44), calls=%async_computation | async-start | bytes 1048576 | tf_op jit(solution)/shard_map/all_to_all | solution.py:33
  14.1 24.7 %collective-permute-start.2 = (bf16[2,16,2048]{2,1,0:T(8,128)(2,1)}, bf16[2,16,2048]{2,1,0:T(8,128)(2,1)S(1)}, u32[]{:S(2)}, u32[]{:S(2)}) collective-permute-start(bf16[2,16,2048]{2,1,0:T(8,128)(2,1)} %bitcast.102), channel_id=1, source_target_pairs={{12,0},{0,4},{4,8},{8,12},{28,16},{16,20},{20,24},{24,28},{44,32},... | collective-permute-start | bytes 393224 | tf_op jit(solution)/shard_map/ppermute | solution.py:20
  22.9 27.9 %collective-permute-start.1 = (bf16[2,16,2048]{2,1,0:T(8,128)(2,1)}, bf16[2,16,2048]{2,1,0:T(8,128)(2,1)S(1)}, u32[]{:S(2)}, u32[]{:S(2)}) collective-permute-start(bf16[2,16,2048]{2,1,0:T(8,128)(2,1)} %bitcast.103), channel_id=1, source_target_pairs={{8,0},{12,4},{0,8},{4,12},{24,16},{28,20},{16,24},{20,28},{40,32},... | collective-permute-start | bytes 393224 | tf_op jit(solution)/shard_map/ppermute | solution.py:20
  33.6 24.3 %collective-permute-start = (bf16[2,16,2048]{2,1,0:T(8,128)(2,1)}, bf16[2,16,2048]{2,1,0:T(8,128)(2,1)S(1)}, u32[]{:S(2)}, u32[]{:S(2)}) collective-permute-start(bf16[2,16,2048]{2,1,0:T(8,128)(2,1)} %bitcast.104), channel_id=1, source_target_pairs={{4,0},{8,4},{12,8},{0,12},{20,16},{24,20},{28,24},{16,28},{36,32},... | collective-permute-start | bytes 393224 | tf_op jit(solution)/shard_map/ppermute | solution.py:20
  57.9 6.0 %copy-start.13 = (bf16[1,512]{1,0:T(2,128)(2,1)S(1)}, bf16[1,512]{1,0:T(2,128)(2,1)}, u32[]{:S(2)}) copy-start(bf16[1,512]{1,0:T(2,128)(2,1)} %param.8) | copy-start | bytes 3076
  57.9 6.0 %copy-start.14 = (s32[1,2]{1,0:T(1,128)S(1)}, s32[1,2]{1,0:T(1,128)}, u32[]{:S(2)}) copy-start(s32[1,2]{1,0:T(1,128)} %param.6) | copy-start | bytes 28
  57.9 6.2 %copy-start.1 = (bf16[4,2,16,2048]{3,2,1,0:T(8,128)(2,1)}, bf16[4,2,16,2048]{3,2,1,0:T(8,128)(2,1)S(1)}, u32[]{:S(2)}) copy-start(bf16[4,2,16,2048]{3,2,1,0:T(8,128)(2,1)S(1)} %all-to-all-done) | copy-start | bytes 1572868
  59.3 4.6 %copy-start.12 = (bf16[1,2,256,512]{3,2,1,0:T(8,128)(2,1)S(1)}, bf16[1,2,256,512]{3,2,1,0:T(8,128)(2,1)}, u32[]{:S(2)}) copy-start(bf16[1,2,256,512]{3,2,1,0:T(8,128)(2,1)} %param.7) | copy-start | bytes 1572868
  59.3 24.5 %all-to-all-start.1 = ((bf16[4,3,2,16,2048]{4,3,2,1,0:T(8,128)(2,1)}), bf16[4,3,2,16,2048]{4,3,2,1,0:T(8,128)(2,1)}, u32[]{:S(2)}, u32[]{:S(2)}) async-start(bf16[4,3,2,16,2048]{4,3,2,1,0:T(8,128)(2,1)} %broadcast_in_dim.45), calls=%async_computation.1 | async-start | bytes 3145728 | tf_op jit(solution)/shard_map/all_to_all | solution.py:33
  63.8 138.2 %all-gather.2.cloned.1.call-start = ((), (), s32[]{:S(2)}) async-start(), calls=%async_computation.8 | async-start | bytes 4718592 | tf_op jit(solution)/shard_map/all_gather | solution.py:72
  86.3 0.9 copy-start.4
  89.3 7.4 %all-to-all-start.2 = ((f32[4,4,128]{2,1,0:T(4,128)}), f32[4,4,128]{2,1,0:T(4,128)S(1)}, u32[]{:S(2)}, u32[]{:S(2)}) async-start(f32[4,4,128]{2,1,0:T(4,128)} %broadcast_in_dim.46), calls=%async_computation.2 | async-start | bytes 16384 | tf_op jit(solution)/shard_map/all_to_all | solution.py:33
  97.3 7.4 %all-to-all-start.4 = ((f32[4,4,128]{2,1,0:T(4,128)}), f32[4,4,128]{2,1,0:T(4,128)S(1)}, u32[]{:S(2)}, u32[]{:S(2)}) async-start(f32[4,4,128]{2,1,0:T(4,128)} %broadcast_in_dim.50), calls=%async_computation.4 | async-start | bytes 16384 | tf_op jit(solution)/shard_map/all_to_all | solution.py:33
  105.3 20.9 %all-to-all-start.3 = ((f32[4,4,128]{2,1,0:T(4,128)}), f32[4,4,128]{2,1,0:T(4,128)S(1)}, u32[]{:S(2)}, u32[]{:S(2)}) async-start(f32[4,4,128]{2,1,0:T(4,128)} %broadcast_in_dim.47), calls=%async_computation.3 | async-start | bytes 16384 | tf_op jit(solution)/shard_map/all_to_all | solution.py:33
  126.8 14.7 %all-to-all-start.5 = ((f32[4,4,128]{2,1,0:T(4,128)}), f32[4,4,128]{2,1,0:T(4,128)S(1)}, u32[]{:S(2)}, u32[]{:S(2)}) async-start(f32[4,4,128]{2,1,0:T(4,128)} %broadcast_in_dim.51), calls=%async_computation.5 | async-start | bytes 16384 | tf_op jit(solution)/shard_map/all_to_all | solution.py:33
  142.3 18.9 %all-to-all-start.6 = ((f32[8,4,128]{2,1,0:T(4,128)}), f32[8,4,128]{2,1,0:T(4,128)S(1)}, u32[]{:S(2)}, u32[]{:S(2)}) async-start(f32[8,4,128]{2,1,0:T(4,128)} %broadcast_in_dim.52), calls=%async_computation.6 | async-start | bytes 32768 | tf_op jit(solution)/shard_map/all_to_all | solution.py:33
  152.0 4.2 %copy-start.2 = (bf16[4,2,16,2048]{3,2,1,0:T(8,128)(2,1)S(1)}, bf16[4,2,16,2048]{3,2,1,0:T(8,128)(2,1)}, u32[]{:S(2)}) copy-start(bf16[4,2,16,2048]{3,2,1,0:T(8,128)(2,1)} %copy-done.1) | copy-start | bytes 1572868
  152.9 12.8 %collective-permute-start.3 = (bf16[512,512]{1,0:T(8,128)(2,1)}, bf16[512,512]{1,0:T(8,128)(2,1)}, u32[]{:S(2)}, u32[]{:S(2)}) collective-permute-start(bf16[512,512]{1,0:T(8,128)(2,1)} %fusion.29), channel_id=1, source_target_pairs={{0,64},{64,0},{128,192},{192,128},{256,320},{320,256},{384,448},{4... | collective-permute-start | bytes 1572872 | tf_op jit(solution)/shard_map/ppermute | solution.py:24
  161.2 37.8 %all-to-all-start.7 = ((bf16[4,512,512]{2,1,0:T(8,128)(2,1)}), bf16[4,512,512]{2,1,0:T(8,128)(2,1)}, u32[]{:S(2)}, u32[]{:S(2)}) async-start(bf16[4,512,512]{2,1,0:T(8,128)(2,1)} %bitcast.84), calls=%async_computation.7 | async-start | bytes 4194304 | tf_op jit(solution)/shard_map/all_to_all | solution.py:127
  165.7 5.3 %copy-start.11 = (bf16[2,256,512]{2,1,0:T(8,128)(2,1)S(1)}, bf16[2,256,512]{2,1,0:T(8,128)(2,1)}, u32[]{:S(2)}) copy-start(bf16[2,256,512]{2,1,0:T(8,128)(2,1)} %param.11) | copy-start | bytes 1572868
  167.1 11.3 %collective-permute-start.6 = (bf16[256,512]{1,0:T(8,128)(2,1)S(1)}, bf16[256,512]{1,0:T(8,128)(2,1)S(1)}, u32[]{:S(2)}, u32[]{:S(2)}) collective-permute-start(bf16[256,512]{1,0:T(8,128)(2,1)S(1)} %fusion.18), channel_id=1, source_target_pairs={{384,0},{448,64},{385,1},{449,65},{386,2},{450,66},{387,3},{451,67... | collective-permute-start | bytes 786440 | tf_op jit(solution)/shard_map/ppermute | solution.py:28
  168.4 22.0 %collective-permute-start.5 = (bf16[256,512]{1,0:T(8,128)(2,1)S(1)}, bf16[256,512]{1,0:T(8,128)(2,1)S(1)}, u32[]{:S(2)}, u32[]{:S(2)}) collective-permute-start(bf16[256,512]{1,0:T(8,128)(2,1)S(1)} %fusion.18), channel_id=1, source_target_pairs={{256,0},{320,64},{384,128},{448,192},{257,1},{321,65},{385,129},{4... | collective-permute-start | bytes 786440 | tf_op jit(solution)/shard_map/ppermute | solution.py:28
  169.7 20.7 %collective-permute-start.4 = (bf16[256,512]{1,0:T(8,128)(2,1)S(1)}, bf16[256,512]{1,0:T(8,128)(2,1)S(1)}, u32[]{:S(2)}, u32[]{:S(2)}) collective-permute-start(bf16[256,512]{1,0:T(8,128)(2,1)S(1)} %fusion.18), channel_id=1, source_target_pairs={{128,0},{192,64},{256,128},{320,192},{384,256},{448,320},{129,1},{... | collective-permute-start | bytes 786440 | tf_op jit(solution)/shard_map/ppermute | solution.py:28
  190.4 0.7 copy-start.7
  191.1 0.8 copy-start.9
  192.0 4.9 %collective-permute-start.7 = (bf16[256,512]{1,0:T(8,128)(2,1)}, bf16[256,512]{1,0:T(8,128)(2,1)}, u32[]{:S(2)}, u32[]{:S(2)}) collective-permute-start(bf16[256,512]{1,0:T(8,128)(2,1)} %fusion.19), channel_id=1, source_target_pairs={{0,64},{64,0},{128,192},{192,128},{256,320},{320,256},{384,448},{4... | collective-permute-start | bytes 786440 | tf_op jit(solution)/shard_map/ppermute | solution.py:24
  194.3 2.6 %copy-start.8 = (bf16[256,512]{1,0:T(8,128)(2,1)S(1)}, bf16[256,512]{1,0:T(8,128)(2,1)}, u32[]{:S(2)}) copy-start(bf16[256,512]{1,0:T(8,128)(2,1)} %copy-done.7) | copy-start | bytes 786436
  194.3 2.6 %copy-start.10 = (bf16[256,512]{1,0:T(8,128)(2,1)S(1)}, bf16[256,512]{1,0:T(8,128)(2,1)}, u32[]{:S(2)}) copy-start(bf16[256,512]{1,0:T(8,128)(2,1)} %copy-done.9) | copy-start | bytes 786436
  201.9 2.9 %copy-start.3 = (f32[4,4,2,16,512]{4,3,2,1,0:T(8,128)S(1)}, f32[4,4,2,16,512]{4,3,2,1,0:T(8,128)}, u32[]{:S(2)}) copy-start(f32[4,4,2,16,512]{4,3,2,1,0:T(8,128)} %copy.21) | copy-start | bytes 3145732
  201.9 2.9 %copy-start.5 = (f32[256,512]{1,0:T(8,128)S(1)}, f32[256,512]{1,0:T(8,128)}, u32[]{:S(2)}) copy-start(f32[256,512]{1,0:T(8,128)} %get-tuple-element.5) | copy-start | bytes 1572868
  201.9 3.0 %copy-start.6 = (f32[256,512]{1,0:T(8,128)S(1)}, f32[256,512]{1,0:T(8,128)}, u32[]{:S(2)}) copy-start(f32[256,512]{1,0:T(8,128)} %get-tuple-element.6) | copy-start | bytes 1572868
Sparse Core Ops, SparseCore 0:
  88.5 56.1 all-gather.1

commit v2 on v1

--- a/solution.py
+++ b/solution.py
@@ -20,6 +20,15 @@
     return lax.ppermute(value, "tensor", perm)
 
 
+def from_y(value, step):
+    perm = [((y + step) % NY * NZ + z, y * NZ + z) for y in range(NY) for z in range(NZ)]
+    return lax.ppermute(value, "tensor", perm)
+
+
+def from_x(value, step):
+    return lax.ppermute(value, "dp", [((x + step) % 4, x) for x in range(4)])
+
+
 def from_other_core(value):
     return lax.ppermute(value, "section", [(s, s ^ 1) for s in range(8)])
 
@@ -33,8 +42,11 @@
     return lax.all_to_all(spread, axis, 0, 0, axis_index_groups=groups)
 
 
-def tensor_sum(value):
-    value = jnp.sum(to_all(value, "tensor", y_groups(), NY), axis=0)
+def y_sum(value):
+    return jnp.sum(to_all(value, "tensor", y_groups(), NY), axis=0)
+
+
+def z_sum(value):
     return jnp.sum(to_all(value, "tensor", z_groups(), NZ), axis=0)
 
 
@@ -42,6 +54,8 @@
     section = lax.axis_index("section")
     core = section % 2
     tz = lax.axis_index("tensor") % NZ
+    ty = lax.axis_index("tensor") // NZ
+    tx = lax.axis_index("dp")
     width = stashed.shape[-1]
     model_width = lax.axis_size("tensor") * width
     data_count = lax.axis_size("dp")
@@ -63,19 +77,27 @@
         return roll_z(value.reshape(NY, NZ, -1), tz).reshape(tokens)
 
     kv0 = kv_grad[0]
-    z_parts = [from_z(kv0, d) for d in (1, 2, 3)]
-    kv_own = to_all(kv0, "tensor", y_groups(), NY)
-    kv_others = to_all(jnp.stack(z_parts), "tensor", y_groups(), NY)
-
+    raw_all = lax.all_gather(stashed[0], "section")
+    spread = jnp.broadcast_to(kv0, (NZ,) + kv0.shape)
+    spread, kv_y = lax.optimization_barrier((spread, kv0))
+    kv_z = lax.all_to_all(spread, "tensor", 0, 0, axis_index_groups=z_groups())
+    y_parts = [from_y(kv_y, d) for d in (1, 2, 3)]
+    kv_own = jnp.stack([kv_y] + y_parts)
+    kv_own = lax.dynamic_slice_in_dim(jnp.concatenate([kv_own, kv_own]), NY - ty, NY)
     slots = jnp.where(plan[0, 0] == 0, stashed[0], stashed[0][::-1])
     hidden16 = turned(slots)
-    hidden_all = lax.all_gather(hidden16, "section")
     hidden = hidden16.astype(jnp.float32)
-    top = turned(top_grad)
+    squares = absolute(jnp.sum(hidden * hidden, -1))
+    squares, _ = lax.optimization_barrier((squares, y_parts[0]))
+    squares = squares + sum(from_y(squares, d) for d in (1, 2, 3))
+    kv_z, kv_own, squares = lax.optimization_barrier((kv_z, kv_own, squares))
+    others = lax.dynamic_slice_in_dim(jnp.concatenate([kv_z, kv_z]), tz + 1, NZ - 1)
+    kv_others = to_all(others, "tensor", y_groups(), NY)
+    squares = squares + sum(from_z(squares, d) for d in (1, 3, 2))
     gains = norm_gain[0].astype(jnp.float32)
-    squares = tensor_sum(absolute(jnp.sum(hidden * hidden, -1)))
     row_rms = jnp.sqrt(relative(squares) / model_width + EPSILON)
     normed = (gains * hidden / row_rms[:, None]).astype(jnp.bfloat16)
+    kv_others, normed, row_rms = lax.optimization_barrier((kv_others, normed, row_rms))
 
     def split(value):
         value = value.reshape((NY, NZ, micro_count * rows) + value.shape[1:])
@@ -97,23 +119,34 @@
     direct = gained / row_rms[:, None]
     direct16 = direct.astype(jnp.bfloat16)
 
-    other = from_other_core(direct16).astype(jnp.float32)
+    other = from_other_core(direct16)
+    aligned_y = y_sum(absolute(aligned_part))
+    other, aligned_y = lax.optimization_barrier((other, aligned_y))
+    other = other.astype(jnp.float32)
     halves = (direct + other).reshape(2, tokens // 2, width)
     half = lax.dynamic_index_in_dim(halves, core, 0, keepdims=False).astype(jnp.bfloat16)
+    normed, half = lax.optimization_barrier((normed, half))
     above = sum(from_chips_above(half, d).astype(jnp.float32) for d in (1, 2, 3))
     above_other = from_other_core(above.astype(jnp.bfloat16)).astype(jnp.float32)
     first = core == 0
     above_all = jnp.concatenate([jnp.where(first, above, above_other), jnp.where(first, above_other, above)])
 
-    aligned = relative(tensor_sum(absolute(aligned_part)))
+    aligned = relative(z_sum(aligned_y))
     scale = (aligned / (model_width * row_rms**3)).reshape(-1, 128)
-    scales = to_all(scale, "section", None, 8).reshape(8, tokens)
+    swap = jnp.broadcast_to(plan[0, 0].astype(jnp.float32), (1, 128))
+    scales = to_all(jnp.concatenate([scale, swap]), "section", None, 8)
+    swaps = scales[:, -1, :1]
+    scales = scales[:, :-1].reshape(8, tokens)
     later = jnp.arange(8)[:, None] >= section
     scales = jnp.where(later, scales, 0.0)
-    correction = jnp.sum(hidden_all.astype(jnp.float32) * scales[:, :, None], axis=0)
-    total = top.astype(jnp.float32) + direct + jnp.where(first, other, 0.0) + above_all - correction
-    out = roll_z(total.astype(jnp.bfloat16).reshape(NY, NZ, micro_count, rows, width), NZ - tz)
-    input_grads = out.transpose(2, 0, 1, 3, 4).reshape(1, micro_count, NY * NZ * rows, width)
+    ordered = jnp.where(swaps[:, :, None, None] == 0, raw_all, raw_all[:, ::-1])
+    flat = scales.reshape(8, NY, NZ, micro_count, rows)
+    flat = jax.vmap(lambda v: roll_z(v, NZ - tz))(flat).transpose(0, 3, 1, 2, 4).reshape(8, micro_count, -1)
+    correction = jnp.sum(ordered.astype(jnp.float32) * flat[..., None], axis=0)
+    total = direct + jnp.where(first, other, 0.0) + above_all
+    total = roll_z(total.reshape(NY, NZ, micro_count, rows, width), NZ - tz)
+    total = total.transpose(2, 0, 1, 3, 4).reshape(micro_count, NY * NZ * rows, width)
+    input_grads = (top_grad.astype(jnp.float32) + total - correction).astype(jnp.bfloat16)[None]
 
     normed_own, normed_others = split(normed)
 
@@ -123,9 +156,14 @@
         )
 
     local_weight = outer(normed_own, flat_own) + outer(normed_others, flat_others)
-    pieces = local_weight.astype(jnp.bfloat16).reshape(width, data_count, -1).transpose(1, 0, 2)
-    got = lax.all_to_all(pieces, "dp", 0, 0)
-    summed = jnp.sum(got.astype(jnp.float32), axis=0)
+    own_piece = lax.dynamic_slice_in_dim(local_weight, tx * width, width, axis=1)
+    sent = local_weight.astype(jnp.bfloat16)
+
+    def piece(step):
+        at = (tx + 4 - step) % 4
+        return lax.dynamic_slice_in_dim(sent, at * width, width, axis=1)
+
+    summed = own_piece + sum(from_x(piece(d), d).astype(jnp.float32) for d in (1, 2, 3))
     weight_grads = (summed / (micro_count * data_count)).astype(jnp.bfloat16)[None]
     return (input_grads, weight_grads)
 

time: 218 us -> 212 us (0.972)
  waiting for transfers between devices: 85.7 us -> 24.3 us
  starting transfers between devices: 75.7 us -> 114 us
  local copies, waits for them, and re-layouts: 13.6 us -> 22.3 us
  other arithmetic: 17.9 us -> 23 us
  matrix products: 6.75 us -> 11.6 us
    all_to_all x7 -> x4, waiting for transfers between devices: 48.5 us -> 7.53 us  [to_all(): return lax.all_to_all(spread, axis, 0, 0, axis_index_groups=groups)]
    ppermute x0 -> x9, starting transfers between devices: none -> 30 us  [the longest x6 20.1 us: from_y(): return lax.ppermute(value, 'tensor', perm)]
    ppermute x3, waiting for transfers between devices: 19.1 us -> 0.01 us  [from_z(): return lax.ppermute(value, 'tensor', perm)]
    ppermute x3, waiting for transfers between devices: 18.2 us -> 0.01 us  [from_chips_above(): lax.ppermute(value, 'section', [(s, s - 2 * chips) for s in range(2 * chi...]
    ppermute x0 -> x9, waiting for transfers between devices: none -> 16.8 us  [the longest x3 16.7 us: from_x(): return lax.ppermute(value, 'dp', [((x + step) % 4, x) for x in range(4)])]
    all_to_all x1, starting transfers between devices: 4.44 us -> 14.8 us  [shards(): kv_z = lax.all_to_all(spread, 'tensor', 0, 0, axis_index_groups=z_groups())]
    ppermute x2, starting transfers between devices: 4.36 us -> 13.6 us  [from_other_core(): return lax.ppermute(value, 'section', [(s, s ^ 1) for s in range(8)])]
    all_to_all x7 -> x4, starting transfers between devices: 38.3 us -> 30.6 us  [to_all(): return lax.all_to_all(spread, axis, 0, 0, axis_index_groups=groups)]
  transfers between devices with their start and end apart: 17 -> 23, of which waited for: 9 -> 4; matrix products, arithmetic and copies ran while one was open for 11% -> 23% of each run, Pallas kernels for 0% -> 0%
where the time goes in v2:
time: 212 us; the launch traced here: 210 us
  starting transfers between devices  114 us (54%)
  waiting for transfers between devices  24.3 us (11%)
  other arithmetic  23 us (11%)
  local copies, waits for them, and re-layouts  22.3 us (11%)
  between operations  14.7 us (7%)
  matrix products  11.6 us (5%)
    all_to_all x4, starting transfers between devices, to_all(): return lax.all_to_all(spread, axis, 0, 0, axis_index_groups=groups)  30.6 us
    ppermute x3, starting transfers between devices, from_z(): return lax.ppermute(value, 'tensor', perm)  21.3 us
    ppermute x6, starting transfers between devices, from_y(): return lax.ppermute(value, 'tensor', perm)  20.1 us
    ppermute x3, waiting for transfers between devices, from_x(): return lax.ppermute(value, 'dp', [((x + step) % 4, x) for x in range(4)])  16.7 us
    all_to_all x1, starting transfers between devices, shards(): kv_z = lax.all_to_all(spread, 'tensor', 0, 0, axis_index_groups=z_groups())  14.8 us
    ppermute x2, starting transfers between devices, from_other_core(): return lax.ppermute(value, 'section', [(s, s ^ 1) for s in range(8)])  13.6 us
    ppermute x3, starting transfers between devices, from_x(): return lax.ppermute(value, 'dp', [((x + step) % 4, x) for x in range(4)])  9.93 us
    all_to_all x4, waiting for transfers between devices, to_all(): return lax.all_to_all(spread, axis, 0, 0, axis_index_groups=groups)  7.53 us
  transfers between devices with their start and end apart: 23, of which 4 were waited for; matrix products, arithmetic and copies ran while one was open for 23% of the time, Pallas kernels for 0%

profile of v2, /device:TPU:1, one launch (start us, length us, event | category | flops | bytes accessed | tf_op | source)
XLA Modules:
  0.0 210.2 jit_solution(2141817390862656531)
XLA Ops:
  7.3 1.9 broadcast_in_dim.54
  9.2 4.0 %collective-permute-start.2 = (bf16[2,16,2048]{2,1,0:T(8,128)(2,1)}, bf16[2,16,2048]{2,1,0:T(8,128)(2,1)S(1)}, u32[]{:S(2)}, u32[]{:S(2)}) collective-permute-start(bf16[2,16,2048]{2,1,0:T(8,128)(2,1)} %bitcast.106), channel_id=1, source_target_pairs={{48,0},{52,4},{56,8},{60,12},{0,16},{4,20},{8,24},{12,28},{16,32},... | collective-permute-start | bytes 393224 | tf_op jit(solution)/shard_map/ppermute | solution.py:25
  13.2 4.5 %collective-permute-start.1 = (bf16[2,16,2048]{2,1,0:T(8,128)(2,1)}, bf16[2,16,2048]{2,1,0:T(8,128)(2,1)S(1)}, u32[]{:S(2)}, u32[]{:S(2)}) collective-permute-start(bf16[2,16,2048]{2,1,0:T(8,128)(2,1)} %bitcast.107), channel_id=1, source_target_pairs={{32,0},{36,4},{40,8},{44,12},{48,16},{52,20},{56,24},{60,28},{0,32... | collective-permute-start | bytes 393224 | tf_op jit(solution)/shard_map/ppermute | solution.py:25
  17.7 3.0 %collective-permute-start = (bf16[2,16,2048]{2,1,0:T(8,128)(2,1)}, bf16[2,16,2048]{2,1,0:T(8,128)(2,1)}, u32[]{:S(2)}, u32[]{:S(2)}) collective-permute-start(bf16[2,16,2048]{2,1,0:T(8,128)(2,1)} %bitcast.108), channel_id=1, source_target_pairs={{16,0},{20,4},{24,8},{28,12},{32,16},{36,20},{40,24},{44,28},{48,3... | collective-permute-start | bytes 393224 | tf_op jit(solution)/shard_map/ppermute | solution.py:25
  20.7 14.8 %all-to-all-start = ((bf16[4,2,16,2048]{3,2,1,0:T(8,128)(2,1)}), bf16[4,2,16,2048]{3,2,1,0:T(8,128)(2,1)}, u32[]{:S(2)}, u32[]{:S(2)}) async-start(bf16[4,2,16,2048]{3,2,1,0:T(8,128)(2,1)} %broadcast_in_dim.54), calls=%async_computation | async-start | bytes 1048576 | tf_op jit(solution)/shard_map/all_to_all | solution.py:83
  37.2 1.4 multiply_reduce_fusion.1
  40.3 2.3 %collective-permute-start.5 = (f32[4,128]{1,0:T(4,128)S(1)}, f32[4,128]{1,0:T(4,128)S(1)}, u32[]{:S(2)}, u32[]{:S(2)}) collective-permute-start(f32[4,128]{1,0:T(4,128)S(1)} %reshape.129), channel_id=1, source_target_pairs={{48,0},{52,4},{56,8},{60,12},{0,16},{4,20},{8,24},{12,28},{16,32},... | collective-permute-start | bytes 6152 | tf_op jit(solution)/shard_map/ppermute | solution.py:25
  42.6 2.7 %collective-permute-start.4 = (f32[4,128]{1,0:T(4,128)S(1)}, f32[4,128]{1,0:T(4,128)S(1)}, u32[]{:S(2)}, u32[]{:S(2)}) collective-permute-start(f32[4,128]{1,0:T(4,128)S(1)} %reshape.129), channel_id=1, source_target_pairs={{32,0},{36,4},{40,8},{44,12},{48,16},{52,20},{56,24},{60,28},{0,32... | collective-permute-start | bytes 6152 | tf_op jit(solution)/shard_map/ppermute | solution.py:25
  45.4 3.5 %collective-permute-start.3 = (f32[4,128]{1,0:T(4,128)S(1)}, f32[4,128]{1,0:T(4,128)S(1)}, u32[]{:S(2)}, u32[]{:S(2)}) collective-permute-start(f32[4,128]{1,0:T(4,128)S(1)} %reshape.129), channel_id=1, source_target_pairs={{16,0},{20,4},{24,8},{28,12},{32,16},{36,20},{40,24},{44,28},{48,3... | collective-permute-start | bytes 6152 | tf_op jit(solution)/shard_map/ppermute | solution.py:25
  48.9 1.6 bitcast_dynamic-update-slice_fusion.4
  52.4 1.5 bitcast_dynamic-update-slice_fusion.5
  55.3 1.9 constant_dynamic-slice_fusion.3
  57.2 1.2 fusion.17
  58.4 1.4 broadcast_in_dim.55
  59.8 4.3 %all-to-all-start.1 = ((bf16[4,3,2,16,2048]{4,3,2,1,0:T(8,128)(2,1)}), bf16[4,3,2,16,2048]{4,3,2,1,0:T(8,128)(2,1)}, u32[]{:S(2)}, u32[]{:S(2)}) async-start(bf16[4,3,2,16,2048]{4,3,2,1,0:T(8,128)(2,1)} %broadcast_in_dim.55), calls=%async_computation.1 | async-start | bytes 3145728 | tf_op jit(solution)/shard_map/all_to_all | solution.py:42
  64.1 12.1 %collective-permute-start.8 = (f32[4,128]{1,0:T(4,128)S(1)}, f32[4,128]{1,0:T(4,128)S(1)}, u32[]{:S(2)}, u32[]{:S(2)}) collective-permute-start(f32[4,128]{1,0:T(4,128)S(1)} %add_add_fusion.1), channel_id=1, source_target_pairs={{8,0},{12,4},{0,8},{4,12},{24,16},{28,20},{16,24},{20,28},{40,32},... | collective-permute-start | bytes 6152 | tf_op jit(solution)/shard_map/ppermute | solution.py:20
  76.2 2.2 %collective-permute-start.7 = (f32[4,128]{1,0:T(4,128)S(1)}, f32[4,128]{1,0:T(4,128)S(1)}, u32[]{:S(2)}, u32[]{:S(2)}) collective-permute-start(f32[4,128]{1,0:T(4,128)S(1)} %add_add_fusion.1), channel_id=1, source_target_pairs={{12,0},{0,4},{4,8},{8,12},{28,16},{16,20},{20,24},{24,28},{44,32},... | collective-permute-start | bytes 6152 | tf_op jit(solution)/shard_map/ppermute | solution.py:20
  78.5 7.0 %collective-permute-start.6 = (f32[4,128]{1,0:T(4,128)S(1)}, f32[4,128]{1,0:T(4,128)S(1)}, u32[]{:S(2)}, u32[]{:S(2)}) collective-permute-start(f32[4,128]{1,0:T(4,128)S(1)} %add_add_fusion.1), channel_id=1, source_target_pairs={{4,0},{8,4},{12,8},{0,12},{20,16},{24,20},{28,24},{16,28},{36,32},... | collective-permute-start | bytes 6152 | tf_op jit(solution)/shard_map/ppermute | solution.py:20
  85.5 1.9 fusion.2
  87.6 0.9 fusion.13
  88.6 2.4 %fusion = f32[4,3,32,512]{3,2,1,0:T(8,128)S(1)} fusion(bf16[4,3,32,2048]{3,2,1,0:T(8,128)(2,1)} %bitcast.16, bf16[1,512,2048]{2,1,0:T(8,128)(2,1)S(1)} %copy-done), kind=kOutput, calls=%fused_computation.5 | convolution fusion | flops 805306368 | bytes 4456448 | tf_op jit(solution)/shard_map/dot_general | solution.py:111
  92.0 0.9 fusion.32
  92.9 10.9 %collective-permute-start.9 = (bf16[512,512]{1,0:T(8,128)(2,1)}, bf16[512,512]{1,0:T(8,128)(2,1)}, u32[]{:S(2)}, u32[]{:S(2)}) collective-permute-start(bf16[512,512]{1,0:T(8,128)(2,1)} %fusion.32), channel_id=1, source_target_pairs={{0,64},{64,0},{128,192},{192,128},{256,320},{320,256},{384,448},{4... | collective-permute-start | bytes 1572872 | tf_op jit(solution)/shard_map/ppermute | solution.py:33
  104.3 1.6 fusion.8
  106.7 4.4 %all-to-all-start.2 = ((f32[4,4,128]{2,1,0:T(4,128)}), f32[4,4,128]{2,1,0:T(4,128)S(1)}, u32[]{:S(2)}, u32[]{:S(2)}) async-start(f32[4,4,128]{2,1,0:T(4,128)} %broadcast_in_dim.56), calls=%async_computation.2 | async-start | bytes 16384 | tf_op jit(solution)/shard_map/all_to_all | solution.py:42
  111.9 3.4 %all-to-all-done.2 = f32[4,4,128]{2,1,0:T(4,128)S(1)} async-done(((f32[4,4,128]{2,1,0:T(4,128)}), f32[4,4,128]{2,1,0:T(4,128)S(1)}, u32[]{:S(2)}, u32[]{:S(2)}) %all-to-all-start.2) | async-done | bytes 8224 | tf_op jit(solution)/shard_map/all_to_all | solution.py:42
  115.4 1.4 convert_add_fusion
  118.1 1.3 collective-permute-start.12
  119.4 1.3 collective-permute-start.11
  120.7 1.3 collective-permute-start.10
  122.6 6.6 %all-to-all-start.3 = ((f32[4,4,128]{2,1,0:T(4,128)}), f32[4,4,128]{2,1,0:T(4,128)S(1)}, u32[]{:S(2)}, u32[]{:S(2)}) async-start(f32[4,4,128]{2,1,0:T(4,128)} %broadcast_in_dim.58), calls=%async_computation.3 | async-start | bytes 16384 | tf_op jit(solution)/shard_map/all_to_all | solution.py:42
  129.3 1.8 fusion.35
  131.1 5.5 %fusion.34 = (bf16[512,2048]{1,0:T(8,128)(2,1)}, f32[512,2048]{1,0:T(8,128)}) fusion(f32[512,2048]{1,0:T(8,128)S(1)} %fusion.35, bf16[384,512]{1,0:T(8,128)(2,1)S(1)} %bitcast.104, bf16[384,2048]{1,0:T(8,128)(2,1)} %bitcast.39), kind=kOutput, calls=%fused_computation.86 | convolution fusion | flops 807403520 | bytes 12451840 | tf_op jit(solution)/shard_map/dot_general | solution.py:154
  136.6 4.1 %all-to-all-done.3 = f32[4,4,128]{2,1,0:T(4,128)S(1)} async-done(((f32[4,4,128]{2,1,0:T(4,128)}), f32[4,4,128]{2,1,0:T(4,128)S(1)}, u32[]{:S(2)}, u32[]{:S(2)}) %all-to-all-start.3) | async-done | bytes 8224 | tf_op jit(solution)/shard_map/all_to_all | solution.py:42
  141.5 15.1 %all-to-all-start.4 = ((f32[8,5,128]{2,1,0:T(8,128)}), f32[8,5,128]{2,1,0:T(8,128)S(1)}, u32[]{:S(2)}, u32[]{:S(2)}) async-start(f32[8,5,128]{2,1,0:T(8,128)} %broadcast_in_dim.59), calls=%async_computation.4 | async-start | bytes 65536 | tf_op jit(solution)/shard_map/all_to_all | solution.py:42
  156.6 2.6 %constant_dynamic-slice_fusion.2 = (bf16[512,512]{1,0:T(8,128)(2,1)}, bf16[512,512]{1,0:T(8,128)(2,1)}, bf16[512,512]{1,0:T(8,128)(2,1)}) fusion(bf16[512,2048]{1,0:T(8,128)(2,1)} %get-tuple-element.46, s32[]{:T(128)S(6)} %select_n.139, s32[]{:T(128)S(6)} %select_n.143, s32[]{:T(128)S(6)} %select_n.141), kind=kLoop, calls=%fused_computation.75 | loop fusion | bytes 3145740 | tf_op jit(solution)/shard_map/dynamic_slice | solution.py:164
  159.2 4.4 %collective-permute-start.14 = (bf16[512,512]{1,0:T(8,128)(2,1)}, bf16[512,512]{1,0:T(8,128)(2,1)}, u32[]{:S(2)}, u32[]{:S(2)}) collective-permute-start(bf16[512,512]{1,0:T(8,128)(2,1)} %get-tuple-element.41), channel_id=1, source_target_pairs={{1,0},{2,1},{3,2},{0,3},{5,4},{6,5},{7,6},{4,7},{9,8},{10,9},{11,1... | collective-permute-start | bytes 1572872 | tf_op jit(solution)/shard_map/ppermute | solution.py:29
  163.6 1.9 collective-permute-start.16
  165.8 3.6 %collective-permute-start.15 = (bf16[512,512]{1,0:T(8,128)(2,1)}, bf16[512,512]{1,0:T(8,128)(2,1)}, u32[]{:S(2)}, u32[]{:S(2)}) collective-permute-start(bf16[512,512]{1,0:T(8,128)(2,1)} %get-tuple-element.43), channel_id=1, source_target_pairs={{2,0},{3,1},{0,2},{1,3},{6,4},{7,5},{4,6},{5,7},{10,8},{11,9},{8,1... | collective-permute-start | bytes 1572872 | tf_op jit(solution)/shard_map/ppermute | solution.py:29
  170.8 1.2 fusion.19
  172.0 2.8 %collective-permute-start.13 = (bf16[256,512]{1,0:T(8,128)(2,1)S(1)}, bf16[256,512]{1,0:T(8,128)(2,1)S(1)}, u32[]{:S(2)}, u32[]{:S(2)}) collective-permute-start(bf16[256,512]{1,0:T(8,128)(2,1)S(1)} %fusion.19), channel_id=1, source_target_pairs={{0,64},{64,0},{128,192},{192,128},{256,320},{320,256},{384,448},{4... | collective-permute-start | bytes 786440 | tf_op jit(solution)/shard_map/ppermute | solution.py:33
  174.7 11.6 %collective-permute-done.14 = bf16[512,512]{1,0:T(8,128)(2,1)} collective-permute-done((bf16[512,512]{1,0:T(8,128)(2,1)}, bf16[512,512]{1,0:T(8,128)(2,1)}, u32[]{:S(2)}, u32[]{:S(2)}) %collective-permute-start.14) | collective-permute-done | bytes 524320 | tf_op jit(solution)/shard_map/ppermute | solution.py:29
  186.3 5.2 %collective-permute-done.16 = bf16[512,512]{1,0:T(8,128)(2,1)} collective-permute-done((bf16[512,512]{1,0:T(8,128)(2,1)}, bf16[512,512]{1,0:T(8,128)(2,1)}, u32[]{:S(2)}, u32[]{:S(2)}) %collective-permute-start.16) | collective-permute-done | bytes 524320 | tf_op jit(solution)/shard_map/ppermute | solution.py:29
  191.5 2.8 %fusion.14 = bf16[1,512,512]{2,1,0:T(8,128)(2,1)} fusion(bf16[512,512]{1,0:T(8,128)(2,1)} %collective-permute-done.16, bf16[512,512]{1,0:T(8,128)(2,1)} %collective-permute-done.15, bf16[512,512]{1,0:T(8,128)(2,1)} %collective-permute-done.14, f32[512,2048]{1,0:T(8,128)} %get-tuple-element.47, s32[]{:T(128)S(6)} %select_n.137), kind=kLoop, calls=%fused_computation.35 | loop fusion | flops 2097152 | bytes 3145732 | tf_op jit(solution)/shard_map/broadcast_in_dim | solution.py:167
  194.3 1.3 convert_select_fusion.2
  195.6 1.3 fusion.5
  197.3 4.9 %multiply_reduce_fusion = f32[2,256,512]{2,1,0:T(8,128)S(1)} fusion(bf16[8,2,256,512]{3,2,1,0:T(8,128)(2,1)} %all-gather.2.cloned.1.call-done, f32[8,2,256]{2,1,0:T(2,128)S(1)} %reshape.182, pred[8]{0:T(512)(128)(4,1)S(1)} %compare_reduce_fusion), kind=kLoop, calls=%fused_computation | loop fusion | flops 8126464 | bytes 5259272 | tf_op jit(solution)/shard_map/reduce_sum | solution.py:145
  202.2 1.1 fusion.10
  (91 shorter events, 14.7 us)
Async XLA Ops:
  7.2 78.3 %copy-start = (bf16[1,512,2048]{2,1,0:T(8,128)(2,1)S(1)}, bf16[1,512,2048]{2,1,0:T(8,128)(2,1)}, u32[]{:S(2)}) copy-start(bf16[1,512,2048]{2,1,0:T(8,128)(2,1)} %param.9) | copy-start | bytes 6291460
  7.2 28.4 %copy-start.5 = (bf16[1,2,16,2048]{3,2,1,0:T(8,128)(2,1)S(1)}, bf16[1,2,16,2048]{3,2,1,0:T(8,128)(2,1)}, u32[]{:S(2)}) copy-start(bf16[1,2,16,2048]{3,2,1,0:T(8,128)(2,1)} %param.10) | copy-start | bytes 393220
  7.2 29.1 %copy-start.4 = (bf16[1,2,256,512]{3,2,1,0:T(8,128)(2,1)S(1)}, bf16[1,2,256,512]{3,2,1,0:T(8,128)(2,1)}, u32[]{:S(2)}) copy-start(bf16[1,2,256,512]{3,2,1,0:T(8,128)(2,1)} %param.7) | copy-start | bytes 1572868
  7.2 29.0 %copy-start.9 = (s32[1,2]{1,0:T(1,128)S(1)}, s32[1,2]{1,0:T(1,128)}, u32[]{:S(2)}) copy-start(s32[1,2]{1,0:T(1,128)} %param.6) | copy-start | bytes 28
  7.2 190.1 %all-gather.2.cloned.1.call-start = ((), (), s32[]{:S(2)}) async-start(), calls=%async_computation.5 | async-start | bytes 4718592 | tf_op jit(solution)/shard_map/all_gather | solution.py:80
  9.2 41.9 %collective-permute-start.2 = (bf16[2,16,2048]{2,1,0:T(8,128)(2,1)}, bf16[2,16,2048]{2,1,0:T(8,128)(2,1)S(1)}, u32[]{:S(2)}, u32[]{:S(2)}) collective-permute-start(bf16[2,16,2048]{2,1,0:T(8,128)(2,1)} %bitcast.106), channel_id=1, source_target_pairs={{48,0},{52,4},{56,8},{60,12},{0,16},{4,20},{8,24},{12,28},{16,32},... | collective-permute-start | bytes 393224 | tf_op jit(solution)/shard_map/ppermute | solution.py:25
  13.2 37.3 %collective-permute-start.1 = (bf16[2,16,2048]{2,1,0:T(8,128)(2,1)}, bf16[2,16,2048]{2,1,0:T(8,128)(2,1)S(1)}, u32[]{:S(2)}, u32[]{:S(2)}) collective-permute-start(bf16[2,16,2048]{2,1,0:T(8,128)(2,1)} %bitcast.107), channel_id=1, source_target_pairs={{32,0},{36,4},{40,8},{44,12},{48,16},{52,20},{56,24},{60,28},{0,32... | collective-permute-start | bytes 393224 | tf_op jit(solution)/shard_map/ppermute | solution.py:25
  17.7 22.6 %collective-permute-start = (bf16[2,16,2048]{2,1,0:T(8,128)(2,1)}, bf16[2,16,2048]{2,1,0:T(8,128)(2,1)}, u32[]{:S(2)}, u32[]{:S(2)}) collective-permute-start(bf16[2,16,2048]{2,1,0:T(8,128)(2,1)} %bitcast.108), channel_id=1, source_target_pairs={{16,0},{20,4},{24,8},{28,12},{32,16},{36,20},{40,24},{44,28},{48,3... | collective-permute-start | bytes 393224 | tf_op jit(solution)/shard_map/ppermute | solution.py:25
  20.7 36.5 %all-to-all-start = ((bf16[4,2,16,2048]{3,2,1,0:T(8,128)(2,1)}), bf16[4,2,16,2048]{3,2,1,0:T(8,128)(2,1)}, u32[]{:S(2)}, u32[]{:S(2)}) async-start(bf16[4,2,16,2048]{3,2,1,0:T(8,128)(2,1)} %broadcast_in_dim.54), calls=%async_computation | async-start | bytes 1048576 | tf_op jit(solution)/shard_map/all_to_all | solution.py:83
  38.6 49.0 %copy-start.1 = (f32[4,4,2,16,512]{4,3,2,1,0:T(8,128)}, f32[4,4,2,16,512]{4,3,2,1,0:T(8,128)S(1)}, u32[]{:S(2)}) copy-start(f32[4,4,2,16,512]{4,3,2,1,0:T(8,128)S(1)} %get-tuple-element.40) | copy-start | bytes 3145732
  40.3 16.8 %collective-permute-start.5 = (f32[4,128]{1,0:T(4,128)S(1)}, f32[4,128]{1,0:T(4,128)S(1)}, u32[]{:S(2)}, u32[]{:S(2)}) collective-permute-start(f32[4,128]{1,0:T(4,128)S(1)} %reshape.129), channel_id=1, source_target_pairs={{48,0},{52,4},{56,8},{60,12},{0,16},{4,20},{8,24},{12,28},{16,32},... | collective-permute-start | bytes 6152 | tf_op jit(solution)/shard_map/ppermute | solution.py:25
  42.6 14.5 %collective-permute-start.4 = (f32[4,128]{1,0:T(4,128)S(1)}, f32[4,128]{1,0:T(4,128)S(1)}, u32[]{:S(2)}, u32[]{:S(2)}) collective-permute-start(f32[4,128]{1,0:T(4,128)S(1)} %reshape.129), channel_id=1, source_target_pairs={{32,0},{36,4},{40,8},{44,12},{48,16},{52,20},{56,24},{60,28},{0,32... | collective-permute-start | bytes 6152 | tf_op jit(solution)/shard_map/ppermute | solution.py:25
  45.4 11.8 %collective-permute-start.3 = (f32[4,128]{1,0:T(4,128)S(1)}, f32[4,128]{1,0:T(4,128)S(1)}, u32[]{:S(2)}, u32[]{:S(2)}) collective-permute-start(f32[4,128]{1,0:T(4,128)S(1)} %reshape.129), channel_id=1, source_target_pairs={{16,0},{20,4},{24,8},{28,12},{32,16},{36,20},{40,24},{44,28},{48,3... | collective-permute-start | bytes 6152 | tf_op jit(solution)/shard_map/ppermute | solution.py:25
  58.4 5.7 %copy-start.7 = (bf16[1,512]{1,0:T(2,128)(2,1)S(1)}, bf16[1,512]{1,0:T(2,128)(2,1)}, u32[]{:S(2)}) copy-start(bf16[1,512]{1,0:T(2,128)(2,1)} %param.8) | copy-start | bytes 3076
  59.8 28.8 %all-to-all-start.1 = ((bf16[4,3,2,16,2048]{4,3,2,1,0:T(8,128)(2,1)}), bf16[4,3,2,16,2048]{4,3,2,1,0:T(8,128)(2,1)}, u32[]{:S(2)}, u32[]{:S(2)}) async-start(bf16[4,3,2,16,2048]{4,3,2,1,0:T(8,128)(2,1)} %broadcast_in_dim.55), calls=%async_computation.1 | async-start | bytes 3145728 | tf_op jit(solution)/shard_map/all_to_all | solution.py:42
  64.1 23.2 %collective-permute-start.8 = (f32[4,128]{1,0:T(4,128)S(1)}, f32[4,128]{1,0:T(4,128)S(1)}, u32[]{:S(2)}, u32[]{:S(2)}) collective-permute-start(f32[4,128]{1,0:T(4,128)S(1)} %add_add_fusion.1), channel_id=1, source_target_pairs={{8,0},{12,4},{0,8},{4,12},{24,16},{28,20},{16,24},{20,28},{40,32},... | collective-permute-start | bytes 6152 | tf_op jit(solution)/shard_map/ppermute | solution.py:20
  76.2 11.1 %collective-permute-start.7 = (f32[4,128]{1,0:T(4,128)S(1)}, f32[4,128]{1,0:T(4,128)S(1)}, u32[]{:S(2)}, u32[]{:S(2)}) collective-permute-start(f32[4,128]{1,0:T(4,128)S(1)} %add_add_fusion.1), channel_id=1, source_target_pairs={{12,0},{0,4},{4,8},{8,12},{28,16},{16,20},{20,24},{24,28},{44,32},... | collective-permute-start | bytes 6152 | tf_op jit(solution)/shard_map/ppermute | solution.py:20
  78.5 8.9 %collective-permute-start.6 = (f32[4,128]{1,0:T(4,128)S(1)}, f32[4,128]{1,0:T(4,128)S(1)}, u32[]{:S(2)}, u32[]{:S(2)}) collective-permute-start(f32[4,128]{1,0:T(4,128)S(1)} %add_add_fusion.1), channel_id=1, source_target_pairs={{4,0},{8,4},{12,8},{0,12},{20,16},{24,20},{28,24},{16,28},{36,32},... | collective-permute-start | bytes 6152 | tf_op jit(solution)/shard_map/ppermute | solution.py:20
  91.0 0.9 copy-start.2
  92.0 19.3 %copy-start.10 = (s32[1,2]{1,0:T(1,128)S(1)}, s32[1,2]{1,0:T(1,128)}, u32[]{:S(2)}) copy-start(s32[1,2]{1,0:T(1,128)} %param.6) | copy-start | bytes 28
  92.9 22.4 %collective-permute-start.9 = (bf16[512,512]{1,0:T(8,128)(2,1)}, bf16[512,512]{1,0:T(8,128)(2,1)}, u32[]{:S(2)}, u32[]{:S(2)}) collective-permute-start(bf16[512,512]{1,0:T(8,128)(2,1)} %fusion.32), channel_id=1, source_target_pairs={{0,64},{64,0},{128,192},{192,128},{256,320},{320,256},{384,448},{4... | collective-permute-start | bytes 1572872 | tf_op jit(solution)/shard_map/ppermute | solution.py:33
  106.7 8.6 %all-to-all-start.2 = ((f32[4,4,128]{2,1,0:T(4,128)}), f32[4,4,128]{2,1,0:T(4,128)S(1)}, u32[]{:S(2)}, u32[]{:S(2)}) async-start(f32[4,4,128]{2,1,0:T(4,128)} %broadcast_in_dim.56), calls=%async_computation.2 | async-start | bytes 16384 | tf_op jit(solution)/shard_map/all_to_all | solution.py:42
  115.4 2.1 copy-start.3
  118.1 47.6 %collective-permute-start.12 = (bf16[256,512]{1,0:T(8,128)(2,1)}, bf16[256,512]{1,0:T(8,128)(2,1)}, u32[]{:S(2)}, u32[]{:S(2)}) collective-permute-start(bf16[256,512]{1,0:T(8,128)(2,1)} %fusion.18), channel_id=1, source_target_pairs={{384,0},{448,64},{385,1},{449,65},{386,2},{450,66},{387,3},{451,67... | collective-permute-start | bytes 786440 | tf_op jit(solution)/shard_map/ppermute | solution.py:37
  119.4 51.3 %collective-permute-start.11 = (bf16[256,512]{1,0:T(8,128)(2,1)}, bf16[256,512]{1,0:T(8,128)(2,1)}, u32[]{:S(2)}, u32[]{:S(2)}) collective-permute-start(bf16[256,512]{1,0:T(8,128)(2,1)} %fusion.18), channel_id=1, source_target_pairs={{256,0},{320,64},{384,128},{448,192},{257,1},{321,65},{385,129},{4... | collective-permute-start | bytes 786440 | tf_op jit(solution)/shard_map/ppermute | solution.py:37
  120.7 50.0 %collective-permute-start.10 = (bf16[256,512]{1,0:T(8,128)(2,1)}, bf16[256,512]{1,0:T(8,128)(2,1)}, u32[]{:S(2)}, u32[]{:S(2)}) collective-permute-start(bf16[256,512]{1,0:T(8,128)(2,1)} %fusion.18), channel_id=1, source_target_pairs={{128,0},{192,64},{256,128},{320,192},{384,256},{448,320},{129,1},{... | collective-permute-start | bytes 786440 | tf_op jit(solution)/shard_map/ppermute | solution.py:37
  122.6 18.0 %all-to-all-start.3 = ((f32[4,4,128]{2,1,0:T(4,128)}), f32[4,4,128]{2,1,0:T(4,128)S(1)}, u32[]{:S(2)}, u32[]{:S(2)}) async-start(f32[4,4,128]{2,1,0:T(4,128)} %broadcast_in_dim.58), calls=%async_computation.3 | async-start | bytes 16384 | tf_op jit(solution)/shard_map/all_to_all | solution.py:42
  136.6 32.8 %copy-start.8 = (pred[8]{0:T(512)(128)(4,1)S(1)}, pred[8]{0:T(512)(128)(4,1)}, u32[]{:S(2)}) copy-start(pred[8]{0:T(512)(128)(4,1)} %iota_compare_fusion) | copy-start | bytes 28
  141.5 24.0 %all-to-all-start.4 = ((f32[8,5,128]{2,1,0:T(8,128)}), f32[8,5,128]{2,1,0:T(8,128)S(1)}, u32[]{:S(2)}, u32[]{:S(2)}) async-start(f32[8,5,128]{2,1,0:T(8,128)} %broadcast_in_dim.59), calls=%async_computation.4 | async-start | bytes 65536 | tf_op jit(solution)/shard_map/all_to_all | solution.py:42
  159.2 27.1 %collective-permute-start.14 = (bf16[512,512]{1,0:T(8,128)(2,1)}, bf16[512,512]{1,0:T(8,128)(2,1)}, u32[]{:S(2)}, u32[]{:S(2)}) collective-permute-start(bf16[512,512]{1,0:T(8,128)(2,1)} %get-tuple-element.41), channel_id=1, source_target_pairs={{1,0},{2,1},{3,2},{0,3},{5,4},{6,5},{7,6},{4,7},{9,8},{10,9},{11,1... | collective-permute-start | bytes 1572872 | tf_op jit(solution)/shard_map/ppermute | solution.py:29
  163.6 27.9 %collective-permute-start.16 = (bf16[512,512]{1,0:T(8,128)(2,1)}, bf16[512,512]{1,0:T(8,128)(2,1)}, u32[]{:S(2)}, u32[]{:S(2)}) collective-permute-start(bf16[512,512]{1,0:T(8,128)(2,1)} %get-tuple-element.42), channel_id=1, source_target_pairs={{3,0},{0,1},{1,2},{2,3},{7,4},{4,5},{5,6},{6,7},{11,8},{8,9},{9,10... | collective-permute-start | bytes 1572872 | tf_op jit(solution)/shard_map/ppermute | solution.py:29
  165.8 25.7 %collective-permute-start.15 = (bf16[512,512]{1,0:T(8,128)(2,1)}, bf16[512,512]{1,0:T(8,128)(2,1)}, u32[]{:S(2)}, u32[]{:S(2)}) collective-permute-start(bf16[512,512]{1,0:T(8,128)(2,1)} %get-tuple-element.43), channel_id=1, source_target_pairs={{2,0},{3,1},{0,2},{1,3},{6,4},{7,5},{4,6},{5,7},{10,8},{11,9},{8,1... | collective-permute-start | bytes 1572872 | tf_op jit(solution)/shard_map/ppermute | solution.py:29
  172.0 22.3 %collective-permute-start.13 = (bf16[256,512]{1,0:T(8,128)(2,1)S(1)}, bf16[256,512]{1,0:T(8,128)(2,1)S(1)}, u32[]{:S(2)}, u32[]{:S(2)}) collective-permute-start(bf16[256,512]{1,0:T(8,128)(2,1)S(1)} %fusion.19), channel_id=1, source_target_pairs={{0,64},{64,0},{128,192},{192,128},{256,320},{320,256},{384,448},{4... | collective-permute-start | bytes 786440 | tf_op jit(solution)/shard_map/ppermute | solution.py:33
  197.3 4.9 %copy-start.6 = (bf16[2,256,512]{2,1,0:T(8,128)(2,1)S(1)}, bf16[2,256,512]{2,1,0:T(8,128)(2,1)}, u32[]{:S(2)}) copy-start(bf16[2,256,512]{2,1,0:T(8,128)(2,1)} %param.11) | copy-start | bytes 1572868
Sparse Core Ops, SparseCore 0:
  20.9 78.8 all-gather.1

commit v3 on v0

v3 whole, which is shorter than its diff:
```python
import functools

import jax
import jax.numpy as jnp
from jax import lax
from jax.experimental import pallas as pl
from jax.experimental.pallas import tpu as pltpu
from jax.sharding import PartitionSpec as P

EPSILON = 1e-06
NY, NZ, NX, NS = 4, 4, 4, 8
MICRO, ROWS, LANES = 2, 16, 128
BLOCKS = NY * NZ
F32, BF16 = jnp.float32, jnp.bfloat16
VMEM = pl.BlockSpec(memory_space=pltpu.VMEM)
SMEM = pl.BlockSpec(memory_space=pltpu.SMEM)


def y_groups():
    return [[y * NZ + z for y in range(NY)] for z in range(NZ)]


def z_groups():
    return [[y * NZ + z for z in range(NZ)] for y in range(NY)]


def from_y(value, step):
    perm = [((y + step) % NY * NZ + z, y * NZ + z) for y in range(NY) for z in range(NZ)]
    return lax.ppermute(value, "tensor", perm)


def from_z(value, step):
    perm = [(y * NZ + (z + step) % NZ, y * NZ + z) for y in range(NY) for z in range(NZ)]
    return lax.ppermute(value, "tensor", perm)


def from_x(value, step):
    return lax.ppermute(value, "dp", [((x + step) % NX, x) for x in range(NX)])


def from_other_core(value):
    return lax.ppermute(value, "section", [(s, s ^ 1) for s in range(NS)])


def from_chips_above(value, chips):
    return lax.ppermute(value, "section", [(s, s - 2 * chips) for s in range(2 * chips, NS)])


def y_exchange(spread):
    return lax.all_to_all(spread, "tensor", 0, 0, axis_index_groups=y_groups())


def z_exchange(spread):
    return lax.all_to_all(spread, "tensor", 0, 0, axis_index_groups=z_groups())


def call(body, out_shape, specs, args, scratch=(), cost=None):
    return pl.pallas_call(
        body,
        out_shape=out_shape,
        in_specs=specs,
        out_specs=jax.tree.map(lambda _: VMEM, out_shape),
        scratch_shapes=list(scratch),
        compiler_params=pltpu.CompilerParams(vmem_limit_bytes=28 * 2**20),
        cost_estimate=cost,
    )(*args)


def columns(row, count):
    return jnp.transpose(jnp.broadcast_to(row, (LANES, LANES)))[:, :1] + jnp.zeros((LANES, count), F32)


def spread_body(place, kv_ref, out_ref):
    for step in range(1, NZ):
        block = kv_ref[lax.rem(place[0] + step, NZ)]
        for y in range(NY):
            out_ref[y, step - 1] = block


def back_body(place, own0, own1, own2, own3, others, weight, gains, stashed, squares, direct, direct16, aligned, grad):
    tz, ty, swap = place[0], place[1], place[2]
    kvw = weight.shape[1]
    width = weight.shape[0]
    model_width = width * BLOCKS
    dims = (((1,), (1,)), ((), ()))

    def put(product, blocks):
        for at, (y, step) in enumerate(blocks):
            for m in range(MICRO):
                row = (at * MICRO + m) * ROWS
                grad[m, y * NZ + lax.rem(tz + step, NZ)] = product[row : row + ROWS]

    mine = jnp.concatenate([ref[...].reshape(MICRO * ROWS, kvw) for ref in (own0, own1, own2, own3)])
    product = lax.dot_general(mine, weight[...], dims, preferred_element_type=F32)
    put(product, [(lax.rem(ty + k, NY), 0) for k in range(NY)])
    for y in range(NY):
        rest = others[y].reshape((NZ - 1) * MICRO * ROWS, kvw)
        product = lax.dot_general(rest, weight[...], dims, preferred_element_type=F32)
        put(product, [(y, step) for step in range(1, NZ)])
    gain = gains[...].astype(F32)
    per = LANES // ROWS
    for chunk in range(MICRO * BLOCKS // per):
        m, first = chunk * per // BLOCKS, chunk * per % BLOCKS
        gained = grad[m, first : first + per].reshape(LANES, width) * gain
        hidden = stashed[m ^ swap, first * ROWS : (first + per) * ROWS].astype(F32)
        inverse = 1.0 / jnp.sqrt(squares[chunk : chunk + 1] / model_width + EPSILON)
        here = gained * columns(inverse, width)
        direct[chunk * LANES : (chunk + 1) * LANES] = here
        direct16[chunk * LANES : (chunk + 1) * LANES] = here.astype(BF16)
        terms = gained * hidden
        folded = sum(terms[:, k * LANES : (k + 1) * LANES] for k in range(width // LANES))
        total = jnp.sum(jnp.transpose(folded), axis=0, keepdims=True)
        for y in range(NY):
            aligned[y, chunk : chunk + 1] = total


def half_body(place, direct, other, out_ref):
    rows = out_ref.shape[0]
    at = pl.ds(pl.multiple_of(place[3] * rows, rows), rows)
    out_ref[...] = (direct[at] + other[at].astype(F32)).astype(BF16)


def outer_body(place, own0, own1, own2, own3, others, gains, stashed, squares, kept, sent1, sent2, sent3, normed, left):
    tz, ty, swap, tx = place[0], place[1], place[2], place[4]
    width = kept.shape[0]
    model_width = width * BLOCKS
    gain = gains[...].astype(F32)
    per = LANES // ROWS
    for chunk in range(MICRO * BLOCKS // per):
        m, first = chunk * per // BLOCKS, chunk * per % BLOCKS
        hidden = stashed[m ^ swap, first * ROWS : (first + per) * ROWS].astype(F32)
        inverse = 1.0 / jnp.sqrt(squares[chunk : chunk + 1] / model_width + EPSILON)
        here = gain * hidden * columns(inverse, width)
        normed[m, first : first + per] = here.astype(BF16).reshape(per, ROWS, width)
    blocks = [(lax.rem(ty + k, NY), 0) for k in range(NY)]
    blocks += [(y, step) for y in range(NY) for step in range(1, NZ)]
    for at, (y, step) in enumerate(blocks):
        for m in range(MICRO):
            row = (at * MICRO + m) * ROWS
            left[row : row + ROWS] = normed[m, y * NZ + lax.rem(tz + step, NZ)]
    turned = jnp.transpose(left[...])
    share = MICRO * ROWS
    for step, out_ref in enumerate((kept, sent1, sent2, sent3)):
        at = pl.ds(pl.multiple_of(lax.rem(tx + NX - step, NX) * width, width), width)
        mine = [ref[:, :, at].reshape(share, width) for ref in (own0, own1, own2, own3)]
        rest = others[:, :, :, :, at].reshape(NY * (NZ - 1) * share, width)
        right = jnp.concatenate(mine + [rest])
        out_ref[...] = jnp.dot(turned, right, preferred_element_type=F32).astype(out_ref.dtype)


def scale_body(place, parts, squares, out_ref, *, model_width):
    mean = squares[...] / model_width + EPSILON
    total = parts[0] + parts[1] + parts[2] + parts[3]
    scale = total / (model_width * (mean * jnp.sqrt(mean)))
    swap = jnp.full((NS - MICRO * BLOCKS * ROWS // LANES, LANES), place[2], jnp.int32).astype(F32)
    value = jnp.concatenate([scale, swap])
    for section in range(NS):
        out_ref[section] = value


def total_body(place, raw, scales, direct, other, above, above_other, top, out_ref):
    section, core = place[5], place[3]
    rows, width = raw.shape[2], raw.shape[3]
    chunk = pl.program_id(0)
    use_other = jnp.where(core == 0, 1.0, 0.0)
    fixes = [jnp.zeros((rows, width), F32) for _ in range(MICRO)]
    turned = []
    for m in range(MICRO):
        row = m * (BLOCKS * ROWS // LANES) + chunk
        turned.append(jnp.transpose(scales[:, pl.ds(row, 1)].reshape(NS, LANES)))
    for u in range(NS):
        live = jnp.where(u >= section, 1.0, 0.0)
        swapped = scales[u, NS - 1 : NS, :1] != 0.0
        slots = [raw[u, k].astype(F32) for k in range(MICRO)]
        for m in range(MICRO):
            hidden = jnp.where(swapped, slots[1 - m], slots[m])
            fixes[m] = fixes[m] + hidden * (turned[m][:, u : u + 1] * live)
    for m in range(MICRO):
        mine = jnp.where(core == m, above[...], above_other[...].astype(F32))
        value = top[m].astype(F32) + direct[m] + use_other * other[m].astype(F32) + mine - fixes[m]
        out_ref[m] = value.astype(BF16)


def shards(plan, stashed, norm_gain, kv_weight, kv_grad, top_grad):
    section = lax.axis_index("section")
    core = section % 2
    index = lax.axis_index("tensor")
    tz, ty, tx = index % NZ, index // NZ, lax.axis_index("dp")
    width = stashed.shape[-1]
    tokens = MICRO * BLOCKS * ROWS
    model_width = width * BLOCKS
    lines = tokens // LANES
    place = jnp.stack([tz, ty, plan[0, 0], core, tx, section]).astype(jnp.int32)
    kv0, slots, weight = kv_grad[0], stashed[0], kv_weight[0]
    kvw = kv0.shape[-1]
    half = (tokens // 2, width)

    spread = jnp.broadcast_to(kv0, (NZ,) + kv0.shape)
    spread, kv_y = lax.optimization_barrier((spread, kv0))
    kv_z = z_exchange(spread)
    own = [kv_y] + [from_y(kv_y, d) for d in (1, 2, 3)]
    squares = jnp.sum(jnp.square(slots.astype(F32)), -1).reshape(MICRO, lines // MICRO, LANES)
    squares = jnp.where(plan[0, 0] == 0, squares, squares[::-1]).reshape(lines, LANES)
    squares, _ = lax.optimization_barrier((squares, own[1]))
    squares = squares + sum(from_y(squares, d) for d in (1, 2, 3))
    kv_z, own, squares, slots_later = lax.optimization_barrier((kv_z, own, squares, slots))

    raw_all = lax.all_gather(slots_later, "section")
    shape = jax.ShapeDtypeStruct((NY, NZ - 1) + kv0.shape, BF16)
    others = y_exchange(call(spread_body, shape, [SMEM, VMEM], (place, kv_z)))
    squares = squares + sum(from_z(squares, d) for d in (1, 3, 2))
    others, squares = lax.optimization_barrier((others, squares))

    flops = 2 * tokens * width * kvw
    direct, direct16, aligned = call(
        back_body,
        (
            jax.ShapeDtypeStruct((tokens, width), F32),
            jax.ShapeDtypeStruct((tokens, width), BF16),
            jax.ShapeDtypeStruct((NY, lines, LANES), F32),
        ),
        [SMEM] + [VMEM] * 9,
        (place, *own, others, weight, norm_gain, slots, squares),
        [pltpu.VMEM((MICRO, BLOCKS, ROWS, width), F32)],
        pl.CostEstimate(flops=flops, bytes_accessed=6 * 2**20, transcendentals=0),
    )
    other = from_other_core(direct16)
    aligned = y_exchange(aligned)
    other, aligned = lax.optimization_barrier((other, aligned))
    aligned = jnp.sum(aligned, axis=0)

    chip = call(half_body, jax.ShapeDtypeStruct(half, BF16), [SMEM, VMEM, VMEM], (place, direct, other))
    above = sum(from_chips_above(chip, d).astype(F32) for d in (1, 2, 3))
    above_other = from_other_core(above.astype(BF16))

    aligned, own, others, _ = lax.optimization_barrier((aligned, own, others, chip))
    piece = jax.ShapeDtypeStruct((width, width), BF16)
    kept, *sent = call(
        outer_body,
        (jax.ShapeDtypeStruct((width, width), F32), piece, piece, piece),
        [SMEM] + [VMEM] * 8,
        (place, *own, others, norm_gain, slots, squares),
        [pltpu.VMEM((MICRO, BLOCKS, ROWS, width), BF16), pltpu.VMEM((tokens, width), BF16)],
        pl.CostEstimate(flops=flops, bytes_accessed=6 * 2**20, transcendentals=0),
    )
    summed = kept + sum(from_x(sent[d - 1], d).astype(F32) for d in (1, 2, 3))
    weight_grads = (summed / (MICRO * NX)).astype(BF16)[None]

    parts = z_exchange(jnp.broadcast_to(aligned, (NZ,) + aligned.shape))
    scales = call(
        functools.partial(scale_body, model_width=model_width),
        jax.ShapeDtypeStruct((NS, NS, LANES), F32),
        [SMEM, VMEM, VMEM],
        (place, parts, squares),
    )
    scales = lax.all_to_all(scales, "section", 0, 0)

    by_micro = (MICRO, tokens // MICRO, width)
    at_rows = pl.BlockSpec((MICRO, LANES, width), lambda i: (0, i, 0))
    at_half = pl.BlockSpec((LANES, width), lambda i: (i, 0))
    input_grads = pl.pallas_call(
        total_body,
        grid=(tokens // MICRO // LANES,),
        out_shape=jax.ShapeDtypeStruct(by_micro, BF16),
        in_specs=[
            SMEM,
            pl.BlockSpec((NS, MICRO, LANES, width), lambda i: (0, 0, i, 0)),
            pl.BlockSpec((NS, NS, LANES), lambda i: (0, 0, 0)),
            at_rows,
            at_rows,
            at_half,
            at_half,
            at_rows,
        ],
        out_specs=at_rows,
        compiler_params=pltpu.CompilerParams(vmem_limit_bytes=28 * 2**20),
    )(
        place,
        raw_all,
        scales,
        direct.reshape(by_micro),
        other.reshape(by_micro),
        above,
        above_other,
        top_grad,
    )
    return (input_grads[None], weight_grads)


def solution(mesh):
    in_specs = (
        P("section", None),
        P("section", None, "dp", "tensor"),
        P("section", "tensor"),
        P("section", "tensor", None),
        P("section", None, ("dp", "tensor"), None),
        P(None, "dp", "tensor"),
    )
    out_specs = (P("section", None, "dp", "tensor"), P("section", "tensor", "dp"))
    return jax.shard_map(shards, mesh=mesh, in_specs=in_specs, out_specs=out_specs, check_vma=False)
```

time: 339 us -> 183 us (0.54)
  waiting for transfers between devices: 247 us -> 7.55 us
  starting transfers between devices: 0.12 us -> 95.1 us
  other arithmetic: 21.3 us -> 6.37 us
  Pallas kernels: 0 us -> 14.5 us
  blocking collectives: 43.8 us -> 31.6 us
  local copies, waits for them, and re-layouts: 1.63 us -> 12.2 us
  matrix products: 8.82 us -> 0 us
    all_gather x2 -> x1, waiting for transfers between devices: 196 us -> 0.01 us  [shards(): raw_all = lax.all_gather(slots_later, 'section')]
    ppermute x0 -> x17, starting transfers between devices: none -> 63.9 us  [the longest x3 21.6 us: from_z(): return lax.ppermute(value, 'tensor', perm)]
    reduce_scatter x1 -> x0, waiting for transfers between devices: 50.2 us -> none  [shards(): lax.psum_scatter(local_weight, 'dp', scatter_dimension=1, tiled=True)]
    psum x1 -> x0, blocking collectives: 43.8 us -> none  [shards(): aligned = lax.psum(jnp.sum(gains * normed_grad * hidden_in, -1), 'tensor')]
    all_to_all x0 -> x2, blocking collectives: none -> 31.6 us  [the longest x1 22.9 us: z_exchange(): return lax.all_to_all(spread, 'tensor', 0, 0, axis_index_groups=z_groups())]
    all_to_all x0 -> x3, starting transfers between devices: none -> 31.2 us  [the longest x1 15.6 us: z_exchange(): return lax.all_to_all(spread, 'tensor', 0, 0, axis_index_groups=z_groups())]
    pallas_call x0 -> x6, Pallas kernels: none -> 14.5 us  [the longest x5 10.7 us: call(): pl.pallas_call(body, out_shape=out_shape, in_specs=specs, out_specs=jax.t...]
    select_n x9 -> x1, other arithmetic: 12.7 us -> 0.01 us  [shards(): jnp.where(plan[0, 0] == 0, squares, squares[::-1]).reshape(lines, LANES)]
  transfers between devices with their start and end apart: 3 -> 21, of which waited for: 3 -> 4; matrix products, arithmetic and copies ran while one was open for 2% -> 4% of each run, Pallas kernels for 0% -> 6%
where the time goes in v3:
time: 183 us; the launch traced here: 182 us
  starting transfers between devices  95.1 us (52%)
  blocking collectives  31.6 us (17%)
  Pallas kernels  14.5 us (8%)
  between operations  14.5 us (8%)
  local copies, waits for them, and re-layouts  12.2 us (7%)
  waiting for transfers between devices  7.55 us (4%)
  other arithmetic  6.37 us (3%)
    all_to_all x1, blocking collectives, z_exchange(): return lax.all_to_all(spread, 'tensor', 0, 0, axis_index_groups=z_groups())  22.9 us
    ppermute x3, starting transfers between devices, from_z(): return lax.ppermute(value, 'tensor', perm)  21.6 us
    ppermute x6, starting transfers between devices, from_y(): return lax.ppermute(value, 'tensor', perm)  20.4 us
    all_to_all x1, starting transfers between devices, z_exchange(): return lax.all_to_all(spread, 'tensor', 0, 0, axis_index_groups=z_groups())  15.6 us
    all_to_all x1, starting transfers between devices, shards(): scales = lax.all_to_all(scales, 'section', 0, 0)  11.9 us
    pallas_call x5, Pallas kernels, call(): pl.pallas_call(body, out_shape=out_shape, in_specs=specs, out_specs=jax.t...  10.7 us
    unnamed x36, local copies, waits for them, and re-layouts  10.3 us
    ppermute x3, starting transfers between devices, from_x(): return lax.ppermute(value, 'dp', [((x + step) % NX, x) for x in range(NX)])  9.45 us
  transfers between devices with their start and end apart: 21, of which 4 were waited for; matrix products, arithmetic and copies ran while one was open for 4% of the time, Pallas kernels for 6%

profile of v3, /device:TPU:1, one launch (start us, length us, event | category | flops | bytes accessed | tf_op | source)
XLA Modules:
  0.0 181.8 jit_solution(11514388923979371832)
XLA Ops:
  7.2 1.8 broadcast_in_dim.12
  9.0 15.6 %all-to-all-start = ((bf16[4,2,16,2048]{3,2,1,0:T(8,128)(2,1)}), bf16[4,2,16,2048]{3,2,1,0:T(8,128)(2,1)S(1)}, u32[]{:S(2)}, u32[]{:S(2)}) async-start(bf16[4,2,16,2048]{3,2,1,0:T(8,128)(2,1)} %broadcast_in_dim.12), calls=%async_computation | async-start | bytes 1048576 | tf_op jit(solution)/shard_map/all_to_all | solution.py:54
  24.6 4.6 %collective-permute-start = (bf16[2,16,2048]{2,1,0:T(8,128)(2,1)}, bf16[2,16,2048]{2,1,0:T(8,128)(2,1)S(1)}, u32[]{:S(2)}, u32[]{:S(2)}) collective-permute-start(bf16[2,16,2048]{2,1,0:T(8,128)(2,1)} %bitcast.27), channel_id=1, source_target_pairs={{16,0},{20,4},{24,8},{28,12},{32,16},{36,20},{40,24},{44,28},{48,3... | collective-permute-start | bytes 393224 | tf_op jit(solution)/shard_map/ppermute | solution.py:29
  29.3 1.2 multiply_reduce_fusion
  30.6 0.9 collective-permute-done.own1
  31.5 4.9 %collective-permute-start.3 = (f32[4,128]{1,0:T(4,128)S(1)}, f32[4,128]{1,0:T(4,128)S(1)}, u32[]{:S(2)}, u32[]{:S(2)}) collective-permute-start(f32[4,128]{1,0:T(4,128)S(1)} %bitcast.33), channel_id=1, source_target_pairs={{16,0},{20,4},{24,8},{28,12},{32,16},{36,20},{40,24},{44,28},{48,3... | collective-permute-start | bytes 6152 | tf_op jit(solution)/shard_map/ppermute | solution.py:29
  36.4 1.9 %collective-permute-start.4 = (f32[4,128]{1,0:T(4,128)S(1)}, f32[4,128]{1,0:T(4,128)S(1)}, u32[]{:S(2)}, u32[]{:S(2)}) collective-permute-start(f32[4,128]{1,0:T(4,128)S(1)} %bitcast.34), channel_id=1, source_target_pairs={{32,0},{36,4},{40,8},{44,12},{48,16},{52,20},{56,24},{60,28},{0,32... | collective-permute-start | bytes 6152 | tf_op jit(solution)/shard_map/ppermute | solution.py:29
  38.3 2.5 %collective-permute-start.5 = (f32[4,128]{1,0:T(4,128)S(1)}, f32[4,128]{1,0:T(4,128)S(1)}, u32[]{:S(2)}, u32[]{:S(2)}) collective-permute-start(f32[4,128]{1,0:T(4,128)S(1)} %bitcast.35), channel_id=1, source_target_pairs={{48,0},{52,4},{56,8},{60,12},{0,16},{4,20},{8,24},{12,28},{16,32},... | collective-permute-start | bytes 6152 | tf_op jit(solution)/shard_map/ppermute | solution.py:29
  40.8 4.3 %collective-permute-start.1 = (bf16[2,16,2048]{2,1,0:T(8,128)(2,1)S(1)}, bf16[2,16,2048]{2,1,0:T(8,128)(2,1)S(1)}, u32[]{:S(2)}, u32[]{:S(2)}) collective-permute-start(bf16[2,16,2048]{2,1,0:T(8,128)(2,1)S(1)} %bitcast.28), channel_id=1, source_target_pairs={{32,0},{36,4},{40,8},{44,12},{48,16},{52,20},{56,24},{60,28},{0,32... | collective-permute-start | bytes 393224 | tf_op jit(solution)/shard_map/ppermute | solution.py:29
  45.1 2.2 %collective-permute-start.2 = (bf16[2,16,2048]{2,1,0:T(8,128)(2,1)S(1)}, bf16[2,16,2048]{2,1,0:T(8,128)(2,1)S(1)}, u32[]{:S(2)}, u32[]{:S(2)}) collective-permute-start(bf16[2,16,2048]{2,1,0:T(8,128)(2,1)S(1)} %bitcast.29), channel_id=1, source_target_pairs={{48,0},{52,4},{56,8},{60,12},{0,16},{4,20},{8,24},{12,28},{16,32},... | collective-permute-start | bytes 393224 | tf_op jit(solution)/shard_map/ppermute | solution.py:29
  47.4 1.0 collective-permute-done.1.own2
  48.4 4.2 %collective-permute-done.2.own3 = bf16[2,16,2048]{2,1,0:T(8,128)(2,1)S(1)} collective-permute-done((bf16[2,16,2048]{2,1,0:T(8,128)(2,1)S(1)}, bf16[2,16,2048]{2,1,0:T(8,128)(2,1)S(1)}, u32[]{:S(2)}, u32[]{:S(2)}) %collective-permute-start.2) | collective-permute-done | bytes 131104 | tf_op jit(solution)/shard_map/ppermute | solution.py:29
  52.6 0.0 all-gather.3.cloned.1.call-update
  52.6 0.1 stack.23.place
  52.7 1.8 shard_map.77
  54.6 3.7 %all-to-all-start.1 = ((bf16[4,3,2,16,2048]{4,3,2,1,0:T(8,128)(2,1)}), bf16[4,3,2,16,2048]{4,3,2,1,0:T(8,128)(2,1)S(1)}, u32[]{:S(2)}, u32[]{:S(2)}) async-start(bf16[4,3,2,16,2048]{4,3,2,1,0:T(8,128)(2,1)} %shard_map.77), calls=%async_computation.1 | async-start | bytes 3145728 | tf_op jit(solution)/shard_map/all_to_all | solution.py:50
  58.3 7.6 %collective-permute-start.6 = (f32[4,128]{1,0:T(4,128)S(1)}, f32[4,128]{1,0:T(4,128)S(1)}, u32[]{:S(2)}, u32[]{:S(2)}) collective-permute-start(f32[4,128]{1,0:T(4,128)S(1)} %add_add_fusion.1), channel_id=1, source_target_pairs={{4,0},{8,4},{12,8},{0,12},{20,16},{24,20},{28,24},{16,28},{36,32},... | collective-permute-start | bytes 6152 | tf_op jit(solution)/shard_map/ppermute | solution.py:34
  65.8 2.2 %collective-permute-start.7 = (f32[4,128]{1,0:T(4,128)S(1)}, f32[4,128]{1,0:T(4,128)S(1)}, u32[]{:S(2)}, u32[]{:S(2)}) collective-permute-start(f32[4,128]{1,0:T(4,128)S(1)} %add_add_fusion.1), channel_id=1, source_target_pairs={{12,0},{0,4},{4,8},{8,12},{28,16},{16,20},{20,24},{24,28},{44,32},... | collective-permute-start | bytes 6152 | tf_op jit(solution)/shard_map/ppermute | solution.py:34
  68.1 11.8 %collective-permute-start.8 = (f32[4,128]{1,0:T(4,128)S(1)}, f32[4,128]{1,0:T(4,128)S(1)}, u32[]{:S(2)}, u32[]{:S(2)}) collective-permute-start(f32[4,128]{1,0:T(4,128)S(1)} %add_add_fusion.1), channel_id=1, source_target_pairs={{8,0},{12,4},{0,8},{4,12},{24,16},{28,20},{16,24},{20,28},{40,32},... | collective-permute-start | bytes 6152 | tf_op jit(solution)/shard_map/ppermute | solution.py:34
  79.9 1.3 collective-permute-done.8
  81.3 1.6 copy-done.2
  82.9 0.9 copy-done.14
  83.8 4.2 %shard_map.78 = (f32[512,512]{1,0:T(8,128)S(1)}, bf16[512,512]{1,0:T(8,128)(2,1)S(1)}, f32[4,4,128]{2,1,0:T(4,128)S(1)}) custom-call(s32[6]{0:T(128)S(1)} %stack.23.place, bf16[2,16,2048]{2,1,0:T(8,128)(2,1)S(1)} %bitcast.30, bf16[2,16,2048]{2,1,0:T(8,128)(2,1)S(1)} %collective-permute-done.own1, bf16[2,16,2048]{2,1,0:T(8,128)(2,1)S(1)} %collective-permute-done.1.own2, ...), custom_call_target="tpu_custom_call" | custom-call | flops 1073741824 | bytes 6291456 | tf_op jit(solution)/shard_map/pallas_call | solution.py:58
  87.9 6.7 %collective-permute-start.9 = (bf16[512,512]{1,0:T(8,128)(2,1)S(1)}, bf16[512,512]{1,0:T(8,128)(2,1)S(1)}, u32[]{:S(2)}, u32[]{:S(2)}) collective-permute-start(bf16[512,512]{1,0:T(8,128)(2,1)S(1)} %get-tuple-element.41), channel_id=1, source_target_pairs={{0,64},{64,0},{128,192},{192,128},{256,320},{320,256},{384,448},{4... | collective-permute-start | bytes 1572872 | tf_op jit(solution)/shard_map/ppermute | solution.py:42
  94.6 8.6 %all_to_all.25 = f32[4,4,128]{2,1,0:T(4,128)} all-to-all(f32[4,4,128]{2,1,0:T(4,128)S(1)} %get-tuple-element.42), channel_id=1, replica_groups={{0,16,32,48},{4,20,36,52},{8,24,40,56},{12,28,44,60},{1,17,33,49},{5,21..., dimensions={0} | all-to-all | bytes 16384 | tf_op jit(solution)/shard_map/all_to_all | solution.py:50
  103.3 0.6 shard_map.79
  103.9 0.8 copy-done.3
  104.7 1.3 collective-permute-start.10
  106.0 1.3 collective-permute-start.11
  107.3 1.3 collective-permute-start.12
  108.6 0.7 reduce_sum.19
  109.3 0.9 copy-done.10
  110.2 0.9 copy-done.12
  111.1 0.9 copy-done.15
  112.0 2.9 %shard_map.82 = (f32[512,512]{1,0:T(8,128)S(1)}, bf16[512,512]{1,0:T(8,128)(2,1)}, bf16[512,512]{1,0:T(8,128)(2,1)}, bf16[512,512]{1,0:T(8,128)(2,1)}) custom-call(s32[6]{0:T(128)S(1)} %stack.23.place, bf16[2,16,2048]{2,1,0:T(8,128)(2,1)S(1)} %bitcast.31, bf16[2,16,2048]{2,1,0:T(8,128)(2,1)S(1)} %copy-done.10, bf16[2,16,2048]{2,1,0:T(8,128)(2,1)S(1)} %copy-done.12, ...), custom_call_target="tpu_custom_call" | custom-call | flops 1073741824 | bytes 6291456 | tf_op jit(solution)/shard_map/pallas_call | solution.py:58
  114.9 1.0 copy-done.5
  115.9 4.5 %collective-permute-start.14 = (bf16[512,512]{1,0:T(8,128)(2,1)}, bf16[512,512]{1,0:T(8,128)(2,1)}, u32[]{:S(2)}, u32[]{:S(2)}) collective-permute-start(bf16[512,512]{1,0:T(8,128)(2,1)} %get-tuple-element.53), channel_id=1, source_target_pairs={{1,0},{2,1},{3,2},{0,3},{5,4},{6,5},{7,6},{4,7},{9,8},{10,9},{11,1... | collective-permute-start | bytes 1572872 | tf_op jit(solution)/shard_map/ppermute | solution.py:38
  120.4 2.4 %collective-permute-start.15 = (bf16[512,512]{1,0:T(8,128)(2,1)}, bf16[512,512]{1,0:T(8,128)(2,1)}, u32[]{:S(2)}, u32[]{:S(2)}) collective-permute-start(bf16[512,512]{1,0:T(8,128)(2,1)} %get-tuple-element.54), channel_id=1, source_target_pairs={{2,0},{3,1},{0,2},{1,3},{6,4},{7,5},{4,6},{5,7},{10,8},{11,9},{8,1... | collective-permute-start | bytes 1572872 | tf_op jit(solution)/shard_map/ppermute | solution.py:38
  122.9 2.5 %collective-permute-start.16 = (bf16[512,512]{1,0:T(8,128)(2,1)}, bf16[512,512]{1,0:T(8,128)(2,1)}, u32[]{:S(2)}, u32[]{:S(2)}) collective-permute-start(bf16[512,512]{1,0:T(8,128)(2,1)} %get-tuple-element.55), channel_id=1, source_target_pairs={{3,0},{0,1},{1,2},{2,3},{7,4},{4,5},{5,6},{6,7},{11,8},{8,9},{9,10... | collective-permute-start | bytes 1572872 | tf_op jit(solution)/shard_map/ppermute | solution.py:38
  125.4 22.9 %all_to_all.26.parts = f32[4,4,128]{2,1,0:T(4,128)S(1)} all-to-all(f32[4,4,128]{2,1,0:T(4,128)S(1)} %broadcast_in_dim.13), channel_id=1, replica_groups={{0,4,8,12},{16,20,24,28},{32,36,40,44},{48,52,56,60},{1,5,9,13},{17,21,..., dimensions={0} | all-to-all | bytes 16384 | tf_op jit(solution)/shard_map/all_to_all | solution.py:54
  148.3 1.2 shard_map.80
  149.5 11.9 %all-to-all-start.4 = ((f32[8,8,128]{2,1,0:T(8,128)}), f32[8,8,128]{2,1,0:T(8,128)}, u32[]{:S(2)}, u32[]{:S(2)}) async-start(f32[8,8,128]{2,1,0:T(8,128)} %shard_map.80), calls=%async_computation.4 | async-start | bytes 65536 | tf_op jit(solution)/shard_map/all_to_all | solution.py:256
  161.4 2.0 %fusion.1 = (bf16[256,512]{1,0:T(8,128)(2,1)}, f32[256,512]{1,0:T(8,128)S(1)}) fusion(bf16[256,512]{1,0:T(8,128)(2,1)} %collective-permute-done.12, bf16[256,512]{1,0:T(8,128)(2,1)} %collective-permute-done.11, bf16[256,512]{1,0:T(8,128)(2,1)} %collective-permute-done.10), kind=kLoop, calls=%fused_computation.7 | loop fusion | flops 786432 | bytes 1572864 | tf_op jit(solution)/shard_map/convert_element_type | solution.py:234
  163.4 1.9 %collective-permute-start.13 = (bf16[256,512]{1,0:T(8,128)(2,1)}, bf16[256,512]{1,0:T(8,128)(2,1)S(1)}, u32[]{:S(2)}, u32[]{:S(2)}) collective-permute-start(bf16[256,512]{1,0:T(8,128)(2,1)} %get-tuple-element.56), channel_id=1, source_target_pairs={{0,64},{64,0},{128,192},{192,128},{256,320},{320,256},{384,448},{4... | collective-permute-start | bytes 786440 | tf_op jit(solution)/shard_map/ppermute | solution.py:42
  165.4 2.4 %fusion = bf16[1,512,512]{2,1,0:T(8,128)(2,1)} fusion(f32[512,512]{1,0:T(8,128)S(1)} %copy-done.6, bf16[512,512]{1,0:T(8,128)(2,1)} %collective-permute-done.16, bf16[512,512]{1,0:T(8,128)(2,1)} %collective-permute-done.15, bf16[512,512]{1,0:T(8,128)(2,1)} %collective-permute-done.14), kind=kLoop, calls=%fused_computation.2 | loop fusion | flops 2097152 | bytes 3145728 | tf_op jit(solution)/shard_map/broadcast_in_dim | solution.py:247
  167.9 2.2 %copy-done.1 = bf16[16,256,512]{2,1,0:T(8,128)(2,1)S(1)} copy-done((bf16[16,256,512]{2,1,0:T(8,128)(2,1)S(1)}, bf16[16,256,512]{2,1,0:T(8,128)(2,1)}, u32[]{:S(2)}) %copy-start.1) | copy-done | bytes 4194328
  170.1 1.0 copy-done.8
  171.1 3.9 %shard_map.81 = bf16[2,256,512]{2,1,0:T(8,128)(2,1)} custom-call(s32[6]{0:T(128)S(1)} %stack.23.place, bf16[8,2,256,512]{3,2,1,0:T(8,128)(2,1)S(1)} %bitcast.22, f32[8,8,128]{2,1,0:T(8,128)} %all-to-all-done.4.scales, f32[2,256,512]{2,1,0:T(8,128)S(1)} %bitcast.23, bf16[2,256,512]{2,1,0:T(8,128)(2,1)S(1)} %bitcast.25, ...), custom_call_target="tpu_custom_call" | custom-call | tf_op jit(solution)/shard_map/pallas_call | solution.py:261
  (50 shorter events, 0.1 us)
Async XLA Ops:
  7.2 33.6 %copy-start.7 = (bf16[1,2,16,2048]{3,2,1,0:T(8,128)(2,1)S(1)}, bf16[1,2,16,2048]{3,2,1,0:T(8,128)(2,1)}, u32[]{:S(2)}) copy-start(bf16[1,2,16,2048]{3,2,1,0:T(8,128)(2,1)} %param.10) | copy-start | bytes 393220
  7.2 23.3 %copy-start.17 = (s32[1,2]{1,0:T(1,128)S(1)}, s32[1,2]{1,0:T(1,128)}, u32[]{:S(2)}) copy-start(s32[1,2]{1,0:T(1,128)} %param.6) | copy-start | bytes 28
  9.0 43.6 %all-to-all-start = ((bf16[4,2,16,2048]{3,2,1,0:T(8,128)(2,1)}), bf16[4,2,16,2048]{3,2,1,0:T(8,128)(2,1)S(1)}, u32[]{:S(2)}, u32[]{:S(2)}) async-start(bf16[4,2,16,2048]{3,2,1,0:T(8,128)(2,1)} %broadcast_in_dim.12), calls=%async_computation | async-start | bytes 1048576 | tf_op jit(solution)/shard_map/all_to_all | solution.py:54
  24.6 143.2 %all-gather.3.cloned.1.call-start = ((), (), s32[]{:S(2)}) async-start(), calls=%async_computation.5 | async-start | bytes 4718592 | tf_op jit(solution)/shard_map/all_gather | solution.py:208
  24.6 6.9 %collective-permute-start = (bf16[2,16,2048]{2,1,0:T(8,128)(2,1)}, bf16[2,16,2048]{2,1,0:T(8,128)(2,1)S(1)}, u32[]{:S(2)}, u32[]{:S(2)}) collective-permute-start(bf16[2,16,2048]{2,1,0:T(8,128)(2,1)} %bitcast.27), channel_id=1, source_target_pairs={{16,0},{20,4},{24,8},{28,12},{32,16},{36,20},{40,24},{44,28},{48,3... | collective-permute-start | bytes 393224 | tf_op jit(solution)/shard_map/ppermute | solution.py:29
  31.5 49.7 %copy-start.9 = (bf16[2,16,2048]{2,1,0:T(8,128)(2,1)}, bf16[2,16,2048]{2,1,0:T(8,128)(2,1)S(1)}, u32[]{:S(2)}) copy-start(bf16[2,16,2048]{2,1,0:T(8,128)(2,1)S(1)} %collective-permute-done.own1) | copy-start | bytes 393220
  31.5 15.8 %collective-permute-start.3 = (f32[4,128]{1,0:T(4,128)S(1)}, f32[4,128]{1,0:T(4,128)S(1)}, u32[]{:S(2)}, u32[]{:S(2)}) collective-permute-start(f32[4,128]{1,0:T(4,128)S(1)} %bitcast.33), channel_id=1, source_target_pairs={{16,0},{20,4},{24,8},{28,12},{32,16},{36,20},{40,24},{44,28},{48,3... | collective-permute-start | bytes 6152 | tf_op jit(solution)/shard_map/ppermute | solution.py:29
  36.4 11.0 %collective-permute-start.4 = (f32[4,128]{1,0:T(4,128)S(1)}, f32[4,128]{1,0:T(4,128)S(1)}, u32[]{:S(2)}, u32[]{:S(2)}) collective-permute-start(f32[4,128]{1,0:T(4,128)S(1)} %bitcast.34), channel_id=1, source_target_pairs={{32,0},{36,4},{40,8},{44,12},{48,16},{52,20},{56,24},{60,28},{0,32... | collective-permute-start | bytes 6152 | tf_op jit(solution)/shard_map/ppermute | solution.py:29
  38.3 9.0 %collective-permute-start.5 = (f32[4,128]{1,0:T(4,128)S(1)}, f32[4,128]{1,0:T(4,128)S(1)}, u32[]{:S(2)}, u32[]{:S(2)}) collective-permute-start(f32[4,128]{1,0:T(4,128)S(1)} %bitcast.35), channel_id=1, source_target_pairs={{48,0},{52,4},{56,8},{60,12},{0,16},{4,20},{8,24},{12,28},{16,32},... | collective-permute-start | bytes 6152 | tf_op jit(solution)/shard_map/ppermute | solution.py:29
  40.8 7.5 %collective-permute-start.1 = (bf16[2,16,2048]{2,1,0:T(8,128)(2,1)S(1)}, bf16[2,16,2048]{2,1,0:T(8,128)(2,1)S(1)}, u32[]{:S(2)}, u32[]{:S(2)}) collective-permute-start(bf16[2,16,2048]{2,1,0:T(8,128)(2,1)S(1)} %bitcast.28), channel_id=1, source_target_pairs={{32,0},{36,4},{40,8},{44,12},{48,16},{52,20},{56,24},{60,28},{0,32... | collective-permute-start | bytes 393224 | tf_op jit(solution)/shard_map/ppermute | solution.py:29
  45.1 7.4 %collective-permute-start.2 = (bf16[2,16,2048]{2,1,0:T(8,128)(2,1)S(1)}, bf16[2,16,2048]{2,1,0:T(8,128)(2,1)S(1)}, u32[]{:S(2)}, u32[]{:S(2)}) collective-permute-start(bf16[2,16,2048]{2,1,0:T(8,128)(2,1)S(1)} %bitcast.29), channel_id=1, source_target_pairs={{48,0},{52,4},{56,8},{60,12},{0,16},{4,20},{8,24},{12,28},{16,32},... | collective-permute-start | bytes 393224 | tf_op jit(solution)/shard_map/ppermute | solution.py:29
  48.4 32.9 %copy-start.11 = (bf16[2,16,2048]{2,1,0:T(8,128)(2,1)}, bf16[2,16,2048]{2,1,0:T(8,128)(2,1)S(1)}, u32[]{:S(2)}) copy-start(bf16[2,16,2048]{2,1,0:T(8,128)(2,1)S(1)} %collective-permute-done.1.own2) | copy-start | bytes 393220
  52.6 2.0 %copy-start.13 = (bf16[2,16,2048]{2,1,0:T(8,128)(2,1)}, bf16[2,16,2048]{2,1,0:T(8,128)(2,1)S(1)}, u32[]{:S(2)}) copy-start(bf16[2,16,2048]{2,1,0:T(8,128)(2,1)S(1)} %collective-permute-done.2.own3) | copy-start | bytes 393220
  54.6 26.7 %copy-start = (bf16[1,2,256,512]{3,2,1,0:T(8,128)(2,1)S(1)}, bf16[1,2,256,512]{3,2,1,0:T(8,128)(2,1)}, u32[]{:S(2)}) copy-start(bf16[1,2,256,512]{3,2,1,0:T(8,128)(2,1)} %param.7) | copy-start | bytes 1572868
  54.6 26.7 %copy-start.16 = (bf16[1,512]{1,0:T(2,128)(2,1)S(1)}, bf16[1,512]{1,0:T(2,128)(2,1)}, u32[]{:S(2)}) copy-start(bf16[1,512]{1,0:T(2,128)(2,1)} %gains.3) | copy-start | bytes 3076
  54.6 26.7 %all-to-all-start.1 = ((bf16[4,3,2,16,2048]{4,3,2,1,0:T(8,128)(2,1)}), bf16[4,3,2,16,2048]{4,3,2,1,0:T(8,128)(2,1)S(1)}, u32[]{:S(2)}, u32[]{:S(2)}) async-start(bf16[4,3,2,16,2048]{4,3,2,1,0:T(8,128)(2,1)} %shard_map.77), calls=%async_computation.1 | async-start | bytes 3145728 | tf_op jit(solution)/shard_map/all_to_all | solution.py:50
  58.3 21.6 %collective-permute-start.6 = (f32[4,128]{1,0:T(4,128)S(1)}, f32[4,128]{1,0:T(4,128)S(1)}, u32[]{:S(2)}, u32[]{:S(2)}) collective-permute-start(f32[4,128]{1,0:T(4,128)S(1)} %add_add_fusion.1), channel_id=1, source_target_pairs={{4,0},{8,4},{12,8},{0,12},{20,16},{24,20},{28,24},{16,28},{36,32},... | collective-permute-start | bytes 6152 | tf_op jit(solution)/shard_map/ppermute | solution.py:34
  65.8 14.0 %collective-permute-start.7 = (f32[4,128]{1,0:T(4,128)S(1)}, f32[4,128]{1,0:T(4,128)S(1)}, u32[]{:S(2)}, u32[]{:S(2)}) collective-permute-start(f32[4,128]{1,0:T(4,128)S(1)} %add_add_fusion.1), channel_id=1, source_target_pairs={{12,0},{0,4},{4,8},{8,12},{28,16},{16,20},{20,24},{24,28},{44,32},... | collective-permute-start | bytes 6152 | tf_op jit(solution)/shard_map/ppermute | solution.py:34
  68.1 13.2 %collective-permute-start.8 = (f32[4,128]{1,0:T(4,128)S(1)}, f32[4,128]{1,0:T(4,128)S(1)}, u32[]{:S(2)}, u32[]{:S(2)}) collective-permute-start(f32[4,128]{1,0:T(4,128)S(1)} %add_add_fusion.1), channel_id=1, source_target_pairs={{8,0},{12,4},{0,8},{4,12},{24,16},{28,20},{16,24},{20,28},{40,32},... | collective-permute-start | bytes 6152 | tf_op jit(solution)/shard_map/ppermute | solution.py:34
  81.3 1.6 copy-start.2
  82.9 0.9 copy-start.14
  87.9 15.3 %collective-permute-start.9 = (bf16[512,512]{1,0:T(8,128)(2,1)S(1)}, bf16[512,512]{1,0:T(8,128)(2,1)S(1)}, u32[]{:S(2)}, u32[]{:S(2)}) collective-permute-start(bf16[512,512]{1,0:T(8,128)(2,1)S(1)} %get-tuple-element.41), channel_id=1, source_target_pairs={{0,64},{64,0},{128,192},{192,128},{256,320},{320,256},{384,448},{4... | collective-permute-start | bytes 1572872 | tf_op jit(solution)/shard_map/ppermute | solution.py:42
  103.9 0.8 copy-start.3
  104.7 18.2 %collective-permute-start.10 = (bf16[256,512]{1,0:T(8,128)(2,1)S(1)}, bf16[256,512]{1,0:T(8,128)(2,1)}, u32[]{:S(2)}, u32[]{:S(2)}) collective-permute-start(bf16[256,512]{1,0:T(8,128)(2,1)S(1)} %shard_map.79), channel_id=1, source_target_pairs={{128,0},{192,64},{256,128},{320,192},{384,256},{448,320},{129,1},{... | collective-permute-start | bytes 786440 | tf_op jit(solution)/shard_map/ppermute | solution.py:46
  106.0 55.5 %collective-permute-start.11 = (bf16[256,512]{1,0:T(8,128)(2,1)S(1)}, bf16[256,512]{1,0:T(8,128)(2,1)}, u32[]{:S(2)}, u32[]{:S(2)}) collective-permute-start(bf16[256,512]{1,0:T(8,128)(2,1)S(1)} %shard_map.79), channel_id=1, source_target_pairs={{256,0},{320,64},{384,128},{448,192},{257,1},{321,65},{385,129},{4... | collective-permute-start | bytes 786440 | tf_op jit(solution)/shard_map/ppermute | solution.py:46
  107.3 54.2 %collective-permute-start.12 = (bf16[256,512]{1,0:T(8,128)(2,1)S(1)}, bf16[256,512]{1,0:T(8,128)(2,1)}, u32[]{:S(2)}, u32[]{:S(2)}) collective-permute-start(bf16[256,512]{1,0:T(8,128)(2,1)S(1)} %shard_map.79), channel_id=1, source_target_pairs={{384,0},{448,64},{385,1},{449,65},{386,2},{450,66},{387,3},{451,67... | collective-permute-start | bytes 786440 | tf_op jit(solution)/shard_map/ppermute | solution.py:46
  109.3 0.9 copy-start.10
  110.2 0.9 copy-start.12
  111.1 0.9 copy-start.15
  114.9 1.0 copy-start.5
  115.9 49.4 %copy-start.6 = (f32[512,512]{1,0:T(8,128)S(1)}, f32[512,512]{1,0:T(8,128)}, u32[]{:S(2)}) copy-start(f32[512,512]{1,0:T(8,128)} %copy-done.5) | copy-start | bytes 3145732
  115.9 49.4 %collective-permute-start.14 = (bf16[512,512]{1,0:T(8,128)(2,1)}, bf16[512,512]{1,0:T(8,128)(2,1)}, u32[]{:S(2)}, u32[]{:S(2)}) collective-permute-start(bf16[512,512]{1,0:T(8,128)(2,1)} %get-tuple-element.53), channel_id=1, source_target_pairs={{1,0},{2,1},{3,2},{0,3},{5,4},{6,5},{7,6},{4,7},{9,8},{10,9},{11,1... | collective-permute-start | bytes 1572872 | tf_op jit(solution)/shard_map/ppermute | solution.py:38
  120.4 44.9 %collective-permute-start.15 = (bf16[512,512]{1,0:T(8,128)(2,1)}, bf16[512,512]{1,0:T(8,128)(2,1)}, u32[]{:S(2)}, u32[]{:S(2)}) collective-permute-start(bf16[512,512]{1,0:T(8,128)(2,1)} %get-tuple-element.54), channel_id=1, source_target_pairs={{2,0},{3,1},{0,2},{1,3},{6,4},{7,5},{4,6},{5,7},{10,8},{11,9},{8,1... | collective-permute-start | bytes 1572872 | tf_op jit(solution)/shard_map/ppermute | solution.py:38
  122.9 42.5 %collective-permute-start.16 = (bf16[512,512]{1,0:T(8,128)(2,1)}, bf16[512,512]{1,0:T(8,128)(2,1)}, u32[]{:S(2)}, u32[]{:S(2)}) collective-permute-start(bf16[512,512]{1,0:T(8,128)(2,1)} %get-tuple-element.55), channel_id=1, source_target_pairs={{3,0},{0,1},{1,2},{2,3},{7,4},{4,5},{5,6},{6,7},{11,8},{8,9},{9,10... | collective-permute-start | bytes 1572872 | tf_op jit(solution)/shard_map/ppermute | solution.py:38
  149.5 18.3 %all-to-all-start.4 = ((f32[8,8,128]{2,1,0:T(8,128)}), f32[8,8,128]{2,1,0:T(8,128)}, u32[]{:S(2)}, u32[]{:S(2)}) async-start(f32[8,8,128]{2,1,0:T(8,128)} %shard_map.80), calls=%async_computation.4 | async-start | bytes 65536 | tf_op jit(solution)/shard_map/all_to_all | solution.py:256
  161.4 6.4 %copy-start.4 = (bf16[512,512]{1,0:T(8,128)(2,1)S(1)}, bf16[512,512]{1,0:T(8,128)(2,1)}, u32[]{:S(2)}) copy-start(bf16[512,512]{1,0:T(8,128)(2,1)} %copy-done.3) | copy-start | bytes 1572868
  163.4 4.4 %collective-permute-start.13 = (bf16[256,512]{1,0:T(8,128)(2,1)}, bf16[256,512]{1,0:T(8,128)(2,1)S(1)}, u32[]{:S(2)}, u32[]{:S(2)}) collective-permute-start(bf16[256,512]{1,0:T(8,128)(2,1)} %get-tuple-element.56), channel_id=1, source_target_pairs={{0,64},{64,0},{128,192},{192,128},{256,320},{320,256},{384,448},{4... | collective-permute-start | bytes 786440 | tf_op jit(solution)/shard_map/ppermute | solution.py:42
  167.9 2.2 %copy-start.1 = (bf16[16,256,512]{2,1,0:T(8,128)(2,1)S(1)}, bf16[16,256,512]{2,1,0:T(8,128)(2,1)}, u32[]{:S(2)}) copy-start(bf16[16,256,512]{2,1,0:T(8,128)(2,1)} %all-gather.3.cloned.1.call-done) | copy-start | bytes 12582916
  170.1 1.0 copy-start.8
Sparse Core Ops, SparseCore 0:
  52.7 63.1 all-gather.2

commit v4 on v3

v4 whole, which is shorter than its diff:
```python
import functools

import jax
import jax.numpy as jnp
from jax import lax
from jax.experimental import pallas as pl
from jax.experimental.pallas import tpu as pltpu
from jax.sharding import PartitionSpec as P

EPSILON = 1e-06
NY, NZ, NX, NS = 4, 4, 4, 8
MICRO, ROWS, LANES = 2, 16, 128
BLOCKS = NY * NZ
SHARE, HALF = MICRO * ROWS, BLOCKS * ROWS
LINES = MICRO * HALF // LANES
F32, BF16 = jnp.float32, jnp.bfloat16
VMEM = pl.BlockSpec(memory_space=pltpu.VMEM)
SMEM = pl.BlockSpec(memory_space=pltpu.SMEM)


def y_groups():
    return [[y * NZ + z for y in range(NY)] for z in range(NZ)]


def z_groups():
    return [[y * NZ + z for z in range(NZ)] for y in range(NY)]


def from_y(value, step):
    perm = [((y + step) % NY * NZ + z, y * NZ + z) for y in range(NY) for z in range(NZ)]
    return lax.ppermute(value, "tensor", perm)


def from_z(value, step):
    perm = [(y * NZ + (z + step) % NZ, y * NZ + z) for y in range(NY) for z in range(NZ)]
    return lax.ppermute(value, "tensor", perm)


def from_other_core(value):
    return lax.ppermute(value, "section", [(s, s ^ 1) for s in range(NS)])


def from_chips_above(value, chips):
    return lax.ppermute(value, "section", [(s, s - 2 * chips) for s in range(2 * chips, NS)])


def y_exchange(spread):
    return lax.all_to_all(spread, "tensor", 0, 0, axis_index_groups=y_groups())


def z_exchange(spread):
    return lax.all_to_all(spread, "tensor", 0, 0, axis_index_groups=z_groups())


def call(body, out_shape, specs, args, scratch=(), cost=None):
    return pl.pallas_call(
        body,
        out_shape=out_shape,
        in_specs=specs,
        out_specs=jax.tree.map(lambda _: VMEM, out_shape),
        scratch_shapes=list(scratch),
        compiler_params=pltpu.CompilerParams(vmem_limit_bytes=14 * 2**20),
        cost_estimate=cost,
    )(*args)


def columns(row, count):
    return jnp.transpose(jnp.broadcast_to(row, (LANES, LANES)))[:, :1] + jnp.zeros((LANES, count), F32)


def parted(value):
    high = value.astype(BF16)
    rest = value - high.astype(F32)
    middle = rest.astype(BF16)
    low = (rest - middle.astype(F32)).astype(BF16)
    unused = jnp.zeros((SHARE - 3 * LINES, LANES), F32)
    stacked = [part.astype(F32) for part in (high, middle, low)]
    return jnp.concatenate(stacked + [unused]).astype(BF16)


def joined(block):
    block = block.astype(F32)
    return block[:LINES] + (block[LINES : 2 * LINES] + block[2 * LINES : 3 * LINES])


def row_sums(terms):
    folded = sum(terms[:, k * LANES : (k + 1) * LANES] for k in range(terms.shape[1] // LANES))
    return jnp.sum(jnp.transpose(folded), axis=0, keepdims=True)


def pack_body(place, kv_ref, stashed, out_ref):
    kvw = kv_ref.shape[1]
    swap = place[2]
    sums = []
    for chunk in range(LINES):
        m, at = chunk * LANES // HALF, chunk * LANES % HALF
        hidden = stashed[m ^ swap, at : at + LANES].astype(F32)
        sums.append(row_sums(hidden * hidden))
    squares = parted(jnp.concatenate(sums))
    for z in range(NZ):
        out_ref[z, :, :kvw] = kv_ref[...]
        out_ref[z, :, kvw:] = squares


def spread_body(place, kv_ref, out_ref):
    kvw = kv_ref.shape[2] - LANES
    squares = parted(sum(joined(kv_ref[z, :, kvw:]) for z in range(NZ)))
    for step in range(1, NZ):
        block = kv_ref[lax.rem(place[0] + step, NZ), :, :kvw]
        rows = slice((step - 1) * SHARE, step * SHARE)
        for y in range(NY):
            out_ref[y, rows, :kvw] = block
            out_ref[y, rows, kvw:] = squares


def back_body(place, own0, own1, own2, own3, others, weight, gains, stashed, direct, direct16, aligned, squares, grad):
    tz, ty, swap = place[0], place[1], place[2]
    kvw = weight.shape[1]
    width = weight.shape[0]
    model_width = width * BLOCKS
    dims = (((1,), (1,)), ((), ()))
    squares[...] = sum(joined(others[y, :SHARE, kvw:]) for y in range(NY))

    def put(product, blocks):
        for at, (y, step) in enumerate(blocks):
            for m in range(MICRO):
                row = (at * MICRO + m) * ROWS
                grad[m, y * NZ + lax.rem(tz + step, NZ)] = product[row : row + ROWS]

    mine = jnp.concatenate([ref[...] for ref in (own0, own1, own2, own3)])
    product = lax.dot_general(mine, weight[...], dims, preferred_element_type=F32)
    put(product, [(lax.rem(ty + k, NY), 0) for k in range(NY)])
    for y in range(NY):
        product = lax.dot_general(others[y, :, :kvw], weight[...], dims, preferred_element_type=F32)
        put(product, [(y, step) for step in range(1, NZ)])
    gain = gains[...].astype(F32)
    per = LANES // ROWS
    for chunk in range(MICRO * BLOCKS // per):
        m, first = chunk * per // BLOCKS, chunk * per % BLOCKS
        gained = grad[m, first : first + per].reshape(LANES, width) * gain
        hidden = stashed[m ^ swap, first * ROWS : (first + per) * ROWS].astype(F32)
        inverse = 1.0 / jnp.sqrt(squares[chunk : chunk + 1] / model_width + EPSILON)
        here = gained * columns(inverse, width)
        direct[chunk * LANES : (chunk + 1) * LANES] = here
        direct16[chunk * LANES : (chunk + 1) * LANES] = here.astype(BF16)
        total = row_sums(gained * hidden)
        for y in range(NY):
            aligned[y, chunk : chunk + 1] = total


def half_body(place, direct, other, out_ref):
    rows = out_ref.shape[0]
    at = pl.ds(pl.multiple_of(place[3] * rows, rows), rows)
    out_ref[...] = (direct[at] + other[at].astype(F32)).astype(BF16)


def outer_body(place, own0, own1, own2, own3, others, gains, stashed, squares, out_ref, normed, left):
    tz, ty, swap = place[0], place[1], place[2]
    width = out_ref.shape[1]
    model_width = width * BLOCKS
    gain = gains[...].astype(F32)
    per = LANES // ROWS
    for chunk in range(MICRO * BLOCKS // per):
        m, first = chunk * per // BLOCKS, chunk * per % BLOCKS
        hidden = stashed[m ^ swap, first * ROWS : (first + per) * ROWS].astype(F32)
        inverse = 1.0 / jnp.sqrt(squares[chunk : chunk + 1] / model_width + EPSILON)
        here = gain * hidden * columns(inverse, width)
        normed[m, first : first + per] = here.astype(BF16).reshape(per, ROWS, width)
    blocks = [(lax.rem(ty + k, NY), 0) for k in range(NY)]
    blocks += [(y, step) for y in range(NY) for step in range(1, NZ)]
    for at, (y, step) in enumerate(blocks):
        for m in range(MICRO):
            row = (at * MICRO + m) * ROWS
            left[row : row + ROWS] = normed[m, y * NZ + lax.rem(tz + step, NZ)]
    turned = jnp.transpose(left[...])
    for x in range(NX):
        at = slice(x * width, (x + 1) * width)
        mine = [ref[:, at] for ref in (own0, own1, own2, own3)]
        right = jnp.concatenate(mine + [others[y, :, at] for y in range(NY)])
        out_ref[x] = jnp.dot(turned, right, preferred_element_type=F32).astype(out_ref.dtype)


def scale_body(place, parts, squares, out_ref, *, model_width):
    mean = squares[...] / model_width + EPSILON
    total = parts[0] + parts[1] + parts[2] + parts[3]
    scale = total / (model_width * (mean * jnp.sqrt(mean)))
    swap = jnp.full((NS - LINES, LANES), place[2], jnp.int32).astype(F32)
    value = jnp.concatenate([scale, swap])
    for section in range(NS):
        out_ref[section] = value


def total_body(place, raw, scales, direct, other, above1, above2, above3, above_other, top, out_ref):
    section, core = place[4], place[3]
    rows, width = raw.shape[2], raw.shape[3]
    chunk = pl.program_id(0)
    use_other = jnp.where(core == 0, 1.0, 0.0)
    fixes = [jnp.zeros((rows, width), F32) for _ in range(MICRO)]
    turned = []
    for m in range(MICRO):
        row = m * (BLOCKS * ROWS // LANES) + chunk
        turned.append(jnp.transpose(scales[:, pl.ds(row, 1)].reshape(NS, LANES)))
    for u in range(NS):
        live = jnp.where(u >= section, 1.0, 0.0)
        swapped = scales[u, NS - 1 : NS, :1] != 0.0
        slots = [raw[u, k].astype(F32) for k in range(MICRO)]
        for m in range(MICRO):
            hidden = jnp.where(swapped, slots[1 - m], slots[m])
            fixes[m] = fixes[m] + hidden * (turned[m][:, u : u + 1] * live)
    above = above1[...].astype(F32) + above2[...].astype(F32) + above3[...].astype(F32)
    for m in range(MICRO):
        mine = jnp.where(core == m, above, above_other[...].astype(F32))
        value = top[m].astype(F32) + direct[m] + use_other * other[m].astype(F32) + mine - fixes[m]
        out_ref[m] = value.astype(BF16)


def shards(plan, stashed, norm_gain, kv_weight, kv_grad, top_grad):
    section = lax.axis_index("section")
    core = section % 2
    index = lax.axis_index("tensor")
    tz, ty = index % NZ, index // NZ
    width = stashed.shape[-1]
    tokens = MICRO * BLOCKS * ROWS
    model_width = width * BLOCKS
    lines = tokens // LANES
    place = jnp.stack([tz, ty, plan[0, 0], core, section]).astype(jnp.int32)
    slots, weight = stashed[0], kv_weight[0]
    kvw = weight.shape[-1]
    kv0 = kv_grad.reshape(SHARE, kvw)
    half = (tokens // 2, width)

    shape = jax.ShapeDtypeStruct((NZ, SHARE, kvw + LANES), BF16)
    packed = call(pack_body, shape, [SMEM, VMEM, VMEM], (place, kv0, slots))
    packed, kv_y = lax.optimization_barrier((packed, kv0))
    kv_z = z_exchange(packed)
    own = [kv_y] + [from_y(kv_y, d) for d in (1, 2, 3)]
    kv_z, own, slots_later = lax.optimization_barrier((kv_z, own, slots))

    raw_all = lax.all_gather(slots_later, "section")
    shape = jax.ShapeDtypeStruct((NY, (NZ - 1) * SHARE, kvw + LANES), BF16)
    others = y_exchange(call(spread_body, shape, [SMEM, VMEM], (place, kv_z)))

    flops = 2 * tokens * width * kvw
    direct, direct16, aligned, squares = call(
        back_body,
        (
            jax.ShapeDtypeStruct((tokens, width), F32),
            jax.ShapeDtypeStruct((tokens, width), BF16),
            jax.ShapeDtypeStruct((NY, lines, LANES), F32),
            jax.ShapeDtypeStruct((lines, LANES), F32),
        ),
        [SMEM] + [VMEM] * 8,
        (place, *own, others, weight, norm_gain, slots),
        [pltpu.VMEM((MICRO, BLOCKS, ROWS, width), F32)],
        pl.CostEstimate(flops=flops, bytes_accessed=6 * 2**20, transcendentals=0),
    )
    other = from_other_core(direct16)
    aligned = y_exchange(aligned)
    other, aligned = lax.optimization_barrier((other, aligned))
    aligned = jnp.sum(aligned, axis=0)

    chip = call(half_body, jax.ShapeDtypeStruct(half, BF16), [SMEM, VMEM, VMEM], (place, direct, other))
    above = [from_chips_above(chip, d) for d in (1, 2, 3)]
    above_other = from_other_core(sum(part.astype(F32) for part in above).astype(BF16))

    own, others, _ = lax.optimization_barrier((own, others, above[0]))
    local = call(
        outer_body,
        jax.ShapeDtypeStruct((NX, width, width), BF16),
        [SMEM] + [VMEM] * 8,
        (place, *own, others, norm_gain, slots, squares),
        [pltpu.VMEM((MICRO, BLOCKS, ROWS, width), BF16), pltpu.VMEM((tokens, width), BF16)],
        pl.CostEstimate(flops=flops, bytes_accessed=6 * 2**20, transcendentals=0),
    )
    summed = lax.psum_scatter(local, "dp", scatter_dimension=0)
    weight_grads = (summed.astype(F32) / (MICRO * NX)).astype(BF16)[None]

    parts = z_exchange(jnp.broadcast_to(aligned, (NZ,) + aligned.shape))
    parts, raw_all = lax.optimization_barrier((parts, raw_all))
    scales = call(
        functools.partial(scale_body, model_width=model_width),
        jax.ShapeDtypeStruct((NS, NS, LANES), F32),
        [SMEM, VMEM, VMEM],
        (place, parts, squares),
    )
    scales = lax.all_to_all(scales, "section", 0, 0)

    by_micro = (MICRO, tokens // MICRO, width)
    at_rows = pl.BlockSpec((MICRO, LANES, width), lambda i: (0, i, 0))
    at_half = pl.BlockSpec((LANES, width), lambda i: (i, 0))
    input_grads = pl.pallas_call(
        total_body,
        grid=(tokens // MICRO // LANES,),
        out_shape=jax.ShapeDtypeStruct(by_micro, BF16),
        in_specs=[
            SMEM,
            pl.BlockSpec((NS, MICRO, LANES, width), lambda i: (0, 0, i, 0)),
            pl.BlockSpec((NS, NS, LANES), lambda i: (0, 0, 0)),
            at_rows,
            at_rows,
            at_half,
            at_half,
            at_half,
            at_half,
            at_rows,
        ],
        out_specs=at_rows,
        compiler_params=pltpu.CompilerParams(vmem_limit_bytes=14 * 2**20),
    )(
        place,
        raw_all,
        scales,
        direct.reshape(by_micro),
        other.reshape(by_micro),
        *above,
        above_other,
        top_grad,
    )
    return (input_grads[None], weight_grads)


def solution(mesh):
    in_specs = (
        P("section", None),
        P("section", None, "dp", "tensor"),
        P("section", "tensor"),
        P("section", "tensor", None),
        P("section", None, ("dp", "tensor"), None),
        P(None, "dp", "tensor"),
    )
    out_specs = (P("section", None, "dp", "tensor"), P("section", "tensor", "dp"))
    return jax.shard_map(shards, mesh=mesh, in_specs=in_specs, out_specs=out_specs, check_vma=False)
```

time: 183 us -> 169 us (0.923)
  starting transfers between devices: 95.1 us -> 46.1 us
  waiting for transfers between devices: 7.55 us -> 52 us
  local copies, waits for them, and re-layouts: 12.2 us -> 5.49 us
  other arithmetic: 6.37 us -> 2.04 us
    ppermute x3, waiting for transfers between devices: 0.01 us -> 31.4 us  [from_chips_above(): lax.ppermute(value, 'section', [(s, s - 2 * chips) for s in range(2 * chi...]
    ppermute x6 -> x0, starting transfers between devices: 31 us -> none  [the longest x3 21.6 us: from_z(): return lax.ppermute(value, 'tensor', perm)]
    all_to_all x1 -> x0, blocking collectives: 22.9 us -> none  [z_exchange(): return lax.all_to_all(spread, 'tensor', 0, 0, axis_index_groups=z_groups())]
    all_to_all x1 -> x2, blocking collectives: 8.64 us -> 31.3 us  [y_exchange(): return lax.all_to_all(spread, 'tensor', 0, 0, axis_index_groups=y_groups())]
    all_to_all x1 -> x2, waiting for transfers between devices: 0.01 us -> 11.4 us  [z_exchange(): return lax.all_to_all(spread, 'tensor', 0, 0, axis_index_groups=z_groups())]
    ppermute x6 -> x3, starting transfers between devices: 20.4 us -> 9.5 us  [from_y(): return lax.ppermute(value, 'tensor', perm)]
    all_to_all x1, starting transfers between devices: 11.9 us -> 4.98 us  [shards(): scales = lax.all_to_all(scales, 'section', 0, 0)]
    unnamed x36 -> x16, local copies, waits for them, and re-layouts: 10.3 us -> 4.16 us
  transfers between devices with their start and end apart: 21 -> 13, of which waited for: 4 -> 7; matrix products, arithmetic and copies ran while one was open for 4% -> 2% of each run, Pallas kernels for 6% -> 6%
where the time goes in v4:
time: 169 us; the launch traced here: 168 us
  waiting for transfers between devices  52 us (31%)
  starting transfers between devices  46.1 us (27%)
  blocking collectives  31.3 us (19%)
  between operations  15.6 us (9%)
  Pallas kernels  15.3 us (9%)
  local copies, waits for them, and re-layouts  5.49 us (3%)
  other arithmetic  2.04 us (1%)
    ppermute x3, waiting for transfers between devices, from_chips_above(): lax.ppermute(value, 'section', [(s, s - 2 * chips) for s in range(2 * chi...  31.4 us
    all_to_all x2, blocking collectives, y_exchange(): return lax.all_to_all(spread, 'tensor', 0, 0, axis_index_groups=y_groups())  31.3 us
    all_to_all x2, starting transfers between devices, z_exchange(): return lax.all_to_all(spread, 'tensor', 0, 0, axis_index_groups=z_groups())  20.6 us
    pallas_call x6, Pallas kernels, call(): pl.pallas_call(body, out_shape=out_shape, in_specs=specs, out_specs=jax.t...  11.6 us
    all_to_all x2, waiting for transfers between devices, z_exchange(): return lax.all_to_all(spread, 'tensor', 0, 0, axis_index_groups=z_groups())  11.4 us
    ppermute x3, starting transfers between devices, from_y(): return lax.ppermute(value, 'tensor', perm)  9.5 us
    ppermute x2, starting transfers between devices, from_other_core(): return lax.ppermute(value, 'section', [(s, s ^ 1) for s in range(NS)])  7 us
    ppermute x3, waiting for transfers between devices, from_y(): return lax.ppermute(value, 'tensor', perm)  6.1 us
  transfers between devices with their start and end apart: 13, of which 7 were waited for; matrix products, arithmetic and copies ran while one was open for 2% of the time, Pallas kernels for 6%

profile of v4, /device:TPU:1, one launch (start us, length us, event | category | flops | bytes accessed | tf_op | source)
XLA Modules:
  0.0 167.9 jit_solution(1587801450127605098)
XLA Ops:
  8.0 0.7 stack.19.place
  8.8 1.0 copy-done
  9.8 0.9 copy-done.4
  10.7 1.5 shard_map.77
  12.2 15.6 %all-to-all-start = ((bf16[4,32,2176]{2,1,0:T(8,128)(2,1)}), bf16[4,32,2176]{2,1,0:T(8,128)(2,1)S(1)}, u32[]{:S(2)}, u32[]{:S(2)}) async-start(bf16[4,32,2176]{2,1,0:T(8,128)(2,1)} %shard_map.77), calls=%async_computation | async-start | bytes 1114112 | tf_op jit(solution)/shard_map/all_to_all | solution.py:52
  27.9 0.0 all-gather.3.cloned.1.call-start
  27.9 4.6 %collective-permute-start = (bf16[32,2048]{1,0:T(8,128)(2,1)S(1)}, bf16[32,2048]{1,0:T(8,128)(2,1)S(1)}, u32[]{:S(2)}, u32[]{:S(2)}) collective-permute-start(bf16[32,2048]{1,0:T(8,128)(2,1)S(1)} %bitcast.22), channel_id=1, source_target_pairs={{16,0},{20,4},{24,8},{28,12},{32,16},{36,20},{40,24},{44,28},{48,3... | collective-permute-start | bytes 393224 | tf_op jit(solution)/shard_map/ppermute | solution.py:31
  32.5 2.3 %collective-permute-start.1 = (bf16[32,2048]{1,0:T(8,128)(2,1)S(1)}, bf16[32,2048]{1,0:T(8,128)(2,1)S(1)}, u32[]{:S(2)}, u32[]{:S(2)}) collective-permute-start(bf16[32,2048]{1,0:T(8,128)(2,1)S(1)} %bitcast.23), channel_id=1, source_target_pairs={{32,0},{36,4},{40,8},{44,12},{48,16},{52,20},{56,24},{60,28},{0,32... | collective-permute-start | bytes 393224 | tf_op jit(solution)/shard_map/ppermute | solution.py:31
  34.8 2.6 %collective-permute-start.2 = (bf16[32,2048]{1,0:T(8,128)(2,1)S(1)}, bf16[32,2048]{1,0:T(8,128)(2,1)S(1)}, u32[]{:S(2)}, u32[]{:S(2)}) collective-permute-start(bf16[32,2048]{1,0:T(8,128)(2,1)S(1)} %bitcast.24), channel_id=1, source_target_pairs={{48,0},{52,4},{56,8},{60,12},{0,16},{4,20},{8,24},{12,28},{16,32},... | collective-permute-start | bytes 393224 | tf_op jit(solution)/shard_map/ppermute | solution.py:31
  37.4 0.0 collective-permute-done.own1
  37.4 2.6 %collective-permute-done.1.own2 = bf16[32,2048]{1,0:T(8,128)(2,1)S(1)} collective-permute-done((bf16[32,2048]{1,0:T(8,128)(2,1)S(1)}, bf16[32,2048]{1,0:T(8,128)(2,1)S(1)}, u32[]{:S(2)}, u32[]{:S(2)}) %collective-permute-start.1) | collective-permute-done | bytes 131104 | tf_op jit(solution)/shard_map/ppermute | solution.py:31
  40.0 3.5 %collective-permute-done.2.own3 = bf16[32,2048]{1,0:T(8,128)(2,1)S(1)} collective-permute-done((bf16[32,2048]{1,0:T(8,128)(2,1)S(1)}, bf16[32,2048]{1,0:T(8,128)(2,1)S(1)}, u32[]{:S(2)}, u32[]{:S(2)}) %collective-permute-start.2) | collective-permute-done | bytes 131104 | tf_op jit(solution)/shard_map/ppermute | solution.py:31
  43.5 11.4 %all-to-all-done.kv_ref = bf16[4,32,2176]{2,1,0:T(8,128)(2,1)S(1)} async-done(((bf16[4,32,2176]{2,1,0:T(8,128)(2,1)}), bf16[4,32,2176]{2,1,0:T(8,128)(2,1)S(1)}, u32[]{:S(2)}, u32[]{:S(2)}) %all-to-all-start) | async-done | bytes 557088 | tf_op jit(solution)/shard_map/all_to_all | solution.py:52
  54.9 0.0 all-gather.3.cloned.1.call-update
  55.0 0.0 reduce-scatter.2.cloned.1.call-start
  55.0 0.7 shard_map.78
  55.7 0.0 copy-start.1
  55.7 0.0 copy-start.3
  55.7 0.0 copy-start.7
  55.7 24.6 %all_to_all.25.others = bf16[4,96,2176]{2,1,0:T(8,128)(2,1)S(1)} all-to-all(bf16[4,96,2176]{2,1,0:T(8,128)(2,1)S(1)} %shard_map.78), channel_id=1, replica_groups={{0,16,32,48},{4,20,36,52},{8,24,40,56},{12,28,44,60},{1,17,33,49},{5,21..., dimensions={0} | all-to-all | bytes 3342336 | tf_op jit(solution)/shard_map/all_to_all | solution.py:48
  80.3 4.2 %shard_map.79 = (f32[512,512]{1,0:T(8,128)S(1)}, bf16[512,512]{1,0:T(8,128)(2,1)S(1)}, f32[4,4,128]{2,1,0:T(4,128)S(1)}, f32[4,128]{1,0:T(4,128)S(1)}) custom-call(s32[5]{0:T(128)S(1)} %stack.19.place, bf16[32,2048]{1,0:T(8,128)(2,1)S(1)} %bitcast.25, bf16[32,2048]{1,0:T(8,128)(2,1)S(1)} %collective-permute-done.own1, ...), custom_call_target="tpu_custom_call" | custom-call | flops 1073741824 | bytes 6291456 | tf_op jit(solution)/shard_map/pallas_call | solution.py:56
  84.5 4.2 %collective-permute-start.3 = (bf16[512,512]{1,0:T(8,128)(2,1)S(1)}, bf16[512,512]{1,0:T(8,128)(2,1)S(1)}, u32[]{:S(2)}, u32[]{:S(2)}) collective-permute-start(bf16[512,512]{1,0:T(8,128)(2,1)S(1)} %get-tuple-element.30), channel_id=1, source_target_pairs={{0,64},{64,0},{128,192},{192,128},{256,320},{320,256},{384,448},{4... | collective-permute-start | bytes 1572872 | tf_op jit(solution)/shard_map/ppermute | solution.py:40
  88.6 6.8 %all_to_all.26 = f32[4,4,128]{2,1,0:T(4,128)S(1)} all-to-all(f32[4,4,128]{2,1,0:T(4,128)S(1)} %get-tuple-element.31), channel_id=1, replica_groups={{0,16,32,48},{4,20,36,52},{8,24,40,56},{12,28,44,60},{1,17,33,49},{5,21..., dimensions={0} | all-to-all | bytes 16384 | tf_op jit(solution)/shard_map/all_to_all | solution.py:48
  95.4 0.0 collective-permute-done.3.other
  95.4 0.6 shard_map.81
  96.0 1.3 collective-permute-start.4
  97.3 17.5 %collective-permute-done.4.above1 = bf16[256,512]{1,0:T(8,128)(2,1)S(1)} collective-permute-done((bf16[256,512]{1,0:T(8,128)(2,1)S(1)}, bf16[256,512]{1,0:T(8,128)(2,1)S(1)}, u32[]{:S(2)}, u32[]{:S(2)}) %collective-permute-start.4) | collective-permute-done | bytes 262176 | tf_op jit(solution)/shard_map/ppermute | solution.py:44
  114.8 3.4 %shard_map.83 = bf16[4,512,512]{2,1,0:T(8,128)(2,1)} custom-call(s32[5]{0:T(128)S(1)} %stack.19.place, bf16[32,2048]{1,0:T(8,128)(2,1)S(1)} %bitcast.26, bf16[32,2048]{1,0:T(8,128)(2,1)S(1)} %collective-permute-done.own1, bf16[32,2048]{1,0:T(8,128)(2,1)S(1)} %collective-permute-done.1.own2, bf16[32,2048]{1,0:T(8,128)(2,1)S(1)} %collective-permute-done.2.own3, ...), custom_call_target="tpu_custom_call" | custom-call | flops 1073741824 | bytes 6291456 | tf_op jit(solution)/shard_map/pallas_call | solution.py:56
  118.2 0.0 reduce-scatter.2.cloned.1.call-update
  118.2 1.4 collective-permute-start.5
  119.7 1.3 collective-permute-start.6
  121.0 0.6 broadcast_in_dim.7
  121.6 5.0 %all-to-all-start.3 = ((f32[4,4,128]{2,1,0:T(4,128)}), f32[4,4,128]{2,1,0:T(4,128)S(1)}, u32[]{:S(2)}, u32[]{:S(2)}) async-start(f32[4,4,128]{2,1,0:T(4,128)} %broadcast_in_dim.7), calls=%async_computation.3 | async-start | bytes 16384 | tf_op jit(solution)/shard_map/all_to_all | solution.py:52
  126.5 13.9 %collective-permute-done.5.above2 = bf16[256,512]{1,0:T(8,128)(2,1)S(1)} collective-permute-done((bf16[256,512]{1,0:T(8,128)(2,1)S(1)}, bf16[256,512]{1,0:T(8,128)(2,1)S(1)}, u32[]{:S(2)}, u32[]{:S(2)}) %collective-permute-start.5) | collective-permute-done | bytes 262176 | tf_op jit(solution)/shard_map/ppermute | solution.py:44
  140.5 0.0 collective-permute-done.6.above3
  140.5 0.1 add_convert_fusion
  140.6 2.8 %collective-permute-start.7 = (bf16[256,512]{1,0:T(8,128)(2,1)S(1)}, bf16[256,512]{1,0:T(8,128)(2,1)S(1)}, u32[]{:S(2)}, u32[]{:S(2)}) collective-permute-start(bf16[256,512]{1,0:T(8,128)(2,1)S(1)} %add_convert_fusion), channel_id=1, source_target_pairs={{0,64},{64,0},{128,192},{192,128},{256,320},{320,256},{384,448},{4... | collective-permute-start | bytes 786440 | tf_op jit(solution)/shard_map/ppermute | solution.py:40
  143.4 0.0 all-to-all-done.3.parts
  143.4 0.0 all-gather.3.cloned.1.call-done
  143.5 1.2 shard_map.80
  144.6 5.0 %all-to-all-start.4 = ((f32[8,8,128]{2,1,0:T(8,128)}), f32[8,8,128]{2,1,0:T(8,128)S(1)}, u32[]{:S(2)}, u32[]{:S(2)}) async-start(f32[8,8,128]{2,1,0:T(8,128)} %shard_map.80), calls=%async_computation.4 | async-start | bytes 65536 | tf_op jit(solution)/shard_map/all_to_all | solution.py:286
  149.6 2.2 %reduce-scatter.2.cloned.1.call-done = bf16[1,512,512]{2,1,0:T(8,128)(2,1)} async-done(((bf16[4,512,512]{2,1,0:T(8,128)(2,1)}), bf16[1,512,512]{2,1,0:T(8,128)(2,1)}) %reduce-scatter.2.cloned.1.call-update) | async-done | bytes 524304 | tf_op jit(solution)/shard_map/reduce_scatter | solution.py:275
  151.8 1.9 %multiply_convert_fusion = bf16[1,512,512]{2,1,0:T(8,128)(2,1)} fusion(bf16[1,512,512]{2,1,0:T(8,128)(2,1)} %reduce-scatter.2.cloned.1.call-done), kind=kLoop, calls=%fused_computation | loop fusion | flops 786432 | bytes 1048576 | tf_op jit(solution)/shard_map/convert_element_type | solution.py:276
  153.8 0.0 collective-permute-done.7.above_other
  153.8 0.8 all-to-all-done.4.scales
  154.6 0.0 copy-done.6
  154.6 2.2 %copy-done.2 = bf16[16,256,512]{2,1,0:T(8,128)(2,1)S(1)} copy-done((bf16[16,256,512]{2,1,0:T(8,128)(2,1)S(1)}, bf16[16,256,512]{2,1,0:T(8,128)(2,1)}, u32[]{:S(2)}) %copy-start.2) | copy-done | bytes 4194328
  156.8 3.7 %shard_map.82 = bf16[2,256,512]{2,1,0:T(8,128)(2,1)} custom-call(s32[5]{0:T(128)S(1)} %stack.19.place, bf16[8,2,256,512]{3,2,1,0:T(8,128)(2,1)S(1)} %bitcast.18, f32[8,8,128]{2,1,0:T(8,128)S(1)} %all-to-all-done.4.scales, f32[2,256,512]{2,1,0:T(8,128)S(1)} %bitcast.17, bf16[2,256,512]{2,1,0:T(8,128)(2,1)S(1)} %bitcast.20, ...), custom_call_target="tpu_custom_call" | custom-call | tf_op jit(solution)/shard_map/pallas_call | solution.py:291
  (10 shorter events, 0.0 us)
Async XLA Ops:
  8.8 1.0 copy-start
  9.8 0.9 copy-start.4
  10.7 17.2 %copy-start.5 = (bf16[1,2,16,2048]{3,2,1,0:T(8,128)(2,1)S(1)}, bf16[1,2,16,2048]{3,2,1,0:T(8,128)(2,1)}, u32[]{:S(2)}) copy-start(bf16[1,2,16,2048]{3,2,1,0:T(8,128)(2,1)} %param.10) | copy-start | bytes 393220
  12.2 42.7 %all-to-all-start = ((bf16[4,32,2176]{2,1,0:T(8,128)(2,1)}), bf16[4,32,2176]{2,1,0:T(8,128)(2,1)S(1)}, u32[]{:S(2)}, u32[]{:S(2)}) async-start(bf16[4,32,2176]{2,1,0:T(8,128)(2,1)} %shard_map.77), calls=%async_computation | async-start | bytes 1114112 | tf_op jit(solution)/shard_map/all_to_all | solution.py:52
  27.9 115.6 %all-gather.3.cloned.1.call-start = ((), (), s32[]{:S(2)}) async-start(), calls=%async_computation.7 | async-start | bytes 4718592 | tf_op jit(solution)/shard_map/all_gather | solution.py:239
  27.9 9.5 %collective-permute-start = (bf16[32,2048]{1,0:T(8,128)(2,1)S(1)}, bf16[32,2048]{1,0:T(8,128)(2,1)S(1)}, u32[]{:S(2)}, u32[]{:S(2)}) collective-permute-start(bf16[32,2048]{1,0:T(8,128)(2,1)S(1)} %bitcast.22), channel_id=1, source_target_pairs={{16,0},{20,4},{24,8},{28,12},{32,16},{36,20},{40,24},{44,28},{48,3... | collective-permute-start | bytes 393224 | tf_op jit(solution)/shard_map/ppermute | solution.py:31
  32.5 7.5 %collective-permute-start.1 = (bf16[32,2048]{1,0:T(8,128)(2,1)S(1)}, bf16[32,2048]{1,0:T(8,128)(2,1)S(1)}, u32[]{:S(2)}, u32[]{:S(2)}) collective-permute-start(bf16[32,2048]{1,0:T(8,128)(2,1)S(1)} %bitcast.23), channel_id=1, source_target_pairs={{32,0},{36,4},{40,8},{44,12},{48,16},{52,20},{56,24},{60,28},{0,32... | collective-permute-start | bytes 393224 | tf_op jit(solution)/shard_map/ppermute | solution.py:31
  34.8 8.7 %collective-permute-start.2 = (bf16[32,2048]{1,0:T(8,128)(2,1)S(1)}, bf16[32,2048]{1,0:T(8,128)(2,1)S(1)}, u32[]{:S(2)}, u32[]{:S(2)}) collective-permute-start(bf16[32,2048]{1,0:T(8,128)(2,1)S(1)} %bitcast.24), channel_id=1, source_target_pairs={{48,0},{52,4},{56,8},{60,12},{0,16},{4,20},{8,24},{12,28},{16,32},... | collective-permute-start | bytes 393224 | tf_op jit(solution)/shard_map/ppermute | solution.py:31
  55.0 96.9 %reduce-scatter.2.cloned.1.call-start = ((), (), s32[]{:S(2)}) async-start(), calls=%async_computation.6 | async-start | bytes 2621440 | tf_op jit(solution)/shard_map/reduce_scatter | solution.py:275
  55.7 24.6 %copy-start.1 = (bf16[1,2,256,512]{3,2,1,0:T(8,128)(2,1)S(1)}, bf16[1,2,256,512]{3,2,1,0:T(8,128)(2,1)}, u32[]{:S(2)}) copy-start(bf16[1,2,256,512]{3,2,1,0:T(8,128)(2,1)} %param.7) | copy-start | bytes 1572868
  55.7 24.6 %copy-start.3 = (bf16[1,512,2048]{2,1,0:T(8,128)(2,1)S(1)}, bf16[1,512,2048]{2,1,0:T(8,128)(2,1)}, u32[]{:S(2)}) copy-start(bf16[1,512,2048]{2,1,0:T(8,128)(2,1)} %param.9) | copy-start | bytes 6291460
  55.7 24.6 %copy-start.7 = (bf16[1,512]{1,0:T(2,128)(2,1)S(1)}, bf16[1,512]{1,0:T(2,128)(2,1)}, u32[]{:S(2)}) copy-start(bf16[1,512]{1,0:T(2,128)(2,1)} %gains.3) | copy-start | bytes 3076
  84.5 10.9 %collective-permute-start.3 = (bf16[512,512]{1,0:T(8,128)(2,1)S(1)}, bf16[512,512]{1,0:T(8,128)(2,1)S(1)}, u32[]{:S(2)}, u32[]{:S(2)}) collective-permute-start(bf16[512,512]{1,0:T(8,128)(2,1)S(1)} %get-tuple-element.30), channel_id=1, source_target_pairs={{0,64},{64,0},{128,192},{192,128},{256,320},{320,256},{384,448},{4... | collective-permute-start | bytes 1572872 | tf_op jit(solution)/shard_map/ppermute | solution.py:40
  96.0 18.8 %collective-permute-start.4 = (bf16[256,512]{1,0:T(8,128)(2,1)S(1)}, bf16[256,512]{1,0:T(8,128)(2,1)S(1)}, u32[]{:S(2)}, u32[]{:S(2)}) collective-permute-start(bf16[256,512]{1,0:T(8,128)(2,1)S(1)} %shard_map.81), channel_id=1, source_target_pairs={{128,0},{192,64},{256,128},{320,192},{384,256},{448,320},{129,1},{... | collective-permute-start | bytes 786440 | tf_op jit(solution)/shard_map/ppermute | solution.py:44
  118.2 36.4 %copy-start.6 = (bf16[2,256,512]{2,1,0:T(8,128)(2,1)S(1)}, bf16[2,256,512]{2,1,0:T(8,128)(2,1)}, u32[]{:S(2)}) copy-start(bf16[2,256,512]{2,1,0:T(8,128)(2,1)} %top.1) | copy-start | bytes 1572868
  118.2 22.2 %collective-permute-start.5 = (bf16[256,512]{1,0:T(8,128)(2,1)S(1)}, bf16[256,512]{1,0:T(8,128)(2,1)S(1)}, u32[]{:S(2)}, u32[]{:S(2)}) collective-permute-start(bf16[256,512]{1,0:T(8,128)(2,1)S(1)} %shard_map.81), channel_id=1, source_target_pairs={{256,0},{320,64},{384,128},{448,192},{257,1},{321,65},{385,129},{4... | collective-permute-start | bytes 786440 | tf_op jit(solution)/shard_map/ppermute | solution.py:44
  119.7 20.8 %collective-permute-start.6 = (bf16[256,512]{1,0:T(8,128)(2,1)S(1)}, bf16[256,512]{1,0:T(8,128)(2,1)S(1)}, u32[]{:S(2)}, u32[]{:S(2)}) collective-permute-start(bf16[256,512]{1,0:T(8,128)(2,1)S(1)} %shard_map.81), channel_id=1, source_target_pairs={{384,0},{448,64},{385,1},{449,65},{386,2},{450,66},{387,3},{451,67... | collective-permute-start | bytes 786440 | tf_op jit(solution)/shard_map/ppermute | solution.py:44
  121.6 21.8 %all-to-all-start.3 = ((f32[4,4,128]{2,1,0:T(4,128)}), f32[4,4,128]{2,1,0:T(4,128)S(1)}, u32[]{:S(2)}, u32[]{:S(2)}) async-start(f32[4,4,128]{2,1,0:T(4,128)} %broadcast_in_dim.7), calls=%async_computation.3 | async-start | bytes 16384 | tf_op jit(solution)/shard_map/all_to_all | solution.py:52
  140.6 13.2 %collective-permute-start.7 = (bf16[256,512]{1,0:T(8,128)(2,1)S(1)}, bf16[256,512]{1,0:T(8,128)(2,1)S(1)}, u32[]{:S(2)}, u32[]{:S(2)}) collective-permute-start(bf16[256,512]{1,0:T(8,128)(2,1)S(1)} %add_convert_fusion), channel_id=1, source_target_pairs={{0,64},{64,0},{128,192},{192,128},{256,320},{320,256},{384,448},{4... | collective-permute-start | bytes 786440 | tf_op jit(solution)/shard_map/ppermute | solution.py:40
  144.6 10.0 %all-to-all-start.4 = ((f32[8,8,128]{2,1,0:T(8,128)}), f32[8,8,128]{2,1,0:T(8,128)S(1)}, u32[]{:S(2)}, u32[]{:S(2)}) async-start(f32[8,8,128]{2,1,0:T(8,128)} %shard_map.80), calls=%async_computation.4 | async-start | bytes 65536 | tf_op jit(solution)/shard_map/all_to_all | solution.py:286
  154.6 2.2 %copy-start.2 = (bf16[16,256,512]{2,1,0:T(8,128)(2,1)S(1)}, bf16[16,256,512]{2,1,0:T(8,128)(2,1)}, u32[]{:S(2)}) copy-start(bf16[16,256,512]{2,1,0:T(8,128)(2,1)} %all-gather.3.cloned.1.call-done) | copy-start | bytes 12582916
Sparse Core Ops, SparseCore 0:
  55.1 62.5 all-gather.2
Sparse Core Ops, SparseCore 1:
  118.3 33.5 reduce-scatter.1

commit v5 on v4

--- a/solution.py
+++ b/solution.py
@@ -52,14 +52,14 @@
     return lax.all_to_all(spread, "tensor", 0, 0, axis_index_groups=z_groups())
 
 
-def call(body, out_shape, specs, args, scratch=(), cost=None):
+def call(body, out_shape, specs, args, scratch=(), cost=None, limit=14):
     return pl.pallas_call(
         body,
         out_shape=out_shape,
         in_specs=specs,
         out_specs=jax.tree.map(lambda _: VMEM, out_shape),
         scratch_shapes=list(scratch),
-        compiler_params=pltpu.CompilerParams(vmem_limit_bytes=14 * 2**20),
+        compiler_params=pltpu.CompilerParams(vmem_limit_bytes=limit * 2**20),
         cost_estimate=cost,
     )(*args)
 
@@ -88,9 +88,9 @@
     return jnp.sum(jnp.transpose(folded), axis=0, keepdims=True)
 
 
-def pack_body(place, kv_ref, stashed, out_ref):
+def pack_body(plan, kv_ref, stashed, out_ref):
     kvw = kv_ref.shape[1]
-    swap = place[2]
+    swap = plan[0, 0]
     sums = []
     for chunk in range(LINES):
         m, at = chunk * LANES // HALF, chunk * LANES % HALF
@@ -113,8 +113,8 @@
             out_ref[y, rows, kvw:] = squares
 
 
-def back_body(place, own0, own1, own2, own3, others, weight, gains, stashed, direct, direct16, aligned, squares, grad):
-    tz, ty, swap = place[0], place[1], place[2]
+def back_body(place, own0, own1, own2, own3, others, weight, gains, saved, direct, direct16, aligned, squares, grad):
+    tz, ty = place[0], place[1]
     kvw = weight.shape[1]
     width = weight.shape[0]
     model_width = width * BLOCKS
@@ -138,7 +138,7 @@
     for chunk in range(MICRO * BLOCKS // per):
         m, first = chunk * per // BLOCKS, chunk * per % BLOCKS
         gained = grad[m, first : first + per].reshape(LANES, width) * gain
-        hidden = stashed[m ^ swap, first * ROWS : (first + per) * ROWS].astype(F32)
+        hidden = saved[m, first * ROWS : (first + per) * ROWS].astype(F32)
         inverse = 1.0 / jnp.sqrt(squares[chunk : chunk + 1] / model_width + EPSILON)
         here = gained * columns(inverse, width)
         direct[chunk * LANES : (chunk + 1) * LANES] = here
@@ -150,19 +150,19 @@
 
 def half_body(place, direct, other, out_ref):
     rows = out_ref.shape[0]
-    at = pl.ds(pl.multiple_of(place[3] * rows, rows), rows)
+    at = pl.ds(pl.multiple_of(place[2] * rows, rows), rows)
     out_ref[...] = (direct[at] + other[at].astype(F32)).astype(BF16)
 
 
-def outer_body(place, own0, own1, own2, own3, others, gains, stashed, squares, out_ref, normed, left):
-    tz, ty, swap = place[0], place[1], place[2]
+def outer_body(place, own0, own1, own2, own3, others, gains, saved, squares, out_ref, normed, left):
+    tz, ty = place[0], place[1]
     width = out_ref.shape[1]
     model_width = width * BLOCKS
     gain = gains[...].astype(F32)
     per = LANES // ROWS
     for chunk in range(MICRO * BLOCKS // per):
         m, first = chunk * per // BLOCKS, chunk * per % BLOCKS
-        hidden = stashed[m ^ swap, first * ROWS : (first + per) * ROWS].astype(F32)
+        hidden = saved[m, first * ROWS : (first + per) * ROWS].astype(F32)
         inverse = 1.0 / jnp.sqrt(squares[chunk : chunk + 1] / model_width + EPSILON)
         here = gain * hidden * columns(inverse, width)
         normed[m, first : first + per] = here.astype(BF16).reshape(per, ROWS, width)
@@ -177,41 +177,41 @@
         at = slice(x * width, (x + 1) * width)
         mine = [ref[:, at] for ref in (own0, own1, own2, own3)]
         right = jnp.concatenate(mine + [others[y, :, at] for y in range(NY)])
-        out_ref[x] = jnp.dot(turned, right, preferred_element_type=F32).astype(out_ref.dtype)
-
-
-def scale_body(place, parts, squares, out_ref, *, model_width):
+        product = jnp.dot(turned, right, preferred_element_type=F32)
+        out_ref[x] = (product / (MICRO * NX)).astype(BF16)
+
+
+def scale_body(parts, squares, out_ref, *, model_width):
     mean = squares[...] / model_width + EPSILON
     total = parts[0] + parts[1] + parts[2] + parts[3]
     scale = total / (model_width * (mean * jnp.sqrt(mean)))
-    swap = jnp.full((NS - LINES, LANES), place[2], jnp.int32).astype(F32)
-    value = jnp.concatenate([scale, swap])
     for section in range(NS):
-        out_ref[section] = value
-
-
-def total_body(place, raw, scales, direct, other, above1, above2, above3, above_other, top, out_ref):
-    section, core = place[4], place[3]
-    rows, width = raw.shape[2], raw.shape[3]
-    chunk = pl.program_id(0)
+        out_ref[section] = scale
+
+
+def total_body(place, saved, scales, direct, other, above1, above2, above3, above_other, top, out_ref, held, sems):
+    copies = [pltpu.make_async_copy(saved.at[u], held.at[u], sems.at[u]) for u in range(NS)]
+    for copy in copies:
+        copy.start()
+    section, core = place[3], place[2]
     use_other = jnp.where(core == 0, 1.0, 0.0)
-    fixes = [jnp.zeros((rows, width), F32) for _ in range(MICRO)]
-    turned = []
+    live = lax.broadcasted_iota(jnp.int32, (LANES, NS), 1) >= section
+    for copy in copies:
+        copy.wait()
+    step = 2 * ROWS
     for m in range(MICRO):
-        row = m * (BLOCKS * ROWS // LANES) + chunk
-        turned.append(jnp.transpose(scales[:, pl.ds(row, 1)].reshape(NS, LANES)))
-    for u in range(NS):
-        live = jnp.where(u >= section, 1.0, 0.0)
-        swapped = scales[u, NS - 1 : NS, :1] != 0.0
-        slots = [raw[u, k].astype(F32) for k in range(MICRO)]
-        for m in range(MICRO):
-            hidden = jnp.where(swapped, slots[1 - m], slots[m])
-            fixes[m] = fixes[m] + hidden * (turned[m][:, u : u + 1] * live)
-    above = above1[...].astype(F32) + above2[...].astype(F32) + above3[...].astype(F32)
-    for m in range(MICRO):
-        mine = jnp.where(core == m, above, above_other[...].astype(F32))
-        value = top[m].astype(F32) + direct[m] + use_other * other[m].astype(F32) + mine - fixes[m]
-        out_ref[m] = value.astype(BF16)
+        for first in range(0, HALF, LANES):
+            scale = scales[:, (m * HALF + first) // LANES].reshape(NS, LANES)
+            scale = jnp.where(live, jnp.transpose(scale), 0.0)
+            for row in range(0, LANES, step):
+                at = slice(first + row, first + row + step)
+                above = above1[at].astype(F32) + above2[at].astype(F32) + above3[at].astype(F32)
+                above = jnp.where(core == m, above, above_other[at].astype(F32))
+                value = top[m, at].astype(F32) + direct[m, at] + above
+                value = value + use_other * other[m, at].astype(F32)
+                for u in range(NS):
+                    value = value - held[u, m, at].astype(F32) * scale[row : row + step, u : u + 1]
+                out_ref[m, at] = value.astype(BF16)
 
 
 def shards(plan, stashed, norm_gain, kv_weight, kv_grad, top_grad):
@@ -223,20 +223,21 @@
     tokens = MICRO * BLOCKS * ROWS
     model_width = width * BLOCKS
     lines = tokens // LANES
-    place = jnp.stack([tz, ty, plan[0, 0], core, section]).astype(jnp.int32)
+    place = jnp.stack([tz, ty, core, section]).astype(jnp.int32)
     slots, weight = stashed[0], kv_weight[0]
     kvw = weight.shape[-1]
     kv0 = kv_grad.reshape(SHARE, kvw)
     half = (tokens // 2, width)
 
     shape = jax.ShapeDtypeStruct((NZ, SHARE, kvw + LANES), BF16)
-    packed = call(pack_body, shape, [SMEM, VMEM, VMEM], (place, kv0, slots))
-    packed, kv_y = lax.optimization_barrier((packed, kv0))
+    packed = call(pack_body, shape, [SMEM, VMEM, VMEM], (plan, kv0, slots))
+    packed, kv_y, slots = lax.optimization_barrier((packed, kv0, slots))
     kv_z = z_exchange(packed)
     own = [kv_y] + [from_y(kv_y, d) for d in (1, 2, 3)]
-    kv_z, own, slots_later = lax.optimization_barrier((kv_z, own, slots))
-
-    raw_all = lax.all_gather(slots_later, "section")
+    hidden = jnp.where(plan[0, 0] == 0, slots, slots[::-1])
+    kv_z, own, hidden = lax.optimization_barrier((kv_z, own, hidden))
+
+    hidden_all = lax.all_gather(hidden, "section")
     shape = jax.ShapeDtypeStruct((NY, (NZ - 1) * SHARE, kvw + LANES), BF16)
     others = y_exchange(call(spread_body, shape, [SMEM, VMEM], (place, kv_z)))
 
@@ -250,7 +251,7 @@
             jax.ShapeDtypeStruct((lines, LANES), F32),
         ),
         [SMEM] + [VMEM] * 8,
-        (place, *own, others, weight, norm_gain, slots),
+        (place, *own, others, weight, norm_gain, hidden),
         [pltpu.VMEM((MICRO, BLOCKS, ROWS, width), F32)],
         pl.CostEstimate(flops=flops, bytes_accessed=6 * 2**20, transcendentals=0),
     )
@@ -261,60 +262,45 @@
 
     chip = call(half_body, jax.ShapeDtypeStruct(half, BF16), [SMEM, VMEM, VMEM], (place, direct, other))
     above = [from_chips_above(chip, d) for d in (1, 2, 3)]
+    parts = z_exchange(jnp.broadcast_to(aligned, (NZ,) + aligned.shape))
+    above, parts, hidden_all = lax.optimization_barrier((above, parts, hidden_all))
     above_other = from_other_core(sum(part.astype(F32) for part in above).astype(BF16))
 
-    own, others, _ = lax.optimization_barrier((own, others, above[0]))
+    own, others, _ = lax.optimization_barrier((own, others, other))
     local = call(
         outer_body,
         jax.ShapeDtypeStruct((NX, width, width), BF16),
         [SMEM] + [VMEM] * 8,
-        (place, *own, others, norm_gain, slots, squares),
+        (place, *own, others, norm_gain, hidden, squares),
         [pltpu.VMEM((MICRO, BLOCKS, ROWS, width), BF16), pltpu.VMEM((tokens, width), BF16)],
         pl.CostEstimate(flops=flops, bytes_accessed=6 * 2**20, transcendentals=0),
     )
-    summed = lax.psum_scatter(local, "dp", scatter_dimension=0)
-    weight_grads = (summed.astype(F32) / (MICRO * NX)).astype(BF16)[None]
-
-    parts = z_exchange(jnp.broadcast_to(aligned, (NZ,) + aligned.shape))
-    parts, raw_all = lax.optimization_barrier((parts, raw_all))
+    weight_grads = lax.psum_scatter(local, "dp", scatter_dimension=0)[None]
+
     scales = call(
         functools.partial(scale_body, model_width=model_width),
-        jax.ShapeDtypeStruct((NS, NS, LANES), F32),
-        [SMEM, VMEM, VMEM],
-        (place, parts, squares),
+        jax.ShapeDtypeStruct((NS, lines, LANES), F32),
+        [VMEM, VMEM],
+        (parts, squares),
     )
     scales = lax.all_to_all(scales, "section", 0, 0)
-
     by_micro = (MICRO, tokens // MICRO, width)
-    at_rows = pl.BlockSpec((MICRO, LANES, width), lambda i: (0, i, 0))
-    at_half = pl.BlockSpec((LANES, width), lambda i: (i, 0))
-    input_grads = pl.pallas_call(
+    input_grads = call(
         total_body,
-        grid=(tokens // MICRO // LANES,),
-        out_shape=jax.ShapeDtypeStruct(by_micro, BF16),
-        in_specs=[
-            SMEM,
-            pl.BlockSpec((NS, MICRO, LANES, width), lambda i: (0, 0, i, 0)),
-            pl.BlockSpec((NS, NS, LANES), lambda i: (0, 0, 0)),
-            at_rows,
-            at_rows,
-            at_half,
-            at_half,
-            at_half,
-            at_half,
-            at_rows,
-        ],
-        out_specs=at_rows,
-        compiler_params=pltpu.CompilerParams(vmem_limit_bytes=14 * 2**20),
-    )(
-        place,
-        raw_all,
-        scales,
-        direct.reshape(by_micro),
-        other.reshape(by_micro),
-        *above,
-        above_other,
-        top_grad,
+        jax.ShapeDtypeStruct(by_micro, BF16),
+        [SMEM, pl.BlockSpec(memory_space=pltpu.HBM)] + [VMEM] * 8,
+        (
+            place,
+            hidden_all,
+            scales,
+            direct.reshape(by_micro),
+            other.reshape(by_micro),
+            *above,
+            above_other,
+            top_grad,
+        ),
+        [pltpu.VMEM((NS,) + by_micro, BF16), pltpu.SemaphoreType.DMA((NS,))],
+        limit=48,
     )
     return (input_grads[None], weight_grads)
 

time: 169 us -> 164 us (0.970)
  blocking collectives: 31.3 us -> 61 us
  waiting for transfers between devices: 52 us -> 31.4 us
  starting transfers between devices: 46.1 us -> 36.1 us
  local copies, waits for them, and re-layouts: 5.49 us -> 2.64 us
    all_to_all x0 -> x2, blocking collectives: none -> 29.7 us  [the longest x1 17.8 us: z_exchange(): return lax.all_to_all(spread, 'tensor', 0, 0, axis_index_groups=z_groups())]
    ppermute x3, waiting for transfers between devices: 31.4 us -> 14.8 us  [from_chips_above(): lax.ppermute(value, 'section', [(s, s - 2 * chips) for s in range(2 * chi...]
    all_to_all x1 -> x0, starting transfers between devices: 4.98 us -> none  [shards(): scales = lax.all_to_all(scales, 'section', 0, 0)]
    all_to_all x2 -> x1, starting transfers between devices: 20.6 us -> 15.6 us  [z_exchange(): return lax.all_to_all(spread, 'tensor', 0, 0, axis_index_groups=z_groups())]
    pallas_call x6 -> x7, Pallas kernels: 11.6 us -> 15.4 us  [call(): pl.pallas_call(body, out_shape=out_shape, in_specs=specs, out_specs=jax.t...]
    pallas_call x1 -> x0, Pallas kernels: 3.71 us -> none  [shards(): pl.pallas_call(total_body, grid=(tokens // MICRO // LANES,), out_shape=ja...]
    reduce_scatter x1, waiting for transfers between devices: 2.22 us -> 0.03 us  [shards(): weight_grads = lax.psum_scatter(local, 'dp', scatter_dimension=0)[None]]
    convert_element_type x1 -> x0, other arithmetic: 1.92 us -> none  [shards(): weight_grads = (summed.astype(F32) / (MICRO * NX)).astype(BF16)[None]]
  transfers between devices with their start and end apart: 13 -> 11, of which waited for: 7 -> 4; matrix products, arithmetic and copies ran while one was open for 2% -> 1% of each run, Pallas kernels for 6% -> 9%
where the time goes in v5:
time: 164 us; the launch traced here: 163 us
  blocking collectives  61 us (37%)
  starting transfers between devices  36.1 us (22%)
  waiting for transfers between devices  31.4 us (19%)
  between operations  15.7 us (10%)
  Pallas kernels  15.4 us (9%)
  local copies, waits for them, and re-layouts  2.64 us (2%)
    all_to_all x2, blocking collectives, y_exchange(): return lax.all_to_all(spread, 'tensor', 0, 0, axis_index_groups=y_groups())  31.3 us
    all_to_all x1, blocking collectives, z_exchange(): return lax.all_to_all(spread, 'tensor', 0, 0, axis_index_groups=z_groups())  17.8 us
    all_to_all x1, starting transfers between devices, z_exchange(): return lax.all_to_all(spread, 'tensor', 0, 0, axis_index_groups=z_groups())  15.6 us
    pallas_call x7, Pallas kernels, call(): pl.pallas_call(body, out_shape=out_shape, in_specs=specs, out_specs=jax.t...  15.4 us
    ppermute x3, waiting for transfers between devices, from_chips_above(): lax.ppermute(value, 'section', [(s, s - 2 * chips) for s in range(2 * chi...  14.8 us
    all_to_all x1, blocking collectives, shards(): scales = lax.all_to_all(scales, 'section', 0, 0)  11.9 us
    all_to_all x1, waiting for transfers between devices, z_exchange(): return lax.all_to_all(spread, 'tensor', 0, 0, axis_index_groups=z_groups())  11.4 us
    ppermute x3, starting transfers between devices, from_y(): return lax.ppermute(value, 'tensor', perm)  9.5 us
  transfers between devices with their start and end apart: 11, of which 4 were waited for; matrix products, arithmetic and copies ran while one was open for 1% of the time, Pallas kernels for 9%

profile of v5, /device:TPU:1, one launch (start us, length us, event | category | flops | bytes accessed | tf_op | source)
XLA Modules:
  0.0 163.4 jit_solution(17470580249534796161)
XLA Ops:
  8.0 0.0 copy-start.9
  8.0 0.0 copy-start.2
  8.0 1.0 copy-done.2
  9.1 0.9 copy-done.4
  10.0 0.7 copy-done.8
  10.6 1.5 shard_map.77
  12.2 15.6 %all-to-all-start = ((bf16[4,32,2176]{2,1,0:T(8,128)(2,1)}), bf16[4,32,2176]{2,1,0:T(8,128)(2,1)S(1)}, u32[]{:S(2)}, u32[]{:S(2)}) async-start(bf16[4,32,2176]{2,1,0:T(8,128)(2,1)} %shard_map.77), calls=%async_computation | async-start | bytes 1114112 | tf_op jit(solution)/shard_map/all_to_all | solution.py:52
  27.8 0.0 all-gather.3.cloned.1.call-start
  27.8 0.0 copy-done.5
  27.8 4.6 %collective-permute-start = (bf16[32,2048]{1,0:T(8,128)(2,1)S(1)}, bf16[32,2048]{1,0:T(8,128)(2,1)S(1)}, u32[]{:S(2)}, u32[]{:S(2)}) collective-permute-start(bf16[32,2048]{1,0:T(8,128)(2,1)S(1)} %bitcast.19), channel_id=1, source_target_pairs={{16,0},{20,4},{24,8},{28,12},{32,16},{36,20},{40,24},{44,28},{48,3... | collective-permute-start | bytes 393224 | tf_op jit(solution)/shard_map/ppermute | solution.py:31
  32.4 2.3 %collective-permute-start.1 = (bf16[32,2048]{1,0:T(8,128)(2,1)S(1)}, bf16[32,2048]{1,0:T(8,128)(2,1)S(1)}, u32[]{:S(2)}, u32[]{:S(2)}) collective-permute-start(bf16[32,2048]{1,0:T(8,128)(2,1)S(1)} %bitcast.20), channel_id=1, source_target_pairs={{32,0},{36,4},{40,8},{44,12},{48,16},{52,20},{56,24},{60,28},{0,32... | collective-permute-start | bytes 393224 | tf_op jit(solution)/shard_map/ppermute | solution.py:31
  34.7 2.6 %collective-permute-start.2 = (bf16[32,2048]{1,0:T(8,128)(2,1)S(1)}, bf16[32,2048]{1,0:T(8,128)(2,1)S(1)}, u32[]{:S(2)}, u32[]{:S(2)}) collective-permute-start(bf16[32,2048]{1,0:T(8,128)(2,1)S(1)} %bitcast.21), channel_id=1, source_target_pairs={{48,0},{52,4},{56,8},{60,12},{0,16},{4,20},{8,24},{12,28},{16,32},... | collective-permute-start | bytes 393224 | tf_op jit(solution)/shard_map/ppermute | solution.py:31
  37.3 0.0 copy-done.9
  37.4 0.0 copy-done.3
  37.4 0.9 reverse_select_fusion.saved
  38.3 0.0 collective-permute-done.own1
  38.3 1.7 %collective-permute-done.1.own2 = bf16[32,2048]{1,0:T(8,128)(2,1)S(1)} collective-permute-done((bf16[32,2048]{1,0:T(8,128)(2,1)S(1)}, bf16[32,2048]{1,0:T(8,128)(2,1)S(1)}, u32[]{:S(2)}, u32[]{:S(2)}) %collective-permute-start.1) | collective-permute-done | bytes 131104 | tf_op jit(solution)/shard_map/ppermute | solution.py:31
  40.0 3.5 %collective-permute-done.2.own3 = bf16[32,2048]{1,0:T(8,128)(2,1)S(1)} collective-permute-done((bf16[32,2048]{1,0:T(8,128)(2,1)S(1)}, bf16[32,2048]{1,0:T(8,128)(2,1)S(1)}, u32[]{:S(2)}, u32[]{:S(2)}) %collective-permute-start.2) | collective-permute-done | bytes 131104 | tf_op jit(solution)/shard_map/ppermute | solution.py:31
  43.4 11.4 %all-to-all-done.kv_ref = bf16[4,32,2176]{2,1,0:T(8,128)(2,1)S(1)} async-done(((bf16[4,32,2176]{2,1,0:T(8,128)(2,1)}), bf16[4,32,2176]{2,1,0:T(8,128)(2,1)S(1)}, u32[]{:S(2)}, u32[]{:S(2)}) %all-to-all-start) | async-done | bytes 557088 | tf_op jit(solution)/shard_map/all_to_all | solution.py:52
  54.9 0.0 all-gather.3.cloned.1.call-update
  54.9 0.0 reduce-scatter.2.cloned.1.call-start
  55.0 0.1 pad_add_fusion.place
  55.0 0.7 shard_map.78
  55.7 0.0 copy-start
  55.7 0.0 copy-start.1
  55.7 0.0 copy-start.7
  55.7 24.6 %all_to_all.25.others = bf16[4,96,2176]{2,1,0:T(8,128)(2,1)S(1)} all-to-all(bf16[4,96,2176]{2,1,0:T(8,128)(2,1)S(1)} %shard_map.78), channel_id=1, replica_groups={{0,16,32,48},{4,20,36,52},{8,24,40,56},{12,28,44,60},{1,17,33,49},{5,21..., dimensions={0} | all-to-all | bytes 3342336 | tf_op jit(solution)/shard_map/all_to_all | solution.py:48
  80.3 0.0 copy-done
  80.3 4.2 %shard_map.79 = (f32[512,512]{1,0:T(8,128)S(1)}, bf16[512,512]{1,0:T(8,128)(2,1)S(1)}, f32[4,4,128]{2,1,0:T(4,128)S(1)}, f32[4,128]{1,0:T(4,128)S(1)}) custom-call(s32[4]{0:T(128)S(1)} %pad_add_fusion.place, bf16[32,2048]{1,0:T(8,128)(2,1)S(1)} %bitcast.22, bf16[32,2048]{1,0:T(8,128)(2,1)S(1)} %collective-permute-done.own1, ...), custom_call_target="tpu_custom_call" | custom-call | flops 1073741824 | bytes 6291456 | tf_op jit(solution)/shard_map/pallas_call | solution.py:56
  84.5 4.2 %collective-permute-start.3 = (bf16[512,512]{1,0:T(8,128)(2,1)S(1)}, bf16[512,512]{1,0:T(8,128)(2,1)S(1)}, u32[]{:S(2)}, u32[]{:S(2)}) collective-permute-start(bf16[512,512]{1,0:T(8,128)(2,1)S(1)} %get-tuple-element.37), channel_id=1, source_target_pairs={{0,64},{64,0},{128,192},{192,128},{256,320},{320,256},{384,448},{4... | collective-permute-start | bytes 1572872 | tf_op jit(solution)/shard_map/ppermute | solution.py:40
  88.7 6.8 %all_to_all.26 = f32[4,4,128]{2,1,0:T(4,128)S(1)} all-to-all(f32[4,4,128]{2,1,0:T(4,128)S(1)} %get-tuple-element.38), channel_id=1, replica_groups={{0,16,32,48},{4,20,36,52},{8,24,40,56},{12,28,44,60},{1,17,33,49},{5,21..., dimensions={0} | all-to-all | bytes 16384 | tf_op jit(solution)/shard_map/all_to_all | solution.py:48
  95.4 0.0 collective-permute-done.3.other
  95.4 3.4 %shard_map.83 = bf16[4,512,512]{2,1,0:T(8,128)(2,1)} custom-call(s32[4]{0:T(128)S(1)} %pad_add_fusion.place, bf16[32,2048]{1,0:T(8,128)(2,1)S(1)} %bitcast.23, bf16[32,2048]{1,0:T(8,128)(2,1)S(1)} %collective-permute-done.own1, bf16[32,2048]{1,0:T(8,128)(2,1)S(1)} %collective-permute-done.1.own2, bf16[32,2048]{1,0:T(8,128)(2,1)S(1)} %collective-permute-done.2.own3, ...), custom_call_target="tpu_custom_call" | custom-call | flops 1073741824 | bytes 6291456 | tf_op jit(solution)/shard_map/pallas_call | solution.py:56
  98.9 0.0 reduce-scatter.2.cloned.1.call-update
  98.9 0.6 shard_map.80
  99.5 1.3 collective-permute-start.4
  100.8 1.3 collective-permute-start.5
  102.1 1.3 collective-permute-start.6
  103.4 17.8 %all_to_all.27.parts = f32[4,4,128]{2,1,0:T(4,128)S(1)} all-to-all(f32[4,4,128]{2,1,0:T(4,128)S(1)} %broadcast_in_dim.6), channel_id=1, replica_groups={{0,4,8,12},{16,20,24,28},{32,36,40,44},{48,52,56,60},{1,5,9,13},{17,21,..., dimensions={0} | all-to-all | bytes 16384 | tf_op jit(solution)/shard_map/all_to_all | solution.py:52
  121.2 0.0 collective-permute-done.4.above1
  121.2 14.8 %collective-permute-done.5.above2 = bf16[256,512]{1,0:T(8,128)(2,1)S(1)} collective-permute-done((bf16[256,512]{1,0:T(8,128)(2,1)S(1)}, bf16[256,512]{1,0:T(8,128)(2,1)S(1)}, u32[]{:S(2)}, u32[]{:S(2)}) %collective-permute-start.5) | collective-permute-done | bytes 262176 | tf_op jit(solution)/shard_map/ppermute | solution.py:44
  136.0 0.0 collective-permute-done.6.above3
  136.0 0.1 add_convert_fusion
  136.1 2.9 %collective-permute-start.7 = (bf16[256,512]{1,0:T(8,128)(2,1)S(1)}, bf16[256,512]{1,0:T(8,128)(2,1)S(1)}, u32[]{:S(2)}, u32[]{:S(2)}) collective-permute-start(bf16[256,512]{1,0:T(8,128)(2,1)S(1)} %add_convert_fusion), channel_id=1, source_target_pairs={{0,64},{64,0},{128,192},{192,128},{256,320},{320,256},{384,448},{4... | collective-permute-start | bytes 786440 | tf_op jit(solution)/shard_map/ppermute | solution.py:40
  139.0 11.9 %all_to_all.28.scales = f32[8,4,128]{2,1,0:T(4,128)S(1)} all-to-all(f32[8,4,128]{2,1,0:T(4,128)S(1)} %shard_map.81), channel_id=1, replica_groups=mesh['section'=8,'tensor'=16,'dp'=4] {'section'}, dimensions={0} | all-to-all | bytes 32768 | tf_op jit(solution)/shard_map/all_to_all | solution.py:286
  150.9 0.0 collective-permute-done.7.above_other
  150.9 5.0 %shard_map.82 = bf16[2,256,512]{2,1,0:T(8,128)(2,1)} custom-call(s32[4]{0:T(128)S(1)} %pad_add_fusion.place, bf16[8,2,256,512]{3,2,1,0:T(8,128)(2,1)} %bitcast.25, f32[8,4,128]{2,1,0:T(4,128)S(1)} %all_to_all.28.scales, f32[2,256,512]{2,1,0:T(8,128)S(1)} %bitcast.13, bf16[2,256,512]{2,1,0:T(8,128)(2,1)S(1)} %bitcast.17, ...), custom_call_target="tpu_custom_call" | custom-call | tf_op jit(solution)/shard_map/pallas_call | solution.py:56
  156.0 0.0 reduce-scatter.2.cloned.1.call-done
  (12 shorter events, 0.1 us)
Async XLA Ops:
  8.0 29.3 %copy-start.9 = (s32[1,2]{1,0:T(1,128)S(1)}, s32[1,2]{1,0:T(1,128)}, u32[]{:S(2)}) copy-start(s32[1,2]{1,0:T(1,128)} %plan.1) | copy-start | bytes 28
  8.0 1.0 copy-start.2
  9.1 0.9 copy-start.4
  10.0 0.7 copy-start.8
  10.6 17.2 %copy-start.5 = (bf16[1,2,16,2048]{3,2,1,0:T(8,128)(2,1)S(1)}, bf16[1,2,16,2048]{3,2,1,0:T(8,128)(2,1)}, u32[]{:S(2)}) copy-start(bf16[1,2,16,2048]{3,2,1,0:T(8,128)(2,1)} %param.10) | copy-start | bytes 393220
  10.6 26.7 %copy-start.3 = (bf16[1,2,256,512]{3,2,1,0:T(8,128)(2,1)S(1)}, bf16[1,2,256,512]{3,2,1,0:T(8,128)(2,1)}, u32[]{:S(2)}) copy-start(bf16[1,2,256,512]{3,2,1,0:T(8,128)(2,1)} %param.7) | copy-start | bytes 1572868
  12.2 42.7 %all-to-all-start = ((bf16[4,32,2176]{2,1,0:T(8,128)(2,1)}), bf16[4,32,2176]{2,1,0:T(8,128)(2,1)S(1)}, u32[]{:S(2)}, u32[]{:S(2)}) async-start(bf16[4,32,2176]{2,1,0:T(8,128)(2,1)} %shard_map.77), calls=%async_computation | async-start | bytes 1114112 | tf_op jit(solution)/shard_map/all_to_all | solution.py:52
  27.8 108.2 %all-gather.3.cloned.1.call-start = ((), (), s32[]{:S(2)}) async-start(), calls=%async_computation.7 | async-start | bytes 4718592 | tf_op jit(solution)/shard_map/all_gather | solution.py:240
  27.8 10.5 %collective-permute-start = (bf16[32,2048]{1,0:T(8,128)(2,1)S(1)}, bf16[32,2048]{1,0:T(8,128)(2,1)S(1)}, u32[]{:S(2)}, u32[]{:S(2)}) collective-permute-start(bf16[32,2048]{1,0:T(8,128)(2,1)S(1)} %bitcast.19), channel_id=1, source_target_pairs={{16,0},{20,4},{24,8},{28,12},{32,16},{36,20},{40,24},{44,28},{48,3... | collective-permute-start | bytes 393224 | tf_op jit(solution)/shard_map/ppermute | solution.py:31
  32.4 7.5 %collective-permute-start.1 = (bf16[32,2048]{1,0:T(8,128)(2,1)S(1)}, bf16[32,2048]{1,0:T(8,128)(2,1)S(1)}, u32[]{:S(2)}, u32[]{:S(2)}) collective-permute-start(bf16[32,2048]{1,0:T(8,128)(2,1)S(1)} %bitcast.20), channel_id=1, source_target_pairs={{32,0},{36,4},{40,8},{44,12},{48,16},{52,20},{56,24},{60,28},{0,32... | collective-permute-start | bytes 393224 | tf_op jit(solution)/shard_map/ppermute | solution.py:31
  34.7 8.7 %collective-permute-start.2 = (bf16[32,2048]{1,0:T(8,128)(2,1)S(1)}, bf16[32,2048]{1,0:T(8,128)(2,1)S(1)}, u32[]{:S(2)}, u32[]{:S(2)}) collective-permute-start(bf16[32,2048]{1,0:T(8,128)(2,1)S(1)} %bitcast.21), channel_id=1, source_target_pairs={{48,0},{52,4},{56,8},{60,12},{0,16},{4,20},{8,24},{12,28},{16,32},... | collective-permute-start | bytes 393224 | tf_op jit(solution)/shard_map/ppermute | solution.py:31
  54.9 101.1 %reduce-scatter.2.cloned.1.call-start = ((), (), s32[]{:S(2)}) async-start(), calls=%async_computation.6 | async-start | bytes 2621440 | tf_op jit(solution)/shard_map/reduce_scatter | solution.py:278
  55.7 24.6 %copy-start = (bf16[2,256,512]{2,1,0:T(8,128)(2,1)S(1)}, bf16[2,256,512]{2,1,0:T(8,128)(2,1)}, u32[]{:S(2)}) copy-start(bf16[2,256,512]{2,1,0:T(8,128)(2,1)} %reverse_select_fusion.saved) | copy-start | bytes 1572868
  55.7 24.6 %copy-start.1 = (bf16[1,512,2048]{2,1,0:T(8,128)(2,1)S(1)}, bf16[1,512,2048]{2,1,0:T(8,128)(2,1)}, u32[]{:S(2)}) copy-start(bf16[1,512,2048]{2,1,0:T(8,128)(2,1)} %param.9) | copy-start | bytes 6291460
  55.7 24.6 %copy-start.7 = (bf16[1,512]{1,0:T(2,128)(2,1)S(1)}, bf16[1,512]{1,0:T(2,128)(2,1)}, u32[]{:S(2)}) copy-start(bf16[1,512]{1,0:T(2,128)(2,1)} %gains.3) | copy-start | bytes 3076
  84.5 10.9 %collective-permute-start.3 = (bf16[512,512]{1,0:T(8,128)(2,1)S(1)}, bf16[512,512]{1,0:T(8,128)(2,1)S(1)}, u32[]{:S(2)}, u32[]{:S(2)}) collective-permute-start(bf16[512,512]{1,0:T(8,128)(2,1)S(1)} %get-tuple-element.37), channel_id=1, source_target_pairs={{0,64},{64,0},{128,192},{192,128},{256,320},{320,256},{384,448},{4... | collective-permute-start | bytes 1572872 | tf_op jit(solution)/shard_map/ppermute | solution.py:40
  98.9 52.0 %copy-start.6 = (bf16[2,256,512]{2,1,0:T(8,128)(2,1)S(1)}, bf16[2,256,512]{2,1,0:T(8,128)(2,1)}, u32[]{:S(2)}) copy-start(bf16[2,256,512]{2,1,0:T(8,128)(2,1)} %top.1) | copy-start | bytes 1572868
  99.5 21.7 %collective-permute-start.4 = (bf16[256,512]{1,0:T(8,128)(2,1)S(1)}, bf16[256,512]{1,0:T(8,128)(2,1)S(1)}, u32[]{:S(2)}, u32[]{:S(2)}) collective-permute-start(bf16[256,512]{1,0:T(8,128)(2,1)S(1)} %shard_map.80), channel_id=1, source_target_pairs={{128,0},{192,64},{256,128},{320,192},{384,256},{448,320},{129,1},{... | collective-permute-start | bytes 786440 | tf_op jit(solution)/shard_map/ppermute | solution.py:44
  100.8 35.2 %collective-permute-start.5 = (bf16[256,512]{1,0:T(8,128)(2,1)S(1)}, bf16[256,512]{1,0:T(8,128)(2,1)S(1)}, u32[]{:S(2)}, u32[]{:S(2)}) collective-permute-start(bf16[256,512]{1,0:T(8,128)(2,1)S(1)} %shard_map.80), channel_id=1, source_target_pairs={{256,0},{320,64},{384,128},{448,192},{257,1},{321,65},{385,129},{4... | collective-permute-start | bytes 786440 | tf_op jit(solution)/shard_map/ppermute | solution.py:44
  102.1 33.9 %collective-permute-start.6 = (bf16[256,512]{1,0:T(8,128)(2,1)S(1)}, bf16[256,512]{1,0:T(8,128)(2,1)S(1)}, u32[]{:S(2)}, u32[]{:S(2)}) collective-permute-start(bf16[256,512]{1,0:T(8,128)(2,1)S(1)} %shard_map.80), channel_id=1, source_target_pairs={{384,0},{448,64},{385,1},{449,65},{386,2},{450,66},{387,3},{451,67... | collective-permute-start | bytes 786440 | tf_op jit(solution)/shard_map/ppermute | solution.py:44
  136.1 14.8 %collective-permute-start.7 = (bf16[256,512]{1,0:T(8,128)(2,1)S(1)}, bf16[256,512]{1,0:T(8,128)(2,1)S(1)}, u32[]{:S(2)}, u32[]{:S(2)}) collective-permute-start(bf16[256,512]{1,0:T(8,128)(2,1)S(1)} %add_convert_fusion), channel_id=1, source_target_pairs={{0,64},{64,0},{128,192},{192,128},{256,320},{320,256},{384,448},{4... | collective-permute-start | bytes 786440 | tf_op jit(solution)/shard_map/ppermute | solution.py:40
Sparse Core Ops, SparseCore 0:
  55.0 61.9 all-gather.2
Sparse Core Ops, SparseCore 1:
  99.0 34.4 reduce-scatter.1

commit v6 on v5

--- a/solution.py
+++ b/solution.py
@@ -130,9 +130,9 @@
     mine = jnp.concatenate([ref[...] for ref in (own0, own1, own2, own3)])
     product = lax.dot_general(mine, weight[...], dims, preferred_element_type=F32)
     put(product, [(lax.rem(ty + k, NY), 0) for k in range(NY)])
-    for y in range(NY):
-        product = lax.dot_general(others[y, :, :kvw], weight[...], dims, preferred_element_type=F32)
-        put(product, [(y, step) for step in range(1, NZ)])
+    rest = others[:, :, :kvw].reshape(NY * (NZ - 1) * SHARE, kvw)
+    product = lax.dot_general(rest, weight[...], dims, preferred_element_type=F32)
+    put(product, [(y, step) for y in range(NY) for step in range(1, NZ)])
     gain = gains[...].astype(F32)
     per = LANES // ROWS
     for chunk in range(MICRO * BLOCKS // per):
@@ -189,28 +189,28 @@
         out_ref[section] = scale
 
 
-def total_body(place, saved, scales, direct, other, above1, above2, above3, above_other, top, out_ref, held, sems):
-    copies = [pltpu.make_async_copy(saved.at[u], held.at[u], sems.at[u]) for u in range(NS)]
-    for copy in copies:
-        copy.start()
+def total_body(place, mine, sibling, scales, direct, other, above1, above2, above3, above_other, top, out_ref):
+    chips = NS // 2
     section, core = place[3], place[2]
     use_other = jnp.where(core == 0, 1.0, 0.0)
-    live = lax.broadcasted_iota(jnp.int32, (LANES, NS), 1) >= section
-    for copy in copies:
-        copy.wait()
+    order = [2 * c + core for c in range(chips)] + [2 * c + 1 - core for c in range(chips)]
+    live = [jnp.where(u >= section, 1.0, 0.0) for u in order]
     step = 2 * ROWS
     for m in range(MICRO):
         for first in range(0, HALF, LANES):
-            scale = scales[:, (m * HALF + first) // LANES].reshape(NS, LANES)
-            scale = jnp.where(live, jnp.transpose(scale), 0.0)
+            line = (m * HALF + first) // LANES
+            scale = [scales[u, line : line + 1] * on for u, on in zip(order, live)]
+            scale = jnp.transpose(jnp.concatenate(scale))
             for row in range(0, LANES, step):
                 at = slice(first + row, first + row + step)
                 above = above1[at].astype(F32) + above2[at].astype(F32) + above3[at].astype(F32)
                 above = jnp.where(core == m, above, above_other[at].astype(F32))
                 value = top[m, at].astype(F32) + direct[m, at] + above
                 value = value + use_other * other[m, at].astype(F32)
-                for u in range(NS):
-                    value = value - held[u, m, at].astype(F32) * scale[row : row + step, u : u + 1]
+                for k in range(NS):
+                    held = mine if k < chips else sibling
+                    here = held[k % chips, m, at].astype(F32)
+                    value = value - here * scale[row : row + step, k : k + 1]
                 out_ref[m, at] = value.astype(BF16)
 
 
@@ -230,14 +230,15 @@
     half = (tokens // 2, width)
 
     shape = jax.ShapeDtypeStruct((NZ, SHARE, kvw + LANES), BF16)
-    packed = call(pack_body, shape, [SMEM, VMEM, VMEM], (plan, kv0, slots))
+    packed = call(pack_body, shape, [SMEM, VMEM, VMEM], (plan, kv0, slots), limit=56)
     packed, kv_y, slots = lax.optimization_barrier((packed, kv0, slots))
     kv_z = z_exchange(packed)
     own = [kv_y] + [from_y(kv_y, d) for d in (1, 2, 3)]
     hidden = jnp.where(plan[0, 0] == 0, slots, slots[::-1])
     kv_z, own, hidden = lax.optimization_barrier((kv_z, own, hidden))
 
-    hidden_all = lax.all_gather(hidden, "section")
+    groups = [list(range(core, NS, 2)) for core in range(2)]
+    hidden_all = lax.all_gather(hidden, "section", axis_index_groups=groups)
     shape = jax.ShapeDtypeStruct((NY, (NZ - 1) * SHARE, kvw + LANES), BF16)
     others = y_exchange(call(spread_body, shape, [SMEM, VMEM], (place, kv_z)))
 
@@ -264,6 +265,7 @@
     above = [from_chips_above(chip, d) for d in (1, 2, 3)]
     parts = z_exchange(jnp.broadcast_to(aligned, (NZ,) + aligned.shape))
     above, parts, hidden_all = lax.optimization_barrier((above, parts, hidden_all))
+    sibling_all = from_other_core(hidden_all)
     above_other = from_other_core(sum(part.astype(F32) for part in above).astype(BF16))
 
     own, others, _ = lax.optimization_barrier((own, others, other))
@@ -288,10 +290,11 @@
     input_grads = call(
         total_body,
         jax.ShapeDtypeStruct(by_micro, BF16),
-        [SMEM, pl.BlockSpec(memory_space=pltpu.HBM)] + [VMEM] * 8,
+        [SMEM] + [VMEM] * 10,
         (
             place,
             hidden_all,
+            sibling_all,
             scales,
             direct.reshape(by_micro),
             other.reshape(by_micro),
@@ -299,8 +302,6 @@
             above_other,
             top_grad,
         ),
-        [pltpu.VMEM((NS,) + by_micro, BF16), pltpu.SemaphoreType.DMA((NS,))],
-        limit=48,
     )
     return (input_grads[None], weight_grads)
 

time: 164 us -> 160 us (0.976)
  Pallas kernels: 15.4 us -> 12.3 us
  waiting for transfers between devices: 31.4 us -> 29.7 us
    pallas_call x7, Pallas kernels: 15.4 us -> 12.3 us  [call(): pl.pallas_call(body, out_shape=out_shape, in_specs=specs, out_specs=jax.t...]
    ppermute x3, waiting for transfers between devices: 14.8 us -> 13.1 us  [from_chips_above(): lax.ppermute(value, 'section', [(s, s - 2 * chips) for s in range(2 * chi...]
    ppermute x2 -> x3, starting transfers between devices: 7.02 us -> 8.63 us  [from_other_core(): return lax.ppermute(value, 'section', [(s, s ^ 1) for s in range(NS)])]
  transfers between devices with their start and end apart: 11 -> 12, of which waited for: 4 -> 4; matrix products, arithmetic and copies ran while one was open for 1% -> 1% of each run, Pallas kernels for 9% -> 6%
where the time goes in v6:
time: 160 us; the launch traced here: 159 us
  blocking collectives  61.2 us (38%)
  starting transfers between devices  37.7 us (24%)
  waiting for transfers between devices  29.7 us (19%)
  between operations  15.7 us (10%)
  Pallas kernels  12.3 us (8%)
  local copies, waits for them, and re-layouts  1.63 us (1%)
    all_to_all x2, blocking collectives, y_exchange(): return lax.all_to_all(spread, 'tensor', 0, 0, axis_index_groups=y_groups())  31.2 us
    all_to_all x1, blocking collectives, z_exchange(): return lax.all_to_all(spread, 'tensor', 0, 0, axis_index_groups=z_groups())  17.7 us
    all_to_all x1, starting transfers between devices, z_exchange(): return lax.all_to_all(spread, 'tensor', 0, 0, axis_index_groups=z_groups())  15.6 us
    ppermute x3, waiting for transfers between devices, from_chips_above(): lax.ppermute(value, 'section', [(s, s - 2 * chips) for s in range(2 * chi...  13.1 us
    all_to_all x1, blocking collectives, shards(): scales = lax.all_to_all(scales, 'section', 0, 0)  12.3 us
    pallas_call x7, Pallas kernels, call(): pl.pallas_call(body, out_shape=out_shape, in_specs=specs, out_specs=jax.t...  12.3 us
    all_to_all x1, waiting for transfers between devices, z_exchange(): return lax.all_to_all(spread, 'tensor', 0, 0, axis_index_groups=z_groups())  11.4 us
    ppermute x3, starting transfers between devices, from_y(): return lax.ppermute(value, 'tensor', perm)  9.5 us
  transfers between devices with their start and end apart: 12, of which 4 were waited for; matrix products, arithmetic and copies ran while one was open for 1% of the time, Pallas kernels for 6%

profile of v6, /device:TPU:1, one launch (start us, length us, event | category | flops | bytes accessed | tf_op | source)
XLA Modules:
  0.0 159.3 jit_solution(6833761401668712101)
XLA Ops:
  8.0 0.0 copy-start.3
  8.0 0.0 copy-start.6
  8.0 0.0 copy-start.7
  8.0 2.2 %shard_map.77 = bf16[4,32,2176]{2,1,0:T(8,128)(2,1)} custom-call(s32[1,2]{1,0:T(1,128)} %plan.1, bf16[32,2048]{1,0:T(8,128)(2,1)} %bitcast.18, bf16[2,256,512]{2,1,0:T(8,128)(2,1)} %bitcast.24), custom_call_target="tpu_custom_call" | custom-call | tf_op jit(solution)/shard_map/pallas_call | solution.py:56
  10.2 15.6 %all-to-all-start = ((bf16[4,32,2176]{2,1,0:T(8,128)(2,1)}), bf16[4,32,2176]{2,1,0:T(8,128)(2,1)S(1)}, u32[]{:S(2)}, u32[]{:S(2)}) async-start(bf16[4,32,2176]{2,1,0:T(8,128)(2,1)} %shard_map.77), calls=%async_computation | async-start | bytes 1114112 | tf_op jit(solution)/shard_map/all_to_all | solution.py:52
  25.8 0.0 all-gather.3.cloned.1.call-start
  25.8 0.0 copy-done.3
  25.8 4.6 %collective-permute-start = (bf16[32,2048]{1,0:T(8,128)(2,1)S(1)}, bf16[32,2048]{1,0:T(8,128)(2,1)S(1)}, u32[]{:S(2)}, u32[]{:S(2)}) collective-permute-start(bf16[32,2048]{1,0:T(8,128)(2,1)S(1)} %bitcast.19), channel_id=1, source_target_pairs={{16,0},{20,4},{24,8},{28,12},{32,16},{36,20},{40,24},{44,28},{48,3... | collective-permute-start | bytes 393224 | tf_op jit(solution)/shard_map/ppermute | solution.py:31
  30.5 2.3 %collective-permute-start.1 = (bf16[32,2048]{1,0:T(8,128)(2,1)S(1)}, bf16[32,2048]{1,0:T(8,128)(2,1)S(1)}, u32[]{:S(2)}, u32[]{:S(2)}) collective-permute-start(bf16[32,2048]{1,0:T(8,128)(2,1)S(1)} %bitcast.20), channel_id=1, source_target_pairs={{32,0},{36,4},{40,8},{44,12},{48,16},{52,20},{56,24},{60,28},{0,32... | collective-permute-start | bytes 393224 | tf_op jit(solution)/shard_map/ppermute | solution.py:31
  32.8 2.6 %collective-permute-start.2 = (bf16[32,2048]{1,0:T(8,128)(2,1)S(1)}, bf16[32,2048]{1,0:T(8,128)(2,1)S(1)}, u32[]{:S(2)}, u32[]{:S(2)}) collective-permute-start(bf16[32,2048]{1,0:T(8,128)(2,1)S(1)} %bitcast.21), channel_id=1, source_target_pairs={{48,0},{52,4},{56,8},{60,12},{0,16},{4,20},{8,24},{12,28},{16,32},... | collective-permute-start | bytes 393224 | tf_op jit(solution)/shard_map/ppermute | solution.py:31
  35.4 0.0 copy-done.7
  35.4 0.0 copy-done.6
  35.4 0.9 reverse_select_fusion.saved
  36.3 0.0 collective-permute-done.own1
  36.3 1.7 %collective-permute-done.1.own2 = bf16[32,2048]{1,0:T(8,128)(2,1)S(1)} collective-permute-done((bf16[32,2048]{1,0:T(8,128)(2,1)S(1)}, bf16[32,2048]{1,0:T(8,128)(2,1)S(1)}, u32[]{:S(2)}, u32[]{:S(2)}) %collective-permute-start.1) | collective-permute-done | bytes 131104 | tf_op jit(solution)/shard_map/ppermute | solution.py:31
  38.0 3.5 %collective-permute-done.2.own3 = bf16[32,2048]{1,0:T(8,128)(2,1)S(1)} collective-permute-done((bf16[32,2048]{1,0:T(8,128)(2,1)S(1)}, bf16[32,2048]{1,0:T(8,128)(2,1)S(1)}, u32[]{:S(2)}, u32[]{:S(2)}) %collective-permute-start.2) | collective-permute-done | bytes 131104 | tf_op jit(solution)/shard_map/ppermute | solution.py:31
  41.5 11.4 %all-to-all-done.kv_ref = bf16[4,32,2176]{2,1,0:T(8,128)(2,1)S(1)} async-done(((bf16[4,32,2176]{2,1,0:T(8,128)(2,1)}), bf16[4,32,2176]{2,1,0:T(8,128)(2,1)S(1)}, u32[]{:S(2)}, u32[]{:S(2)}) %all-to-all-start) | async-done | bytes 557088 | tf_op jit(solution)/shard_map/all_to_all | solution.py:52
  52.9 0.0 all-gather.3.cloned.1.call-update
  52.9 0.0 reduce-scatter.2.cloned.1.call-start
  53.0 0.1 pad_add_fusion.place
  53.1 0.7 shard_map.78
  53.8 0.0 copy-start
  53.8 0.0 copy-start.1
  53.8 0.0 copy-start.5
  53.8 24.7 %all_to_all.25.others = bf16[4,96,2176]{2,1,0:T(8,128)(2,1)S(1)} all-to-all(bf16[4,96,2176]{2,1,0:T(8,128)(2,1)S(1)} %shard_map.78), channel_id=1, replica_groups={{0,16,32,48},{4,20,36,52},{8,24,40,56},{12,28,44,60},{1,17,33,49},{5,21..., dimensions={0} | all-to-all | bytes 3342336 | tf_op jit(solution)/shard_map/all_to_all | solution.py:48
  78.5 2.6 %shard_map.79 = (f32[512,512]{1,0:T(8,128)S(1)}, bf16[512,512]{1,0:T(8,128)(2,1)S(1)}, f32[4,4,128]{2,1,0:T(4,128)S(1)}, f32[4,128]{1,0:T(4,128)S(1)}) custom-call(s32[4]{0:T(128)S(1)} %pad_add_fusion.place, bf16[32,2048]{1,0:T(8,128)(2,1)S(1)} %bitcast.22, bf16[32,2048]{1,0:T(8,128)(2,1)S(1)} %collective-permute-done.own1, ...), custom_call_target="tpu_custom_call" | custom-call | flops 1073741824 | bytes 6291456 | tf_op jit(solution)/shard_map/pallas_call | solution.py:56
  81.1 4.1 %collective-permute-start.3 = (bf16[512,512]{1,0:T(8,128)(2,1)S(1)}, bf16[512,512]{1,0:T(8,128)(2,1)S(1)}, u32[]{:S(2)}, u32[]{:S(2)}) collective-permute-start(bf16[512,512]{1,0:T(8,128)(2,1)S(1)} %get-tuple-element.37), channel_id=1, source_target_pairs={{0,64},{64,0},{128,192},{192,128},{256,320},{320,256},{384,448},{4... | collective-permute-start | bytes 1572872 | tf_op jit(solution)/shard_map/ppermute | solution.py:40
  85.1 6.5 %all_to_all.26 = f32[4,4,128]{2,1,0:T(4,128)S(1)} all-to-all(f32[4,4,128]{2,1,0:T(4,128)S(1)} %get-tuple-element.38), channel_id=1, replica_groups={{0,16,32,48},{4,20,36,52},{8,24,40,56},{12,28,44,60},{1,17,33,49},{5,21..., dimensions={0} | all-to-all | bytes 16384 | tf_op jit(solution)/shard_map/all_to_all | solution.py:48
  91.6 0.0 collective-permute-done.3.other
  91.6 3.4 %shard_map.83 = bf16[4,512,512]{2,1,0:T(8,128)(2,1)} custom-call(s32[4]{0:T(128)S(1)} %pad_add_fusion.place, bf16[32,2048]{1,0:T(8,128)(2,1)S(1)} %bitcast.23, bf16[32,2048]{1,0:T(8,128)(2,1)S(1)} %collective-permute-done.own1, bf16[32,2048]{1,0:T(8,128)(2,1)S(1)} %collective-permute-done.1.own2, bf16[32,2048]{1,0:T(8,128)(2,1)S(1)} %collective-permute-done.2.own3, ...), custom_call_target="tpu_custom_call" | custom-call | flops 1073741824 | bytes 6291456 | tf_op jit(solution)/shard_map/pallas_call | solution.py:56
  95.0 0.0 reduce-scatter.2.cloned.1.call-update
  95.1 0.6 shard_map.80
  95.7 1.3 collective-permute-start.4
  97.0 1.3 collective-permute-start.5
  98.3 1.3 collective-permute-start.6
  99.6 17.7 %all_to_all.27.parts = f32[4,4,128]{2,1,0:T(4,128)S(1)} all-to-all(f32[4,4,128]{2,1,0:T(4,128)S(1)} %broadcast_in_dim.6), channel_id=1, replica_groups={{0,4,8,12},{16,20,24,28},{32,36,40,44},{48,52,56,60},{1,5,9,13},{17,21,..., dimensions={0} | all-to-all | bytes 16384 | tf_op jit(solution)/shard_map/all_to_all | solution.py:52
  117.3 0.0 collective-permute-done.4.above1
  117.3 13.1 %collective-permute-done.5.above2 = bf16[256,512]{1,0:T(8,128)(2,1)S(1)} collective-permute-done((bf16[256,512]{1,0:T(8,128)(2,1)S(1)}, bf16[256,512]{1,0:T(8,128)(2,1)S(1)}, u32[]{:S(2)}, u32[]{:S(2)}) %collective-permute-start.5) | collective-permute-done | bytes 262176 | tf_op jit(solution)/shard_map/ppermute | solution.py:44
  130.4 0.0 collective-permute-done.6.above3
  130.4 2.6 %collective-permute-start.7 = (bf16[4,2,256,512]{3,2,1,0:T(8,128)(2,1)}, bf16[4,2,256,512]{3,2,1,0:T(8,128)(2,1)S(1)}, u32[]{:S(2)}, u32[]{:S(2)}) collective-permute-start(bf16[4,2,256,512]{3,2,1,0:T(8,128)(2,1)} %bitcast.16), channel_id=1, source_target_pairs={{0,64},{64,0},{128,192},{192,128},{256,320},{320,256},{384,448},{4... | collective-permute-start | bytes 6291464 | tf_op jit(solution)/shard_map/ppermute | solution.py:40
  133.0 0.1 add_convert_fusion
  133.1 1.9 %collective-permute-start.8 = (bf16[256,512]{1,0:T(8,128)(2,1)S(1)}, bf16[256,512]{1,0:T(8,128)(2,1)S(1)}, u32[]{:S(2)}, u32[]{:S(2)}) collective-permute-start(bf16[256,512]{1,0:T(8,128)(2,1)S(1)} %add_convert_fusion), channel_id=1, source_target_pairs={{0,64},{64,0},{128,192},{192,128},{256,320},{320,256},{384,448},{4... | collective-permute-start | bytes 786440 | tf_op jit(solution)/shard_map/ppermute | solution.py:40
  135.1 12.3 %all_to_all.28.scales = f32[8,4,128]{2,1,0:T(4,128)S(1)} all-to-all(f32[8,4,128]{2,1,0:T(4,128)S(1)} %shard_map.81), channel_id=1, replica_groups=mesh['section'=8,'tensor'=16,'dp'=4] {'section'}, dimensions={0} | all-to-all | bytes 32768 | tf_op jit(solution)/shard_map/all_to_all | solution.py:288
  147.4 0.0 collective-permute-done.8.above_other
  147.4 0.0 collective-permute-done.7.sibling
  147.4 0.0 copy-done.4
  147.4 1.6 copy-done.2
  149.0 2.9 %shard_map.82 = bf16[2,256,512]{2,1,0:T(8,128)(2,1)} custom-call(s32[4]{0:T(128)S(1)} %pad_add_fusion.place, bf16[4,2,256,512]{3,2,1,0:T(8,128)(2,1)S(1)} %bitcast.17, bf16[4,2,256,512]{3,2,1,0:T(8,128)(2,1)S(1)} %collective-permute-done.7.sibling, f32[8,4,128]{2,1,0:T(4,128)S(1)} %all_to_all.28.scales, f32[2,256,512]{2,1,0:T(8,128)S(1)} %bitcast.13, ...), custom_call_target="tpu_custom_call" | custom-call | tf_op jit(solution)/shard_map/pallas_call | solution.py:56
  (10 shorter events, 0.0 us)
Async XLA Ops:
  8.0 17.9 %copy-start.3 = (bf16[1,2,16,2048]{3,2,1,0:T(8,128)(2,1)S(1)}, bf16[1,2,16,2048]{3,2,1,0:T(8,128)(2,1)}, u32[]{:S(2)}) copy-start(bf16[1,2,16,2048]{3,2,1,0:T(8,128)(2,1)} %param.10) | copy-start | bytes 393220
  8.0 27.4 %copy-start.6 = (bf16[1,2,256,512]{3,2,1,0:T(8,128)(2,1)S(1)}, bf16[1,2,256,512]{3,2,1,0:T(8,128)(2,1)}, u32[]{:S(2)}) copy-start(bf16[1,2,256,512]{3,2,1,0:T(8,128)(2,1)} %param.7) | copy-start | bytes 1572868
  8.0 27.4 %copy-start.7 = (s32[1,2]{1,0:T(1,128)S(1)}, s32[1,2]{1,0:T(1,128)}, u32[]{:S(2)}) copy-start(s32[1,2]{1,0:T(1,128)} %plan.1) | copy-start | bytes 28
  10.2 42.7 %all-to-all-start = ((bf16[4,32,2176]{2,1,0:T(8,128)(2,1)}), bf16[4,32,2176]{2,1,0:T(8,128)(2,1)S(1)}, u32[]{:S(2)}, u32[]{:S(2)}) async-start(bf16[4,32,2176]{2,1,0:T(8,128)(2,1)} %shard_map.77), calls=%async_computation | async-start | bytes 1114112 | tf_op jit(solution)/shard_map/all_to_all | solution.py:52
  25.8 104.5 %all-gather.3.cloned.1.call-start = ((), (), s32[]{:S(2)}) async-start(), calls=%async_computation.7 | async-start | bytes 2621440 | tf_op jit(solution)/shard_map/all_gather | solution.py:241
  25.8 10.5 %collective-permute-start = (bf16[32,2048]{1,0:T(8,128)(2,1)S(1)}, bf16[32,2048]{1,0:T(8,128)(2,1)S(1)}, u32[]{:S(2)}, u32[]{:S(2)}) collective-permute-start(bf16[32,2048]{1,0:T(8,128)(2,1)S(1)} %bitcast.19), channel_id=1, source_target_pairs={{16,0},{20,4},{24,8},{28,12},{32,16},{36,20},{40,24},{44,28},{48,3... | collective-permute-start | bytes 393224 | tf_op jit(solution)/shard_map/ppermute | solution.py:31
  30.5 7.5 %collective-permute-start.1 = (bf16[32,2048]{1,0:T(8,128)(2,1)S(1)}, bf16[32,2048]{1,0:T(8,128)(2,1)S(1)}, u32[]{:S(2)}, u32[]{:S(2)}) collective-permute-start(bf16[32,2048]{1,0:T(8,128)(2,1)S(1)} %bitcast.20), channel_id=1, source_target_pairs={{32,0},{36,4},{40,8},{44,12},{48,16},{52,20},{56,24},{60,28},{0,32... | collective-permute-start | bytes 393224 | tf_op jit(solution)/shard_map/ppermute | solution.py:31
  32.8 8.7 %collective-permute-start.2 = (bf16[32,2048]{1,0:T(8,128)(2,1)S(1)}, bf16[32,2048]{1,0:T(8,128)(2,1)S(1)}, u32[]{:S(2)}, u32[]{:S(2)}) collective-permute-start(bf16[32,2048]{1,0:T(8,128)(2,1)S(1)} %bitcast.21), channel_id=1, source_target_pairs={{48,0},{52,4},{56,8},{60,12},{0,16},{4,20},{8,24},{12,28},{16,32},... | collective-permute-start | bytes 393224 | tf_op jit(solution)/shard_map/ppermute | solution.py:31
  52.9 99.0 %reduce-scatter.2.cloned.1.call-start = ((), (), s32[]{:S(2)}) async-start(), calls=%async_computation.6 | async-start | bytes 2621440 | tf_op jit(solution)/shard_map/reduce_scatter | solution.py:280
  53.8 24.7 %copy-start = (bf16[2,256,512]{2,1,0:T(8,128)(2,1)S(1)}, bf16[2,256,512]{2,1,0:T(8,128)(2,1)}, u32[]{:S(2)}) copy-start(bf16[2,256,512]{2,1,0:T(8,128)(2,1)} %reverse_select_fusion.saved) | copy-start | bytes 1572868
  53.8 24.7 %copy-start.1 = (bf16[1,512,2048]{2,1,0:T(8,128)(2,1)S(1)}, bf16[1,512,2048]{2,1,0:T(8,128)(2,1)}, u32[]{:S(2)}) copy-start(bf16[1,512,2048]{2,1,0:T(8,128)(2,1)} %param.9) | copy-start | bytes 6291460
  53.8 24.7 %copy-start.5 = (bf16[1,512]{1,0:T(2,128)(2,1)S(1)}, bf16[1,512]{1,0:T(2,128)(2,1)}, u32[]{:S(2)}) copy-start(bf16[1,512]{1,0:T(2,128)(2,1)} %gains.3) | copy-start | bytes 3076
  81.1 10.6 %collective-permute-start.3 = (bf16[512,512]{1,0:T(8,128)(2,1)S(1)}, bf16[512,512]{1,0:T(8,128)(2,1)S(1)}, u32[]{:S(2)}, u32[]{:S(2)}) collective-permute-start(bf16[512,512]{1,0:T(8,128)(2,1)S(1)} %get-tuple-element.37), channel_id=1, source_target_pairs={{0,64},{64,0},{128,192},{192,128},{256,320},{320,256},{384,448},{4... | collective-permute-start | bytes 1572872 | tf_op jit(solution)/shard_map/ppermute | solution.py:40
  95.0 52.4 %copy-start.4 = (bf16[2,256,512]{2,1,0:T(8,128)(2,1)S(1)}, bf16[2,256,512]{2,1,0:T(8,128)(2,1)}, u32[]{:S(2)}) copy-start(bf16[2,256,512]{2,1,0:T(8,128)(2,1)} %top.1) | copy-start | bytes 1572868
  95.7 21.6 %collective-permute-start.4 = (bf16[256,512]{1,0:T(8,128)(2,1)S(1)}, bf16[256,512]{1,0:T(8,128)(2,1)S(1)}, u32[]{:S(2)}, u32[]{:S(2)}) collective-permute-start(bf16[256,512]{1,0:T(8,128)(2,1)S(1)} %shard_map.80), channel_id=1, source_target_pairs={{128,0},{192,64},{256,128},{320,192},{384,256},{448,320},{129,1},{... | collective-permute-start | bytes 786440 | tf_op jit(solution)/shard_map/ppermute | solution.py:44
  97.0 33.4 %collective-permute-start.5 = (bf16[256,512]{1,0:T(8,128)(2,1)S(1)}, bf16[256,512]{1,0:T(8,128)(2,1)S(1)}, u32[]{:S(2)}, u32[]{:S(2)}) collective-permute-start(bf16[256,512]{1,0:T(8,128)(2,1)S(1)} %shard_map.80), channel_id=1, source_target_pairs={{256,0},{320,64},{384,128},{448,192},{257,1},{321,65},{385,129},{4... | collective-permute-start | bytes 786440 | tf_op jit(solution)/shard_map/ppermute | solution.py:44
  98.3 32.1 %collective-permute-start.6 = (bf16[256,512]{1,0:T(8,128)(2,1)S(1)}, bf16[256,512]{1,0:T(8,128)(2,1)S(1)}, u32[]{:S(2)}, u32[]{:S(2)}) collective-permute-start(bf16[256,512]{1,0:T(8,128)(2,1)S(1)} %shard_map.80), channel_id=1, source_target_pairs={{384,0},{448,64},{385,1},{449,65},{386,2},{450,66},{387,3},{451,67... | collective-permute-start | bytes 786440 | tf_op jit(solution)/shard_map/ppermute | solution.py:44
  130.4 17.1 %collective-permute-start.7 = (bf16[4,2,256,512]{3,2,1,0:T(8,128)(2,1)}, bf16[4,2,256,512]{3,2,1,0:T(8,128)(2,1)S(1)}, u32[]{:S(2)}, u32[]{:S(2)}) collective-permute-start(bf16[4,2,256,512]{3,2,1,0:T(8,128)(2,1)} %bitcast.16), channel_id=1, source_target_pairs={{0,64},{64,0},{128,192},{192,128},{256,320},{320,256},{384,448},{4... | collective-permute-start | bytes 6291464 | tf_op jit(solution)/shard_map/ppermute | solution.py:40
  133.1 14.3 %collective-permute-start.8 = (bf16[256,512]{1,0:T(8,128)(2,1)S(1)}, bf16[256,512]{1,0:T(8,128)(2,1)S(1)}, u32[]{:S(2)}, u32[]{:S(2)}) collective-permute-start(bf16[256,512]{1,0:T(8,128)(2,1)S(1)} %add_convert_fusion), channel_id=1, source_target_pairs={{0,64},{64,0},{128,192},{192,128},{256,320},{320,256},{384,448},{4... | collective-permute-start | bytes 786440 | tf_op jit(solution)/shard_map/ppermute | solution.py:40
  147.4 1.6 copy-start.2
Sparse Core Ops, SparseCore 0:
  53.1 56.8 all-gather.2
Sparse Core Ops, SparseCore 1:
  95.1 34.6 reduce-scatter.1

commit v7 on v6

--- a/solution.py
+++ b/solution.py
@@ -189,29 +189,37 @@
         out_ref[section] = scale
 
 
-def total_body(place, mine, sibling, scales, direct, other, above1, above2, above3, above_other, top, out_ref):
+def fix_body(place, saved, scales, above1, above2, above3, kept, sent):
+    section, core = place[3], place[2]
     chips = NS // 2
-    section, core = place[3], place[2]
-    use_other = jnp.where(core == 0, 1.0, 0.0)
-    order = [2 * c + core for c in range(chips)] + [2 * c + 1 - core for c in range(chips)]
-    live = [jnp.where(u >= section, 1.0, 0.0) for u in order]
+    chip = section // 2
+    chip_at = [jnp.minimum(chip + d, chips - 1) for d in range(chips)]
     step = 2 * ROWS
     for m in range(MICRO):
         for first in range(0, HALF, LANES):
             line = (m * HALF + first) // LANES
-            scale = [scales[u, line : line + 1] * on for u, on in zip(order, live)]
-            scale = jnp.transpose(jnp.concatenate(scale))
+            scale = []
+            for d in range(chips):
+                at = jnp.minimum(section + 2 * d, NS - 1)
+                live = jnp.where(chip + d < chips, 1.0, 0.0)
+                scale.append(scales[at, line : line + 1] * live)
+            scale = jnp.transpose(jnp.concatenate(scale + scale))
             for row in range(0, LANES, step):
                 at = slice(first + row, first + row + step)
+                here = slice(row, row + step)
                 above = above1[at].astype(F32) + above2[at].astype(F32) + above3[at].astype(F32)
-                above = jnp.where(core == m, above, above_other[at].astype(F32))
-                value = top[m, at].astype(F32) + direct[m, at] + above
-                value = value + use_other * other[m, at].astype(F32)
-                for k in range(NS):
-                    held = mine if k < chips else sibling
-                    here = held[k % chips, m, at].astype(F32)
-                    value = value - here * scale[row : row + step, k : k + 1]
-                out_ref[m, at] = value.astype(BF16)
+                value = jnp.where(core == m, above, 0.0)
+                for d in range(1, chips):
+                    value = value - saved[chip_at[d], m, at].astype(F32) * scale[here, d : d + 1]
+                whole = value - saved[chip, m, at].astype(F32) * scale[here, :1]
+                kept[m, at] = whole
+                sent[m, at] = jnp.where(core == 1, whole, value).astype(BF16)
+
+
+def total_body(place, kept, got, direct, other, top, out_ref):
+    use_other = jnp.where(place[2] == 0, 1.0, 0.0)
+    value = top[...].astype(F32) + direct[...] + use_other * other[...].astype(F32)
+    out_ref[...] = (value + (kept[...] + got[...].astype(F32))).astype(BF16)
 
 
 def shards(plan, stashed, norm_gain, kv_weight, kv_grad, top_grad):
@@ -238,7 +246,7 @@
     kv_z, own, hidden = lax.optimization_barrier((kv_z, own, hidden))
 
     groups = [list(range(core, NS, 2)) for core in range(2)]
-    hidden_all = lax.all_gather(hidden, "section", axis_index_groups=groups)
+    saved = lax.all_gather(hidden, "section", axis_index_groups=groups)
     shape = jax.ShapeDtypeStruct((NY, (NZ - 1) * SHARE, kvw + LANES), BF16)
     others = y_exchange(call(spread_body, shape, [SMEM, VMEM], (place, kv_z)))
 
@@ -264,9 +272,7 @@
     chip = call(half_body, jax.ShapeDtypeStruct(half, BF16), [SMEM, VMEM, VMEM], (place, direct, other))
     above = [from_chips_above(chip, d) for d in (1, 2, 3)]
     parts = z_exchange(jnp.broadcast_to(aligned, (NZ,) + aligned.shape))
-    above, parts, hidden_all = lax.optimization_barrier((above, parts, hidden_all))
-    sibling_all = from_other_core(hidden_all)
-    above_other = from_other_core(sum(part.astype(F32) for part in above).astype(BF16))
+    parts, saved = lax.optimization_barrier((parts, saved))
 
     own, others, _ = lax.optimization_barrier((own, others, other))
     local = call(
@@ -287,21 +293,18 @@
     )
     scales = lax.all_to_all(scales, "section", 0, 0)
     by_micro = (MICRO, tokens // MICRO, width)
+    kept, sent = call(
+        fix_body,
+        (jax.ShapeDtypeStruct(by_micro, F32), jax.ShapeDtypeStruct(by_micro, BF16)),
+        [SMEM] + [VMEM] * 5,
+        (place, saved, scales, *above),
+    )
+    got = from_other_core(sent)
     input_grads = call(
         total_body,
         jax.ShapeDtypeStruct(by_micro, BF16),
-        [SMEM] + [VMEM] * 10,
-        (
-            place,
-            hidden_all,
-            sibling_all,
-            scales,
-            direct.reshape(by_micro),
-            other.reshape(by_micro),
-            *above,
-            above_other,
-            top_grad,
-        ),
+        [SMEM] + [VMEM] * 5,
+        (place, kept, got, direct.reshape(by_micro), other.reshape(by_micro), top_grad),
     )
     return (input_grads[None], weight_grads)
 

time: 160 us -> 161 us (level)
  starting transfers between devices: 37.7 us -> 56.7 us
  blocking collectives: 61.2 us -> 48.9 us
  waiting for transfers between devices: 29.7 us -> 23.1 us
    all_to_all x0 -> x1, starting transfers between devices: none -> 20.9 us  [shards(): scales = lax.all_to_all(scales, 'section', 0, 0)]
    ppermute x3, waiting for transfers between devices: 13.1 us -> 0.01 us  [from_chips_above(): lax.ppermute(value, 'section', [(s, s - 2 * chips) for s in range(2 * chi...]
    all_to_all x1 -> x0, blocking collectives: 12.3 us -> none  [shards(): scales = lax.all_to_all(scales, 'section', 0, 0)]
    all_to_all x0 -> x1, waiting for transfers between devices: none -> 4.91 us  [shards(): scales = lax.all_to_all(scales, 'section', 0, 0)]
    ppermute x3 -> x2, starting transfers between devices: 8.63 us -> 6.71 us  [from_other_core(): return lax.ppermute(value, 'section', [(s, s ^ 1) for s in range(NS)])]
    pallas_call x7 -> x8, Pallas kernels: 12.3 us -> 13.1 us  [call(): pl.pallas_call(body, out_shape=out_shape, in_specs=specs, out_specs=jax.t...]
  transfers between devices with their start and end apart: 12 -> 12, of which waited for: 4 -> 5; matrix products, arithmetic and copies ran while one was open for 1% -> 1% of each run, Pallas kernels for 6% -> 7%
where the time goes in v7:
time: 161 us; the launch traced here: 160 us
  starting transfers between devices  56.7 us (35%)
  blocking collectives  48.9 us (30%)
  waiting for transfers between devices  23.1 us (14%)
  between operations  15.7 us (10%)
  Pallas kernels  13.1 us (8%)
  local copies, waits for them, and re-layouts  1.63 us (1%)
    all_to_all x2, blocking collectives, y_exchange(): return lax.all_to_all(spread, 'tensor', 0, 0, axis_index_groups=y_groups())  31.2 us
    all_to_all x1, starting transfers between devices, shards(): scales = lax.all_to_all(scales, 'section', 0, 0)  20.9 us
    all_to_all x1, blocking collectives, z_exchange(): return lax.all_to_all(spread, 'tensor', 0, 0, axis_index_groups=z_groups())  17.7 us
    all_to_all x1, starting transfers between devices, z_exchange(): return lax.all_to_all(spread, 'tensor', 0, 0, axis_index_groups=z_groups())  15.6 us
    pallas_call x8, Pallas kernels, call(): pl.pallas_call(body, out_shape=out_shape, in_specs=specs, out_specs=jax.t...  13.1 us
    all_to_all x1, waiting for transfers between devices, z_exchange(): return lax.all_to_all(spread, 'tensor', 0, 0, axis_index_groups=z_groups())  11.4 us
    ppermute x3, starting transfers between devices, from_y(): return lax.ppermute(value, 'tensor', perm)  9.5 us
    ppermute x2, starting transfers between devices, from_other_core(): return lax.ppermute(value, 'section', [(s, s ^ 1) for s in range(NS)])  6.71 us
  transfers between devices with their start and end apart: 12, of which 5 were waited for; matrix products, arithmetic and copies ran while one was open for 1% of the time, Pallas kernels for 7%

profile of v7, /device:TPU:1, one launch (start us, length us, event | category | flops | bytes accessed | tf_op | source)
XLA Modules:
  0.0 160.0 jit_solution(14758104189684859065)
XLA Ops:
  8.0 0.0 copy-start.3
  8.0 0.0 copy-start.6
  8.0 0.0 copy-start.7
  8.0 2.2 %shard_map.77 = bf16[4,32,2176]{2,1,0:T(8,128)(2,1)} custom-call(s32[1,2]{1,0:T(1,128)} %plan.1, bf16[32,2048]{1,0:T(8,128)(2,1)} %bitcast.17, bf16[2,256,512]{2,1,0:T(8,128)(2,1)} %bitcast.23), custom_call_target="tpu_custom_call" | custom-call | tf_op jit(solution)/shard_map/pallas_call | solution.py:56
  10.2 15.6 %all-to-all-start = ((bf16[4,32,2176]{2,1,0:T(8,128)(2,1)}), bf16[4,32,2176]{2,1,0:T(8,128)(2,1)S(1)}, u32[]{:S(2)}, u32[]{:S(2)}) async-start(bf16[4,32,2176]{2,1,0:T(8,128)(2,1)} %shard_map.77), calls=%async_computation | async-start | bytes 1114112 | tf_op jit(solution)/shard_map/all_to_all | solution.py:52
  25.8 0.0 all-gather.3.cloned.1.call-start
  25.8 0.0 copy-done.3
  25.9 4.6 %collective-permute-start = (bf16[32,2048]{1,0:T(8,128)(2,1)S(1)}, bf16[32,2048]{1,0:T(8,128)(2,1)S(1)}, u32[]{:S(2)}, u32[]{:S(2)}) collective-permute-start(bf16[32,2048]{1,0:T(8,128)(2,1)S(1)} %bitcast.18), channel_id=1, source_target_pairs={{16,0},{20,4},{24,8},{28,12},{32,16},{36,20},{40,24},{44,28},{48,3... | collective-permute-start | bytes 393224 | tf_op jit(solution)/shard_map/ppermute | solution.py:31
  30.5 2.3 %collective-permute-start.1 = (bf16[32,2048]{1,0:T(8,128)(2,1)S(1)}, bf16[32,2048]{1,0:T(8,128)(2,1)S(1)}, u32[]{:S(2)}, u32[]{:S(2)}) collective-permute-start(bf16[32,2048]{1,0:T(8,128)(2,1)S(1)} %bitcast.19), channel_id=1, source_target_pairs={{32,0},{36,4},{40,8},{44,12},{48,16},{52,20},{56,24},{60,28},{0,32... | collective-permute-start | bytes 393224 | tf_op jit(solution)/shard_map/ppermute | solution.py:31
  32.8 2.6 %collective-permute-start.2 = (bf16[32,2048]{1,0:T(8,128)(2,1)S(1)}, bf16[32,2048]{1,0:T(8,128)(2,1)S(1)}, u32[]{:S(2)}, u32[]{:S(2)}) collective-permute-start(bf16[32,2048]{1,0:T(8,128)(2,1)S(1)} %bitcast.20), channel_id=1, source_target_pairs={{48,0},{52,4},{56,8},{60,12},{0,16},{4,20},{8,24},{12,28},{16,32},... | collective-permute-start | bytes 393224 | tf_op jit(solution)/shard_map/ppermute | solution.py:31
  35.4 0.0 copy-done.7
  35.4 0.9 reverse_select_fusion.saved
  36.3 0.0 collective-permute-done.own1
  36.3 1.7 %collective-permute-done.1.own2 = bf16[32,2048]{1,0:T(8,128)(2,1)S(1)} collective-permute-done((bf16[32,2048]{1,0:T(8,128)(2,1)S(1)}, bf16[32,2048]{1,0:T(8,128)(2,1)S(1)}, u32[]{:S(2)}, u32[]{:S(2)}) %collective-permute-start.1) | collective-permute-done | bytes 131104 | tf_op jit(solution)/shard_map/ppermute | solution.py:31
  38.0 3.5 %collective-permute-done.2.own3 = bf16[32,2048]{1,0:T(8,128)(2,1)S(1)} collective-permute-done((bf16[32,2048]{1,0:T(8,128)(2,1)S(1)}, bf16[32,2048]{1,0:T(8,128)(2,1)S(1)}, u32[]{:S(2)}, u32[]{:S(2)}) %collective-permute-start.2) | collective-permute-done | bytes 131104 | tf_op jit(solution)/shard_map/ppermute | solution.py:31
  41.5 11.4 %all-to-all-done.kv_ref = bf16[4,32,2176]{2,1,0:T(8,128)(2,1)S(1)} async-done(((bf16[4,32,2176]{2,1,0:T(8,128)(2,1)}), bf16[4,32,2176]{2,1,0:T(8,128)(2,1)S(1)}, u32[]{:S(2)}, u32[]{:S(2)}) %all-to-all-start) | async-done | bytes 557088 | tf_op jit(solution)/shard_map/all_to_all | solution.py:52
  52.9 0.0 all-gather.3.cloned.1.call-update
  52.9 0.0 reduce-scatter.2.cloned.1.call-start
  53.0 0.1 pad_add_fusion.place
  53.1 0.7 shard_map.78
  53.8 0.0 copy-start
  53.8 0.0 copy-start.2
  53.8 0.0 copy-start.5
  53.8 24.7 %all_to_all.25.others = bf16[4,96,2176]{2,1,0:T(8,128)(2,1)S(1)} all-to-all(bf16[4,96,2176]{2,1,0:T(8,128)(2,1)S(1)} %shard_map.78), channel_id=1, replica_groups={{0,16,32,48},{4,20,36,52},{8,24,40,56},{12,28,44,60},{1,17,33,49},{5,21..., dimensions={0} | all-to-all | bytes 3342336 | tf_op jit(solution)/shard_map/all_to_all | solution.py:48
  78.5 0.0 copy-done.2
  78.5 2.6 %shard_map.79 = (f32[512,512]{1,0:T(8,128)S(1)}, bf16[512,512]{1,0:T(8,128)(2,1)S(1)}, f32[4,4,128]{2,1,0:T(4,128)S(1)}, f32[4,128]{1,0:T(4,128)S(1)}) custom-call(s32[4]{0:T(128)S(1)} %pad_add_fusion.place, bf16[32,2048]{1,0:T(8,128)(2,1)S(1)} %bitcast.21, bf16[32,2048]{1,0:T(8,128)(2,1)S(1)} %collective-permute-done.own1, ...), custom_call_target="tpu_custom_call" | custom-call | flops 1073741824 | bytes 6291456 | tf_op jit(solution)/shard_map/pallas_call | solution.py:56
  81.0 4.1 %collective-permute-start.3 = (bf16[512,512]{1,0:T(8,128)(2,1)S(1)}, bf16[512,512]{1,0:T(8,128)(2,1)S(1)}, u32[]{:S(2)}, u32[]{:S(2)}) collective-permute-start(bf16[512,512]{1,0:T(8,128)(2,1)S(1)} %get-tuple-element.35), channel_id=1, source_target_pairs={{0,64},{64,0},{128,192},{192,128},{256,320},{320,256},{384,448},{4... | collective-permute-start | bytes 1572872 | tf_op jit(solution)/shard_map/ppermute | solution.py:40
  85.1 6.5 %all_to_all.26 = f32[4,4,128]{2,1,0:T(4,128)S(1)} all-to-all(f32[4,4,128]{2,1,0:T(4,128)S(1)} %get-tuple-element.36), channel_id=1, replica_groups={{0,16,32,48},{4,20,36,52},{8,24,40,56},{12,28,44,60},{1,17,33,49},{5,21..., dimensions={0} | all-to-all | bytes 16384 | tf_op jit(solution)/shard_map/all_to_all | solution.py:48
  91.6 0.0 collective-permute-done.3.other
  91.6 3.4 %shard_map.84 = bf16[4,512,512]{2,1,0:T(8,128)(2,1)} custom-call(s32[4]{0:T(128)S(1)} %pad_add_fusion.place, bf16[32,2048]{1,0:T(8,128)(2,1)S(1)} %bitcast.22, bf16[32,2048]{1,0:T(8,128)(2,1)S(1)} %collective-permute-done.own1, bf16[32,2048]{1,0:T(8,128)(2,1)S(1)} %collective-permute-done.1.own2, bf16[32,2048]{1,0:T(8,128)(2,1)S(1)} %collective-permute-done.2.own3, ...), custom_call_target="tpu_custom_call" | custom-call | flops 1073741824 | bytes 6291456 | tf_op jit(solution)/shard_map/pallas_call | solution.py:56
  95.0 0.0 reduce-scatter.2.cloned.1.call-update
  95.0 0.0 copy-start.4
  95.1 0.6 shard_map.81
  95.7 1.3 collective-permute-start.4
  97.0 1.3 collective-permute-start.5
  98.3 1.3 collective-permute-start.6
  99.6 17.7 %all_to_all.27.parts = f32[4,4,128]{2,1,0:T(4,128)S(1)} all-to-all(f32[4,4,128]{2,1,0:T(4,128)S(1)} %broadcast_in_dim.6), channel_id=1, replica_groups={{0,4,8,12},{16,20,24,28},{32,36,40,44},{48,52,56,60},{1,5,9,13},{17,21,..., dimensions={0} | all-to-all | bytes 16384 | tf_op jit(solution)/shard_map/all_to_all | solution.py:52
  117.3 0.6 shard_map.80
  117.9 20.9 %all-to-all-start.4 = ((f32[8,4,128]{2,1,0:T(4,128)}), f32[8,4,128]{2,1,0:T(4,128)S(1)}, u32[]{:S(2)}, u32[]{:S(2)}) async-start(f32[8,4,128]{2,1,0:T(4,128)} %shard_map.80), calls=%async_computation.4 | async-start | bytes 32768 | tf_op jit(solution)/shard_map/all_to_all | solution.py:294
  138.8 0.0 collective-permute-done.4.above1
  138.8 0.0 collective-permute-done.5.above2
  138.8 0.0 collective-permute-done.6.above3
  138.8 4.9 %all-to-all-done.4.scales = f32[8,4,128]{2,1,0:T(4,128)S(1)} async-done(((f32[8,4,128]{2,1,0:T(4,128)}), f32[8,4,128]{2,1,0:T(4,128)S(1)}, u32[]{:S(2)}, u32[]{:S(2)}) %all-to-all-start.4) | async-done | bytes 16416 | tf_op jit(solution)/shard_map/all_to_all | solution.py:294
  143.7 1.6 copy-done.1
  145.3 1.4 shard_map.82
  146.7 2.6 %collective-permute-start.7 = (bf16[2,256,512]{2,1,0:T(8,128)(2,1)S(1)}, bf16[2,256,512]{2,1,0:T(8,128)(2,1)S(1)}, u32[]{:S(2)}, u32[]{:S(2)}) collective-permute-start(bf16[2,256,512]{2,1,0:T(8,128)(2,1)S(1)} %get-tuple-element.44), channel_id=1, source_target_pairs={{0,64},{64,0},{128,192},{192,128},{256,320},{320,256},{384,448},{4... | collective-permute-start | bytes 1572872 | tf_op jit(solution)/shard_map/ppermute | solution.py:40
  149.4 1.5 collective-permute-done.7.got
  150.9 1.6 %shard_map.83 = bf16[2,256,512]{2,1,0:T(8,128)(2,1)} custom-call(s32[4]{0:T(128)S(1)} %pad_add_fusion.place, f32[2,256,512]{2,1,0:T(8,128)S(1)} %get-tuple-element.43.kept, bf16[2,256,512]{2,1,0:T(8,128)(2,1)S(1)} %collective-permute-done.7.got, f32[2,256,512]{2,1,0:T(8,128)S(1)} %bitcast.13, bf16[2,256,512]{2,1,0:T(8,128)(2,1)S(1)} %bitcast.16, ...), custom_call_target="tpu_custom_call" | custom-call | tf_op jit(solution)/shard_map/pallas_call | solution.py:56
  (9 shorter events, 0.0 us)
Async XLA Ops:
  8.0 17.9 %copy-start.3 = (bf16[1,2,16,2048]{3,2,1,0:T(8,128)(2,1)S(1)}, bf16[1,2,16,2048]{3,2,1,0:T(8,128)(2,1)}, u32[]{:S(2)}) copy-start(bf16[1,2,16,2048]{3,2,1,0:T(8,128)(2,1)} %param.10) | copy-start | bytes 393220
  8.0 27.4 %copy-start.6 = (bf16[1,2,256,512]{3,2,1,0:T(8,128)(2,1)S(1)}, bf16[1,2,256,512]{3,2,1,0:T(8,128)(2,1)}, u32[]{:S(2)}) copy-start(bf16[1,2,256,512]{3,2,1,0:T(8,128)(2,1)} %param.7) | copy-start | bytes 1572868
  8.0 27.4 %copy-start.7 = (s32[1,2]{1,0:T(1,128)S(1)}, s32[1,2]{1,0:T(1,128)}, u32[]{:S(2)}) copy-start(s32[1,2]{1,0:T(1,128)} %plan.1) | copy-start | bytes 28
  10.2 42.7 %all-to-all-start = ((bf16[4,32,2176]{2,1,0:T(8,128)(2,1)}), bf16[4,32,2176]{2,1,0:T(8,128)(2,1)S(1)}, u32[]{:S(2)}, u32[]{:S(2)}) async-start(bf16[4,32,2176]{2,1,0:T(8,128)(2,1)} %shard_map.77), calls=%async_computation | async-start | bytes 1114112 | tf_op jit(solution)/shard_map/all_to_all | solution.py:52
  25.8 91.4 %all-gather.3.cloned.1.call-start = ((), (), s32[]{:S(2)}) async-start(), calls=%async_computation.7 | async-start | bytes 2621440 | tf_op jit(solution)/shard_map/all_gather | solution.py:249
  25.9 10.5 %collective-permute-start = (bf16[32,2048]{1,0:T(8,128)(2,1)S(1)}, bf16[32,2048]{1,0:T(8,128)(2,1)S(1)}, u32[]{:S(2)}, u32[]{:S(2)}) collective-permute-start(bf16[32,2048]{1,0:T(8,128)(2,1)S(1)} %bitcast.18), channel_id=1, source_target_pairs={{16,0},{20,4},{24,8},{28,12},{32,16},{36,20},{40,24},{44,28},{48,3... | collective-permute-start | bytes 393224 | tf_op jit(solution)/shard_map/ppermute | solution.py:31
  30.5 7.5 %collective-permute-start.1 = (bf16[32,2048]{1,0:T(8,128)(2,1)S(1)}, bf16[32,2048]{1,0:T(8,128)(2,1)S(1)}, u32[]{:S(2)}, u32[]{:S(2)}) collective-permute-start(bf16[32,2048]{1,0:T(8,128)(2,1)S(1)} %bitcast.19), channel_id=1, source_target_pairs={{32,0},{36,4},{40,8},{44,12},{48,16},{52,20},{56,24},{60,28},{0,32... | collective-permute-start | bytes 393224 | tf_op jit(solution)/shard_map/ppermute | solution.py:31
  32.8 8.7 %collective-permute-start.2 = (bf16[32,2048]{1,0:T(8,128)(2,1)S(1)}, bf16[32,2048]{1,0:T(8,128)(2,1)S(1)}, u32[]{:S(2)}, u32[]{:S(2)}) collective-permute-start(bf16[32,2048]{1,0:T(8,128)(2,1)S(1)} %bitcast.20), channel_id=1, source_target_pairs={{48,0},{52,4},{56,8},{60,12},{0,16},{4,20},{8,24},{12,28},{16,32},... | collective-permute-start | bytes 393224 | tf_op jit(solution)/shard_map/ppermute | solution.py:31
  52.9 99.6 %reduce-scatter.2.cloned.1.call-start = ((), (), s32[]{:S(2)}) async-start(), calls=%async_computation.6 | async-start | bytes 2621440 | tf_op jit(solution)/shard_map/reduce_scatter | solution.py:286
  53.8 24.7 %copy-start = (bf16[2,256,512]{2,1,0:T(8,128)(2,1)S(1)}, bf16[2,256,512]{2,1,0:T(8,128)(2,1)}, u32[]{:S(2)}) copy-start(bf16[2,256,512]{2,1,0:T(8,128)(2,1)} %reverse_select_fusion.saved) | copy-start | bytes 1572868
  53.8 24.7 %copy-start.2 = (bf16[1,512,2048]{2,1,0:T(8,128)(2,1)S(1)}, bf16[1,512,2048]{2,1,0:T(8,128)(2,1)}, u32[]{:S(2)}) copy-start(bf16[1,512,2048]{2,1,0:T(8,128)(2,1)} %param.9) | copy-start | bytes 6291460
  53.8 24.7 %copy-start.5 = (bf16[1,512]{1,0:T(2,128)(2,1)S(1)}, bf16[1,512]{1,0:T(2,128)(2,1)}, u32[]{:S(2)}) copy-start(bf16[1,512]{1,0:T(2,128)(2,1)} %gains.3) | copy-start | bytes 3076
  81.0 10.6 %collective-permute-start.3 = (bf16[512,512]{1,0:T(8,128)(2,1)S(1)}, bf16[512,512]{1,0:T(8,128)(2,1)S(1)}, u32[]{:S(2)}, u32[]{:S(2)}) collective-permute-start(bf16[512,512]{1,0:T(8,128)(2,1)S(1)} %get-tuple-element.35), channel_id=1, source_target_pairs={{0,64},{64,0},{128,192},{192,128},{256,320},{320,256},{384,448},{4... | collective-permute-start | bytes 1572872 | tf_op jit(solution)/shard_map/ppermute | solution.py:40
  95.0 55.8 %copy-start.4 = (bf16[2,256,512]{2,1,0:T(8,128)(2,1)S(1)}, bf16[2,256,512]{2,1,0:T(8,128)(2,1)}, u32[]{:S(2)}) copy-start(bf16[2,256,512]{2,1,0:T(8,128)(2,1)} %top.1) | copy-start | bytes 1572868
  95.7 43.1 %collective-permute-start.4 = (bf16[256,512]{1,0:T(8,128)(2,1)S(1)}, bf16[256,512]{1,0:T(8,128)(2,1)S(1)}, u32[]{:S(2)}, u32[]{:S(2)}) collective-permute-start(bf16[256,512]{1,0:T(8,128)(2,1)S(1)} %shard_map.81), channel_id=1, source_target_pairs={{128,0},{192,64},{256,128},{320,192},{384,256},{448,320},{129,1},{... | collective-permute-start | bytes 786440 | tf_op jit(solution)/shard_map/ppermute | solution.py:44
  97.0 41.8 %collective-permute-start.5 = (bf16[256,512]{1,0:T(8,128)(2,1)S(1)}, bf16[256,512]{1,0:T(8,128)(2,1)S(1)}, u32[]{:S(2)}, u32[]{:S(2)}) collective-permute-start(bf16[256,512]{1,0:T(8,128)(2,1)S(1)} %shard_map.81), channel_id=1, source_target_pairs={{256,0},{320,64},{384,128},{448,192},{257,1},{321,65},{385,129},{4... | collective-permute-start | bytes 786440 | tf_op jit(solution)/shard_map/ppermute | solution.py:44
  98.3 40.5 %collective-permute-start.6 = (bf16[256,512]{1,0:T(8,128)(2,1)S(1)}, bf16[256,512]{1,0:T(8,128)(2,1)S(1)}, u32[]{:S(2)}, u32[]{:S(2)}) collective-permute-start(bf16[256,512]{1,0:T(8,128)(2,1)S(1)} %shard_map.81), channel_id=1, source_target_pairs={{384,0},{448,64},{385,1},{449,65},{386,2},{450,66},{387,3},{451,67... | collective-permute-start | bytes 786440 | tf_op jit(solution)/shard_map/ppermute | solution.py:44
  117.9 25.8 %all-to-all-start.4 = ((f32[8,4,128]{2,1,0:T(4,128)}), f32[8,4,128]{2,1,0:T(4,128)S(1)}, u32[]{:S(2)}, u32[]{:S(2)}) async-start(f32[8,4,128]{2,1,0:T(4,128)} %shard_map.80), calls=%async_computation.4 | async-start | bytes 32768 | tf_op jit(solution)/shard_map/all_to_all | solution.py:294
  143.7 1.6 copy-start.1
  146.7 4.2 %collective-permute-start.7 = (bf16[2,256,512]{2,1,0:T(8,128)(2,1)S(1)}, bf16[2,256,512]{2,1,0:T(8,128)(2,1)S(1)}, u32[]{:S(2)}, u32[]{:S(2)}) collective-permute-start(bf16[2,256,512]{2,1,0:T(8,128)(2,1)S(1)} %get-tuple-element.44), channel_id=1, source_target_pairs={{0,64},{64,0},{128,192},{192,128},{256,320},{320,256},{384,448},{4... | collective-permute-start | bytes 1572872 | tf_op jit(solution)/shard_map/ppermute | solution.py:40
Sparse Core Ops, SparseCore 0:
  53.1 56.8 all-gather.2
Sparse Core Ops, SparseCore 1:
  95.1 34.6 reduce-scatter.1

commit v8 on v7

--- a/solution.py
+++ b/solution.py
@@ -265,16 +265,14 @@
         pl.CostEstimate(flops=flops, bytes_accessed=6 * 2**20, transcendentals=0),
     )
     other = from_other_core(direct16)
-    aligned = y_exchange(aligned)
+    aligned = jnp.sum(z_exchange(aligned), axis=0)
     other, aligned = lax.optimization_barrier((other, aligned))
-    aligned = jnp.sum(aligned, axis=0)
 
     chip = call(half_body, jax.ShapeDtypeStruct(half, BF16), [SMEM, VMEM, VMEM], (place, direct, other))
     above = [from_chips_above(chip, d) for d in (1, 2, 3)]
-    parts = z_exchange(jnp.broadcast_to(aligned, (NZ,) + aligned.shape))
+    parts = y_exchange(jnp.broadcast_to(aligned, (NY,) + aligned.shape))
     parts, saved = lax.optimization_barrier((parts, saved))
 
-    own, others, _ = lax.optimization_barrier((own, others, other))
     local = call(
         outer_body,
         jax.ShapeDtypeStruct((NX, width, width), BF16),

time: 161 us -> 154 us (0.957)
  starting transfers between devices: 56.7 us -> 46.5 us
  waiting for transfers between devices: 23.1 us -> 26.7 us
    all_to_all x1, starting transfers between devices: 20.9 us -> 11 us  [shards(): scales = lax.all_to_all(scales, 'section', 0, 0)]
    ppermute x3, waiting for transfers between devices: 0.01 us -> 7.05 us  [from_chips_above(): lax.ppermute(value, 'section', [(s, s - 2 * chips) for s in range(2 * chi...]
    all_to_all x1, waiting for transfers between devices: 4.91 us -> 1.53 us  [shards(): scales = lax.all_to_all(scales, 'section', 0, 0)]
  transfers between devices with their start and end apart: 12 -> 12, of which waited for: 5 -> 6; matrix products, arithmetic and copies ran while one was open for 1% -> 1% of each run, Pallas kernels for 7% -> 7%
where the time goes in v8:
time: 154 us
  blocking collectives  49 us (32%)
  starting transfers between devices  46.5 us (30%)
  waiting for transfers between devices  26.7 us (17%)
  between operations  15.7 us (10%)
  Pallas kernels  13.1 us (9%)
  local copies, waits for them, and re-layouts  1.63 us (1%)
    all_to_all x2, blocking collectives, y_exchange(): return lax.all_to_all(spread, 'tensor', 0, 0, axis_index_groups=y_groups())  31.3 us
    all_to_all x1, blocking collectives, z_exchange(): return lax.all_to_all(spread, 'tensor', 0, 0, axis_index_groups=z_groups())  17.7 us
    all_to_all x1, starting transfers between devices, z_exchange(): return lax.all_to_all(spread, 'tensor', 0, 0, axis_index_groups=z_groups())  15.6 us
    pallas_call x8, Pallas kernels, call(): pl.pallas_call(body, out_shape=out_shape, in_specs=specs, out_specs=jax.t...  13.1 us
    all_to_all x1, waiting for transfers between devices, z_exchange(): return lax.all_to_all(spread, 'tensor', 0, 0, axis_index_groups=z_groups())  11.4 us
    all_to_all x1, starting transfers between devices, shards(): scales = lax.all_to_all(scales, 'section', 0, 0)  11 us
    ppermute x3, starting transfers between devices, from_y(): return lax.ppermute(value, 'tensor', perm)  9.5 us
    ppermute x3, waiting for transfers between devices, from_chips_above(): lax.ppermute(value, 'section', [(s, s - 2 * chips) for s in range(2 * chi...  7.05 us
  transfers between devices with their start and end apart: 12, of which 6 were waited for; matrix products, arithmetic and copies ran while one was open for 1% of the time, Pallas kernels for 7%

profile of v8, /device:TPU:1, one launch (start us, length us, event | category | flops | bytes accessed | tf_op | source)
XLA Modules:
  0.0 153.6 jit_solution(12162288282772771205)
XLA Ops:
  8.0 0.0 copy-start.3
  8.0 0.0 copy-start.6
  8.0 0.0 copy-start.7
  8.0 2.2 %shard_map.77 = bf16[4,32,2176]{2,1,0:T(8,128)(2,1)} custom-call(s32[1,2]{1,0:T(1,128)} %plan.1, bf16[32,2048]{1,0:T(8,128)(2,1)} %bitcast.17, bf16[2,256,512]{2,1,0:T(8,128)(2,1)} %bitcast.23), custom_call_target="tpu_custom_call" | custom-call | tf_op jit(solution)/shard_map/pallas_call | solution.py:56
  10.2 15.6 %all-to-all-start = ((bf16[4,32,2176]{2,1,0:T(8,128)(2,1)}), bf16[4,32,2176]{2,1,0:T(8,128)(2,1)S(1)}, u32[]{:S(2)}, u32[]{:S(2)}) async-start(bf16[4,32,2176]{2,1,0:T(8,128)(2,1)} %shard_map.77), calls=%async_computation | async-start | bytes 1114112 | tf_op jit(solution)/shard_map/all_to_all | solution.py:52
  25.8 0.0 all-gather.3.cloned.1.call-start
  25.8 0.0 copy-done.3
  25.9 4.6 %collective-permute-start = (bf16[32,2048]{1,0:T(8,128)(2,1)S(1)}, bf16[32,2048]{1,0:T(8,128)(2,1)S(1)}, u32[]{:S(2)}, u32[]{:S(2)}) collective-permute-start(bf16[32,2048]{1,0:T(8,128)(2,1)S(1)} %bitcast.18), channel_id=1, source_target_pairs={{16,0},{20,4},{24,8},{28,12},{32,16},{36,20},{40,24},{44,28},{48,3... | collective-permute-start | bytes 393224 | tf_op jit(solution)/shard_map/ppermute | solution.py:31
  30.5 2.3 %collective-permute-start.1 = (bf16[32,2048]{1,0:T(8,128)(2,1)S(1)}, bf16[32,2048]{1,0:T(8,128)(2,1)S(1)}, u32[]{:S(2)}, u32[]{:S(2)}) collective-permute-start(bf16[32,2048]{1,0:T(8,128)(2,1)S(1)} %bitcast.19), channel_id=1, source_target_pairs={{32,0},{36,4},{40,8},{44,12},{48,16},{52,20},{56,24},{60,28},{0,32... | collective-permute-start | bytes 393224 | tf_op jit(solution)/shard_map/ppermute | solution.py:31
  32.8 2.6 %collective-permute-start.2 = (bf16[32,2048]{1,0:T(8,128)(2,1)S(1)}, bf16[32,2048]{1,0:T(8,128)(2,1)S(1)}, u32[]{:S(2)}, u32[]{:S(2)}) collective-permute-start(bf16[32,2048]{1,0:T(8,128)(2,1)S(1)} %bitcast.20), channel_id=1, source_target_pairs={{48,0},{52,4},{56,8},{60,12},{0,16},{4,20},{8,24},{12,28},{16,32},... | collective-permute-start | bytes 393224 | tf_op jit(solution)/shard_map/ppermute | solution.py:31
  35.4 0.0 copy-done.7
  35.4 0.0 copy-done.6
  35.4 0.9 reverse_select_fusion.saved
  36.3 0.0 collective-permute-done.own1
  36.3 1.7 %collective-permute-done.1.own2 = bf16[32,2048]{1,0:T(8,128)(2,1)S(1)} collective-permute-done((bf16[32,2048]{1,0:T(8,128)(2,1)S(1)}, bf16[32,2048]{1,0:T(8,128)(2,1)S(1)}, u32[]{:S(2)}, u32[]{:S(2)}) %collective-permute-start.1) | collective-permute-done | bytes 131104 | tf_op jit(solution)/shard_map/ppermute | solution.py:31
  38.0 3.5 %collective-permute-done.2.own3 = bf16[32,2048]{1,0:T(8,128)(2,1)S(1)} collective-permute-done((bf16[32,2048]{1,0:T(8,128)(2,1)S(1)}, bf16[32,2048]{1,0:T(8,128)(2,1)S(1)}, u32[]{:S(2)}, u32[]{:S(2)}) %collective-permute-start.2) | collective-permute-done | bytes 131104 | tf_op jit(solution)/shard_map/ppermute | solution.py:31
  41.5 11.4 %all-to-all-done.kv_ref = bf16[4,32,2176]{2,1,0:T(8,128)(2,1)S(1)} async-done(((bf16[4,32,2176]{2,1,0:T(8,128)(2,1)}), bf16[4,32,2176]{2,1,0:T(8,128)(2,1)S(1)}, u32[]{:S(2)}, u32[]{:S(2)}) %all-to-all-start) | async-done | bytes 557088 | tf_op jit(solution)/shard_map/all_to_all | solution.py:52
  52.9 0.0 all-gather.3.cloned.1.call-update
  52.9 0.0 reduce-scatter.2.cloned.1.call-start
  53.0 0.1 pad_add_fusion.place
  53.1 0.7 shard_map.78
  53.8 0.0 copy-start
  53.8 0.0 copy-start.2
  53.8 0.0 copy-start.5
  53.8 24.7 %all_to_all.25.others = bf16[4,96,2176]{2,1,0:T(8,128)(2,1)S(1)} all-to-all(bf16[4,96,2176]{2,1,0:T(8,128)(2,1)S(1)} %shard_map.78), channel_id=1, replica_groups={{0,16,32,48},{4,20,36,52},{8,24,40,56},{12,28,44,60},{1,17,33,49},{5,21..., dimensions={0} | all-to-all | bytes 3342336 | tf_op jit(solution)/shard_map/all_to_all | solution.py:48
  78.5 0.0 copy-done.2
  78.5 2.6 %shard_map.79 = (f32[512,512]{1,0:T(8,128)S(1)}, bf16[512,512]{1,0:T(8,128)(2,1)S(1)}, f32[4,4,128]{2,1,0:T(4,128)S(1)}, f32[4,128]{1,0:T(4,128)S(1)}) custom-call(s32[4]{0:T(128)S(1)} %pad_add_fusion.place, bf16[32,2048]{1,0:T(8,128)(2,1)S(1)} %bitcast.21, bf16[32,2048]{1,0:T(8,128)(2,1)S(1)} %collective-permute-done.own1, ...), custom_call_target="tpu_custom_call" | custom-call | flops 1073741824 | bytes 6291456 | tf_op jit(solution)/shard_map/pallas_call | solution.py:56
  81.0 3.4 %shard_map.84 = bf16[4,512,512]{2,1,0:T(8,128)(2,1)} custom-call(s32[4]{0:T(128)S(1)} %pad_add_fusion.place, bf16[32,2048]{1,0:T(8,128)(2,1)S(1)} %bitcast.22, bf16[32,2048]{1,0:T(8,128)(2,1)S(1)} %collective-permute-done.own1, bf16[32,2048]{1,0:T(8,128)(2,1)S(1)} %collective-permute-done.1.own2, bf16[32,2048]{1,0:T(8,128)(2,1)S(1)} %collective-permute-done.2.own3, ...), custom_call_target="tpu_custom_call" | custom-call | flops 1073741824 | bytes 6291456 | tf_op jit(solution)/shard_map/pallas_call | solution.py:56
  84.4 0.0 reduce-scatter.2.cloned.1.call-update
  84.5 4.1 %collective-permute-start.3 = (bf16[512,512]{1,0:T(8,128)(2,1)S(1)}, bf16[512,512]{1,0:T(8,128)(2,1)S(1)}, u32[]{:S(2)}, u32[]{:S(2)}) collective-permute-start(bf16[512,512]{1,0:T(8,128)(2,1)S(1)} %get-tuple-element.30), channel_id=1, source_target_pairs={{0,64},{64,0},{128,192},{192,128},{256,320},{320,256},{384,448},{4... | collective-permute-start | bytes 1572872 | tf_op jit(solution)/shard_map/ppermute | solution.py:40
  88.5 17.7 %all_to_all.26 = f32[4,4,128]{2,1,0:T(4,128)S(1)} all-to-all(f32[4,4,128]{2,1,0:T(4,128)S(1)} %get-tuple-element.31), channel_id=1, replica_groups={{0,4,8,12},{16,20,24,28},{32,36,40,44},{48,52,56,60},{1,5,9,13},{17,21,..., dimensions={0} | all-to-all | bytes 16384 | tf_op jit(solution)/shard_map/all_to_all | solution.py:52
  106.3 0.0 collective-permute-done.3.other
  106.3 0.6 shard_map.81
  106.9 1.3 collective-permute-start.4
  108.2 1.3 collective-permute-start.5
  109.5 1.3 collective-permute-start.6
  110.8 6.6 %all_to_all.27.parts = f32[4,4,128]{2,1,0:T(4,128)S(1)} all-to-all(f32[4,4,128]{2,1,0:T(4,128)S(1)} %broadcast_in_dim.6), channel_id=1, replica_groups={{0,16,32,48},{4,20,36,52},{8,24,40,56},{12,28,44,60},{1,17,33,49},{5,21..., dimensions={0} | all-to-all | bytes 16384 | tf_op jit(solution)/shard_map/all_to_all | solution.py:48
  117.4 0.6 shard_map.80
  118.0 11.0 %all-to-all-start.4 = ((f32[8,4,128]{2,1,0:T(4,128)}), f32[8,4,128]{2,1,0:T(4,128)S(1)}, u32[]{:S(2)}, u32[]{:S(2)}) async-start(f32[8,4,128]{2,1,0:T(4,128)} %shard_map.80), calls=%async_computation.4 | async-start | bytes 32768 | tf_op jit(solution)/shard_map/all_to_all | solution.py:292
  129.0 0.0 collective-permute-done.4.above1
  129.0 7.0 %collective-permute-done.5.above2 = bf16[256,512]{1,0:T(8,128)(2,1)S(1)} collective-permute-done((bf16[256,512]{1,0:T(8,128)(2,1)S(1)}, bf16[256,512]{1,0:T(8,128)(2,1)S(1)}, u32[]{:S(2)}, u32[]{:S(2)}) %collective-permute-start.5) | collective-permute-done | bytes 262176 | tf_op jit(solution)/shard_map/ppermute | solution.py:44
  136.1 0.0 collective-permute-done.6.above3
  136.1 1.5 all-to-all-done.4.scales
  137.6 1.6 %copy-done.1 = bf16[8,256,512]{2,1,0:T(8,128)(2,1)S(1)} copy-done((bf16[8,256,512]{2,1,0:T(8,128)(2,1)S(1)}, bf16[8,256,512]{2,1,0:T(8,128)(2,1)}, u32[]{:S(2)}) %copy-start.1) | copy-done | bytes 2097176
  139.2 1.4 shard_map.82
  140.6 2.4 %collective-permute-start.7 = (bf16[2,256,512]{2,1,0:T(8,128)(2,1)S(1)}, bf16[2,256,512]{2,1,0:T(8,128)(2,1)S(1)}, u32[]{:S(2)}, u32[]{:S(2)}) collective-permute-start(bf16[2,256,512]{2,1,0:T(8,128)(2,1)S(1)} %get-tuple-element.39), channel_id=1, source_target_pairs={{0,64},{64,0},{128,192},{192,128},{256,320},{320,256},{384,448},{4... | collective-permute-start | bytes 1572872 | tf_op jit(solution)/shard_map/ppermute | solution.py:40
  143.0 1.5 collective-permute-done.7.got
  144.5 1.6 %shard_map.83 = bf16[2,256,512]{2,1,0:T(8,128)(2,1)} custom-call(s32[4]{0:T(128)S(1)} %pad_add_fusion.place, f32[2,256,512]{2,1,0:T(8,128)S(1)} %get-tuple-element.38.kept, bf16[2,256,512]{2,1,0:T(8,128)(2,1)S(1)} %collective-permute-done.7.got, f32[2,256,512]{2,1,0:T(8,128)S(1)} %bitcast.13, bf16[2,256,512]{2,1,0:T(8,128)(2,1)S(1)} %bitcast.16, ...), custom_call_target="tpu_custom_call" | custom-call | tf_op jit(solution)/shard_map/pallas_call | solution.py:56
  (9 shorter events, 0.0 us)
Async XLA Ops:
  8.0 17.9 %copy-start.3 = (bf16[1,2,16,2048]{3,2,1,0:T(8,128)(2,1)S(1)}, bf16[1,2,16,2048]{3,2,1,0:T(8,128)(2,1)}, u32[]{:S(2)}) copy-start(bf16[1,2,16,2048]{3,2,1,0:T(8,128)(2,1)} %param.10) | copy-start | bytes 393220
  8.0 27.4 %copy-start.6 = (bf16[1,2,256,512]{3,2,1,0:T(8,128)(2,1)S(1)}, bf16[1,2,256,512]{3,2,1,0:T(8,128)(2,1)}, u32[]{:S(2)}) copy-start(bf16[1,2,256,512]{3,2,1,0:T(8,128)(2,1)} %param.7) | copy-start | bytes 1572868
  8.0 27.4 %copy-start.7 = (s32[1,2]{1,0:T(1,128)S(1)}, s32[1,2]{1,0:T(1,128)}, u32[]{:S(2)}) copy-start(s32[1,2]{1,0:T(1,128)} %plan.1) | copy-start | bytes 28
  10.2 42.7 %all-to-all-start = ((bf16[4,32,2176]{2,1,0:T(8,128)(2,1)}), bf16[4,32,2176]{2,1,0:T(8,128)(2,1)S(1)}, u32[]{:S(2)}, u32[]{:S(2)}) async-start(bf16[4,32,2176]{2,1,0:T(8,128)(2,1)} %shard_map.77), calls=%async_computation | async-start | bytes 1114112 | tf_op jit(solution)/shard_map/all_to_all | solution.py:52
  25.8 91.6 %all-gather.3.cloned.1.call-start = ((), (), s32[]{:S(2)}) async-start(), calls=%async_computation.7 | async-start | bytes 2621440 | tf_op jit(solution)/shard_map/all_gather | solution.py:249
  25.9 10.5 %collective-permute-start = (bf16[32,2048]{1,0:T(8,128)(2,1)S(1)}, bf16[32,2048]{1,0:T(8,128)(2,1)S(1)}, u32[]{:S(2)}, u32[]{:S(2)}) collective-permute-start(bf16[32,2048]{1,0:T(8,128)(2,1)S(1)} %bitcast.18), channel_id=1, source_target_pairs={{16,0},{20,4},{24,8},{28,12},{32,16},{36,20},{40,24},{44,28},{48,3... | collective-permute-start | bytes 393224 | tf_op jit(solution)/shard_map/ppermute | solution.py:31
  30.5 7.5 %collective-permute-start.1 = (bf16[32,2048]{1,0:T(8,128)(2,1)S(1)}, bf16[32,2048]{1,0:T(8,128)(2,1)S(1)}, u32[]{:S(2)}, u32[]{:S(2)}) collective-permute-start(bf16[32,2048]{1,0:T(8,128)(2,1)S(1)} %bitcast.19), channel_id=1, source_target_pairs={{32,0},{36,4},{40,8},{44,12},{48,16},{52,20},{56,24},{60,28},{0,32... | collective-permute-start | bytes 393224 | tf_op jit(solution)/shard_map/ppermute | solution.py:31
  32.8 8.7 %collective-permute-start.2 = (bf16[32,2048]{1,0:T(8,128)(2,1)S(1)}, bf16[32,2048]{1,0:T(8,128)(2,1)S(1)}, u32[]{:S(2)}, u32[]{:S(2)}) collective-permute-start(bf16[32,2048]{1,0:T(8,128)(2,1)S(1)} %bitcast.20), channel_id=1, source_target_pairs={{48,0},{52,4},{56,8},{60,12},{0,16},{4,20},{8,24},{12,28},{16,32},... | collective-permute-start | bytes 393224 | tf_op jit(solution)/shard_map/ppermute | solution.py:31
  52.9 93.2 %reduce-scatter.2.cloned.1.call-start = ((), (), s32[]{:S(2)}) async-start(), calls=%async_computation.6 | async-start | bytes 2621440 | tf_op jit(solution)/shard_map/reduce_scatter | solution.py:284
  53.8 24.7 %copy-start = (bf16[2,256,512]{2,1,0:T(8,128)(2,1)S(1)}, bf16[2,256,512]{2,1,0:T(8,128)(2,1)}, u32[]{:S(2)}) copy-start(bf16[2,256,512]{2,1,0:T(8,128)(2,1)} %reverse_select_fusion.saved) | copy-start | bytes 1572868
  53.8 24.7 %copy-start.2 = (bf16[1,512,2048]{2,1,0:T(8,128)(2,1)S(1)}, bf16[1,512,2048]{2,1,0:T(8,128)(2,1)}, u32[]{:S(2)}) copy-start(bf16[1,512,2048]{2,1,0:T(8,128)(2,1)} %param.9) | copy-start | bytes 6291460
  53.8 24.7 %copy-start.5 = (bf16[1,512]{1,0:T(2,128)(2,1)S(1)}, bf16[1,512]{1,0:T(2,128)(2,1)}, u32[]{:S(2)}) copy-start(bf16[1,512]{1,0:T(2,128)(2,1)} %gains.3) | copy-start | bytes 3076
  84.5 21.8 %collective-permute-start.3 = (bf16[512,512]{1,0:T(8,128)(2,1)S(1)}, bf16[512,512]{1,0:T(8,128)(2,1)S(1)}, u32[]{:S(2)}, u32[]{:S(2)}) collective-permute-start(bf16[512,512]{1,0:T(8,128)(2,1)S(1)} %get-tuple-element.30), channel_id=1, source_target_pairs={{0,64},{64,0},{128,192},{192,128},{256,320},{320,256},{384,448},{4... | collective-permute-start | bytes 1572872 | tf_op jit(solution)/shard_map/ppermute | solution.py:40
  106.3 38.2 %copy-start.4 = (bf16[2,256,512]{2,1,0:T(8,128)(2,1)S(1)}, bf16[2,256,512]{2,1,0:T(8,128)(2,1)}, u32[]{:S(2)}) copy-start(bf16[2,256,512]{2,1,0:T(8,128)(2,1)} %top.1) | copy-start | bytes 1572868
  106.9 22.1 %collective-permute-start.4 = (bf16[256,512]{1,0:T(8,128)(2,1)S(1)}, bf16[256,512]{1,0:T(8,128)(2,1)S(1)}, u32[]{:S(2)}, u32[]{:S(2)}) collective-permute-start(bf16[256,512]{1,0:T(8,128)(2,1)S(1)} %shard_map.81), channel_id=1, source_target_pairs={{128,0},{192,64},{256,128},{320,192},{384,256},{448,320},{129,1},{... | collective-permute-start | bytes 786440 | tf_op jit(solution)/shard_map/ppermute | solution.py:44
  108.2 27.9 %collective-permute-start.5 = (bf16[256,512]{1,0:T(8,128)(2,1)S(1)}, bf16[256,512]{1,0:T(8,128)(2,1)S(1)}, u32[]{:S(2)}, u32[]{:S(2)}) collective-permute-start(bf16[256,512]{1,0:T(8,128)(2,1)S(1)} %shard_map.81), channel_id=1, source_target_pairs={{256,0},{320,64},{384,128},{448,192},{257,1},{321,65},{385,129},{4... | collective-permute-start | bytes 786440 | tf_op jit(solution)/shard_map/ppermute | solution.py:44
  109.5 26.6 %collective-permute-start.6 = (bf16[256,512]{1,0:T(8,128)(2,1)S(1)}, bf16[256,512]{1,0:T(8,128)(2,1)S(1)}, u32[]{:S(2)}, u32[]{:S(2)}) collective-permute-start(bf16[256,512]{1,0:T(8,128)(2,1)S(1)} %shard_map.81), channel_id=1, source_target_pairs={{384,0},{448,64},{385,1},{449,65},{386,2},{450,66},{387,3},{451,67... | collective-permute-start | bytes 786440 | tf_op jit(solution)/shard_map/ppermute | solution.py:44
  118.0 19.6 %all-to-all-start.4 = ((f32[8,4,128]{2,1,0:T(4,128)}), f32[8,4,128]{2,1,0:T(4,128)S(1)}, u32[]{:S(2)}, u32[]{:S(2)}) async-start(f32[8,4,128]{2,1,0:T(4,128)} %shard_map.80), calls=%async_computation.4 | async-start | bytes 32768 | tf_op jit(solution)/shard_map/all_to_all | solution.py:292
  137.6 1.6 %copy-start.1 = (bf16[8,256,512]{2,1,0:T(8,128)(2,1)S(1)}, bf16[8,256,512]{2,1,0:T(8,128)(2,1)}, u32[]{:S(2)}) copy-start(bf16[8,256,512]{2,1,0:T(8,128)(2,1)} %all-gather.3.cloned.1.call-done) | copy-start | bytes 6291460
  140.6 3.9 %collective-permute-start.7 = (bf16[2,256,512]{2,1,0:T(8,128)(2,1)S(1)}, bf16[2,256,512]{2,1,0:T(8,128)(2,1)S(1)}, u32[]{:S(2)}, u32[]{:S(2)}) collective-permute-start(bf16[2,256,512]{2,1,0:T(8,128)(2,1)S(1)} %get-tuple-element.39), channel_id=1, source_target_pairs={{0,64},{64,0},{128,192},{192,128},{256,320},{320,256},{384,448},{4... | collective-permute-start | bytes 1572872 | tf_op jit(solution)/shard_map/ppermute | solution.py:40
Sparse Core Ops, SparseCore 0:
  53.1 54.9 all-gather.2
Sparse Core Ops, SparseCore 1:
  84.5 35.6 reduce-scatter.1

commit v9 on v8

--- a/solution.py
+++ b/solution.py
@@ -50,6 +50,15 @@
 
 def z_exchange(spread):
     return lax.all_to_all(spread, "tensor", 0, 0, axis_index_groups=z_groups())
+
+
+def section_y_exchange(spread):
+    groups = [
+        [s * BLOCKS + y * NZ + z for s in range(core, NS, 2) for y in range(NY)]
+        for core in range(2)
+        for z in range(NZ)
+    ]
+    return lax.all_to_all(spread, ("section", "tensor"), 0, 0, axis_index_groups=groups)
 
 
 def call(body, out_shape, specs, args, scratch=(), cost=None, limit=14):
@@ -143,7 +152,8 @@
         here = gained * columns(inverse, width)
         direct[chunk * LANES : (chunk + 1) * LANES] = here
         direct16[chunk * LANES : (chunk + 1) * LANES] = here.astype(BF16)
-        total = row_sums(gained * hidden)
+        mean = squares[chunk : chunk + 1] / model_width + EPSILON
+        total = row_sums(gained * hidden) / (model_width * (mean * jnp.sqrt(mean)))
         for y in range(NY):
             aligned[y, chunk : chunk + 1] = total
 
@@ -181,15 +191,7 @@
         out_ref[x] = (product / (MICRO * NX)).astype(BF16)
 
 
-def scale_body(parts, squares, out_ref, *, model_width):
-    mean = squares[...] / model_width + EPSILON
-    total = parts[0] + parts[1] + parts[2] + parts[3]
-    scale = total / (model_width * (mean * jnp.sqrt(mean)))
-    for section in range(NS):
-        out_ref[section] = scale
-
-
-def fix_body(place, saved, scales, above1, above2, above3, kept, sent):
+def fix_body(place, saved, parts, above1, above2, kept, sent):
     section, core = place[3], place[2]
     chips = NS // 2
     chip = section // 2
@@ -200,14 +202,15 @@
             line = (m * HALF + first) // LANES
             scale = []
             for d in range(chips):
-                at = jnp.minimum(section + 2 * d, NS - 1)
+                at = jnp.minimum(chip + d, chips - 1)
                 live = jnp.where(chip + d < chips, 1.0, 0.0)
-                scale.append(scales[at, line : line + 1] * live)
+                total = sum(parts[at * NY + y, line : line + 1] for y in range(NY))
+                scale.append(total * live)
             scale = jnp.transpose(jnp.concatenate(scale + scale))
             for row in range(0, LANES, step):
                 at = slice(first + row, first + row + step)
                 here = slice(row, row + step)
-                above = above1[at].astype(F32) + above2[at].astype(F32) + above3[at].astype(F32)
+                above = above1[at].astype(F32) + above2[at].astype(F32)
                 value = jnp.where(core == m, above, 0.0)
                 for d in range(1, chips):
                     value = value - saved[chip_at[d], m, at].astype(F32) * scale[here, d : d + 1]
@@ -266,11 +269,13 @@
     )
     other = from_other_core(direct16)
     aligned = jnp.sum(z_exchange(aligned), axis=0)
-    other, aligned = lax.optimization_barrier((other, aligned))
 
     chip = call(half_body, jax.ShapeDtypeStruct(half, BF16), [SMEM, VMEM, VMEM], (place, direct, other))
-    above = [from_chips_above(chip, d) for d in (1, 2, 3)]
-    parts = y_exchange(jnp.broadcast_to(aligned, (NY,) + aligned.shape))
+    above1 = from_chips_above(chip, 1)
+    chip, above1, aligned = lax.optimization_barrier((chip, above1, aligned))
+    pair = (chip.astype(F32) + above1.astype(F32)).astype(BF16)
+    above2 = from_chips_above(pair, 2)
+    parts = section_y_exchange(jnp.broadcast_to(aligned, (NS // 2 * NY,) + aligned.shape))
     parts, saved = lax.optimization_barrier((parts, saved))
 
     local = call(
@@ -283,19 +288,12 @@
     )
     weight_grads = lax.psum_scatter(local, "dp", scatter_dimension=0)[None]
 
-    scales = call(
-        functools.partial(scale_body, model_width=model_width),
-        jax.ShapeDtypeStruct((NS, lines, LANES), F32),
-        [VMEM, VMEM],
-        (parts, squares),
-    )
-    scales = lax.all_to_all(scales, "section", 0, 0)
     by_micro = (MICRO, tokens // MICRO, width)
     kept, sent = call(
         fix_body,
         (jax.ShapeDtypeStruct(by_micro, F32), jax.ShapeDtypeStruct(by_micro, BF16)),
-        [SMEM] + [VMEM] * 5,
-        (place, saved, scales, *above),
+        [SMEM] + [VMEM] * 4,
+        (place, saved, parts, above1, above2),
     )
     got = from_other_core(sent)
     input_grads = call(

time: 154 us -> 152 us (0.987)
  blocking collectives: 49 us -> 64.5 us
  starting transfers between devices: 46.5 us -> 35.2 us
  waiting for transfers between devices: 26.7 us -> 21 us
    all_to_all x0 -> x1, blocking collectives: none -> 21.9 us  [section_y_exchange(): lax.all_to_all(spread, ('section', 'tensor'), 0, 0, axis_index_groups=gro...]
    all_to_all x1 -> x0, starting transfers between devices: 11 us -> none  [shards(): scales = lax.all_to_all(scales, 'section', 0, 0)]
    all_to_all x2 -> x1, blocking collectives: 31.3 us -> 24.7 us  [y_exchange(): return lax.all_to_all(spread, 'tensor', 0, 0, axis_index_groups=y_groups())]
    ppermute x3 -> x2, waiting for transfers between devices: 7.05 us -> 1.34 us  [from_chips_above(): lax.ppermute(value, 'section', [(s, s - 2 * chips) for s in range(2 * chi...]
    ppermute x3 -> x2, starting transfers between devices: 3.88 us -> 2.72 us  [from_chips_above(): lax.ppermute(value, 'section', [(s, s - 2 * chips) for s in range(2 * chi...]
    pallas_call x8 -> x7, Pallas kernels: 13.1 us -> 12.4 us  [call(): pl.pallas_call(body, out_shape=out_shape, in_specs=specs, out_specs=jax.t...]
  transfers between devices with their start and end apart: 12 -> 10, of which waited for: 6 -> 6; matrix products, arithmetic and copies ran while one was open for 1% -> 1% of each run, Pallas kernels for 7% -> 7%
where the time goes in v9:
time: 152 us; the launch traced here: 151 us
  blocking collectives  64.5 us (42%)
  starting transfers between devices  35.2 us (23%)
  waiting for transfers between devices  21 us (14%)
  between operations  15.7 us (10%)
  Pallas kernels  12.4 us (8%)
  local copies, waits for them, and re-layouts  1.64 us (1%)
    all_to_all x1, blocking collectives, y_exchange(): return lax.all_to_all(spread, 'tensor', 0, 0, axis_index_groups=y_groups())  24.7 us
    all_to_all x1, blocking collectives, section_y_exchange(): lax.all_to_all(spread, ('section', 'tensor'), 0, 0, axis_index_groups=gro...  21.9 us
    all_to_all x1, blocking collectives, z_exchange(): return lax.all_to_all(spread, 'tensor', 0, 0, axis_index_groups=z_groups())  17.9 us
    all_to_all x1, starting transfers between devices, z_exchange(): return lax.all_to_all(spread, 'tensor', 0, 0, axis_index_groups=z_groups())  15.6 us
    pallas_call x7, Pallas kernels, call(): pl.pallas_call(body, out_shape=out_shape, in_specs=specs, out_specs=jax.t...  12.4 us
    all_to_all x1, waiting for transfers between devices, z_exchange(): return lax.all_to_all(spread, 'tensor', 0, 0, axis_index_groups=z_groups())  11.4 us
    ppermute x3, starting transfers between devices, from_y(): return lax.ppermute(value, 'tensor', perm)  9.5 us
    ppermute x2, starting transfers between devices, from_other_core(): return lax.ppermute(value, 'section', [(s, s ^ 1) for s in range(NS)])  7.3 us
  transfers between devices with their start and end apart: 10, of which 6 were waited for; matrix products, arithmetic and copies ran while one was open for 1% of the time, Pallas kernels for 7%

profile of v9, /device:TPU:1, one launch (start us, length us, event | category | flops | bytes accessed | tf_op | source)
XLA Modules:
  0.0 151.5 jit_solution(13965868626601124291)
XLA Ops:
  8.0 0.0 copy-start.3
  8.0 0.0 copy-start.6
  8.0 0.0 copy-start.7
  8.0 2.2 %shard_map.77 = bf16[4,32,2176]{2,1,0:T(8,128)(2,1)} custom-call(s32[1,2]{1,0:T(1,128)} %plan.1, bf16[32,2048]{1,0:T(8,128)(2,1)} %bitcast.17, bf16[2,256,512]{2,1,0:T(8,128)(2,1)} %bitcast.23), custom_call_target="tpu_custom_call" | custom-call | tf_op jit(solution)/shard_map/pallas_call | solution.py:65
  10.2 15.6 %all-to-all-start = ((bf16[4,32,2176]{2,1,0:T(8,128)(2,1)}), bf16[4,32,2176]{2,1,0:T(8,128)(2,1)S(1)}, u32[]{:S(2)}, u32[]{:S(2)}) async-start(bf16[4,32,2176]{2,1,0:T(8,128)(2,1)} %shard_map.77), calls=%async_computation | async-start | bytes 1114112 | tf_op jit(solution)/shard_map/all_to_all | solution.py:52
  25.8 0.0 all-gather.3.cloned.1.call-start
  25.8 0.0 copy-done.3
  25.8 4.6 %collective-permute-start = (bf16[32,2048]{1,0:T(8,128)(2,1)S(1)}, bf16[32,2048]{1,0:T(8,128)(2,1)S(1)}, u32[]{:S(2)}, u32[]{:S(2)}) collective-permute-start(bf16[32,2048]{1,0:T(8,128)(2,1)S(1)} %bitcast.18), channel_id=1, source_target_pairs={{16,0},{20,4},{24,8},{28,12},{32,16},{36,20},{40,24},{44,28},{48,3... | collective-permute-start | bytes 393224 | tf_op jit(solution)/shard_map/ppermute | solution.py:31
  30.5 2.3 %collective-permute-start.1 = (bf16[32,2048]{1,0:T(8,128)(2,1)S(1)}, bf16[32,2048]{1,0:T(8,128)(2,1)S(1)}, u32[]{:S(2)}, u32[]{:S(2)}) collective-permute-start(bf16[32,2048]{1,0:T(8,128)(2,1)S(1)} %bitcast.19), channel_id=1, source_target_pairs={{32,0},{36,4},{40,8},{44,12},{48,16},{52,20},{56,24},{60,28},{0,32... | collective-permute-start | bytes 393224 | tf_op jit(solution)/shard_map/ppermute | solution.py:31
  32.8 2.6 %collective-permute-start.2 = (bf16[32,2048]{1,0:T(8,128)(2,1)S(1)}, bf16[32,2048]{1,0:T(8,128)(2,1)S(1)}, u32[]{:S(2)}, u32[]{:S(2)}) collective-permute-start(bf16[32,2048]{1,0:T(8,128)(2,1)S(1)} %bitcast.20), channel_id=1, source_target_pairs={{48,0},{52,4},{56,8},{60,12},{0,16},{4,20},{8,24},{12,28},{16,32},... | collective-permute-start | bytes 393224 | tf_op jit(solution)/shard_map/ppermute | solution.py:31
  35.4 0.0 copy-done.7
  35.4 0.0 copy-done.6
  35.4 0.9 reverse_select_fusion.saved
  36.3 0.0 collective-permute-done.own1
  36.3 1.7 %collective-permute-done.1.own2 = bf16[32,2048]{1,0:T(8,128)(2,1)S(1)} collective-permute-done((bf16[32,2048]{1,0:T(8,128)(2,1)S(1)}, bf16[32,2048]{1,0:T(8,128)(2,1)S(1)}, u32[]{:S(2)}, u32[]{:S(2)}) %collective-permute-start.1) | collective-permute-done | bytes 131104 | tf_op jit(solution)/shard_map/ppermute | solution.py:31
  38.0 3.5 %collective-permute-done.2.own3 = bf16[32,2048]{1,0:T(8,128)(2,1)S(1)} collective-permute-done((bf16[32,2048]{1,0:T(8,128)(2,1)S(1)}, bf16[32,2048]{1,0:T(8,128)(2,1)S(1)}, u32[]{:S(2)}, u32[]{:S(2)}) %collective-permute-start.2) | collective-permute-done | bytes 131104 | tf_op jit(solution)/shard_map/ppermute | solution.py:31
  41.5 11.4 %all-to-all-done.kv_ref = bf16[4,32,2176]{2,1,0:T(8,128)(2,1)S(1)} async-done(((bf16[4,32,2176]{2,1,0:T(8,128)(2,1)}), bf16[4,32,2176]{2,1,0:T(8,128)(2,1)S(1)}, u32[]{:S(2)}, u32[]{:S(2)}) %all-to-all-start) | async-done | bytes 557088 | tf_op jit(solution)/shard_map/all_to_all | solution.py:52
  52.9 0.0 all-gather.3.cloned.1.call-update
  52.9 0.0 reduce-scatter.2.cloned.1.call-start
  53.0 0.1 pad_add_fusion.place
  53.1 0.7 shard_map.78
  53.8 0.0 copy-start
  53.8 0.0 copy-start.1
  53.8 0.0 copy-start.5
  53.8 24.7 %all_to_all.20.others = bf16[4,96,2176]{2,1,0:T(8,128)(2,1)S(1)} all-to-all(bf16[4,96,2176]{2,1,0:T(8,128)(2,1)S(1)} %shard_map.78), channel_id=1, replica_groups={{0,16,32,48},{4,20,36,52},{8,24,40,56},{12,28,44,60},{1,17,33,49},{5,21..., dimensions={0} | all-to-all | bytes 3342336 | tf_op jit(solution)/shard_map/all_to_all | solution.py:48
  78.5 0.0 copy-done
  78.5 0.0 copy-done.1
  78.5 0.0 copy-done.5
  78.5 2.6 %shard_map.79 = (f32[512,512]{1,0:T(8,128)S(1)}, bf16[512,512]{1,0:T(8,128)(2,1)S(1)}, f32[4,4,128]{2,1,0:T(4,128)S(1)}, f32[4,128]{1,0:T(4,128)S(1)}) custom-call(s32[4]{0:T(128)S(1)} %pad_add_fusion.place, bf16[32,2048]{1,0:T(8,128)(2,1)S(1)} %bitcast.21, bf16[32,2048]{1,0:T(8,128)(2,1)S(1)} %collective-permute-done.own1, ...), custom_call_target="tpu_custom_call" | custom-call | flops 1073741824 | bytes 6291456 | tf_op jit(solution)/shard_map/pallas_call | solution.py:65
  81.1 3.4 %shard_map.83 = bf16[4,512,512]{2,1,0:T(8,128)(2,1)} custom-call(s32[4]{0:T(128)S(1)} %pad_add_fusion.place, bf16[32,2048]{1,0:T(8,128)(2,1)S(1)} %bitcast.22, bf16[32,2048]{1,0:T(8,128)(2,1)S(1)} %collective-permute-done.own1, bf16[32,2048]{1,0:T(8,128)(2,1)S(1)} %collective-permute-done.1.own2, bf16[32,2048]{1,0:T(8,128)(2,1)S(1)} %collective-permute-done.2.own3, ...), custom_call_target="tpu_custom_call" | custom-call | flops 1073741824 | bytes 6291456 | tf_op jit(solution)/shard_map/pallas_call | solution.py:65
  84.5 0.0 reduce-scatter.2.cloned.1.call-update
  84.5 4.1 %collective-permute-start.3 = (bf16[512,512]{1,0:T(8,128)(2,1)S(1)}, bf16[512,512]{1,0:T(8,128)(2,1)S(1)}, u32[]{:S(2)}, u32[]{:S(2)}) collective-permute-start(bf16[512,512]{1,0:T(8,128)(2,1)S(1)} %get-tuple-element.32), channel_id=1, source_target_pairs={{0,64},{64,0},{128,192},{192,128},{256,320},{320,256},{384,448},{4... | collective-permute-start | bytes 1572872 | tf_op jit(solution)/shard_map/ppermute | solution.py:40
  88.6 1.5 collective-permute-done.3.other
  90.1 0.6 shard_map.80
  90.7 0.0 copy-start.4
  90.7 1.4 collective-permute-start.4
  92.1 17.9 %all_to_all.21 = f32[4,4,128]{2,1,0:T(4,128)S(1)} all-to-all(f32[4,4,128]{2,1,0:T(4,128)S(1)} %get-tuple-element.33), channel_id=1, replica_groups={{0,4,8,12},{16,20,24,28},{32,36,40,44},{48,52,56,60},{1,5,9,13},{17,21,..., dimensions={0} | all-to-all | bytes 16384 | tf_op jit(solution)/shard_map/all_to_all | solution.py:52
  110.0 1.3 collective-permute-done.4.above1
  111.4 0.1 add_convert_fusion
  111.4 1.3 collective-permute-start.5
  112.8 21.9 %all_to_all.22.parts = f32[16,4,128]{2,1,0:T(4,128)S(1)} all-to-all(f32[16,4,128]{2,1,0:T(4,128)S(1)} %broadcast_in_dim.6), channel_id=1, replica_groups={{0,16,32,48,128,144,160,176,256,272,288,304,384,400,416,432},{4,20,36,5..., dimensions={0} | all-to-all | bytes 65536 | tf_op jit(solution)/shard_map/all_to_all | solution.py:61
  134.7 0.0 collective-permute-done.5.above2
  134.7 1.6 %copy-done.2 = bf16[8,256,512]{2,1,0:T(8,128)(2,1)S(1)} copy-done((bf16[8,256,512]{2,1,0:T(8,128)(2,1)S(1)}, bf16[8,256,512]{2,1,0:T(8,128)(2,1)}, u32[]{:S(2)}) %copy-start.2) | copy-done | bytes 2097176
  136.3 1.3 shard_map.81
  137.7 3.2 %collective-permute-start.6 = (bf16[2,256,512]{2,1,0:T(8,128)(2,1)S(1)}, bf16[2,256,512]{2,1,0:T(8,128)(2,1)S(1)}, u32[]{:S(2)}, u32[]{:S(2)}) collective-permute-start(bf16[2,256,512]{2,1,0:T(8,128)(2,1)S(1)} %get-tuple-element.40), channel_id=1, source_target_pairs={{0,64},{64,0},{128,192},{192,128},{256,320},{320,256},{384,448},{4... | collective-permute-start | bytes 1572872 | tf_op jit(solution)/shard_map/ppermute | solution.py:40
  140.9 1.5 collective-permute-done.6.got
  142.4 0.0 copy-done.4
  142.4 1.6 %shard_map.82 = bf16[2,256,512]{2,1,0:T(8,128)(2,1)} custom-call(s32[4]{0:T(128)S(1)} %pad_add_fusion.place, f32[2,256,512]{2,1,0:T(8,128)S(1)} %get-tuple-element.39.kept, bf16[2,256,512]{2,1,0:T(8,128)(2,1)S(1)} %collective-permute-done.6.got, f32[2,256,512]{2,1,0:T(8,128)S(1)} %bitcast.13, bf16[2,256,512]{2,1,0:T(8,128)(2,1)S(1)} %bitcast.16, ...), custom_call_target="tpu_custom_call" | custom-call | tf_op jit(solution)/shard_map/pallas_call | solution.py:65
  (5 shorter events, 0.0 us)
Async XLA Ops:
  8.0 17.9 %copy-start.3 = (bf16[1,2,16,2048]{3,2,1,0:T(8,128)(2,1)S(1)}, bf16[1,2,16,2048]{3,2,1,0:T(8,128)(2,1)}, u32[]{:S(2)}) copy-start(bf16[1,2,16,2048]{3,2,1,0:T(8,128)(2,1)} %param.10) | copy-start | bytes 393220
  8.0 27.4 %copy-start.6 = (bf16[1,2,256,512]{3,2,1,0:T(8,128)(2,1)S(1)}, bf16[1,2,256,512]{3,2,1,0:T(8,128)(2,1)}, u32[]{:S(2)}) copy-start(bf16[1,2,256,512]{3,2,1,0:T(8,128)(2,1)} %param.7) | copy-start | bytes 1572868
  8.0 27.4 %copy-start.7 = (s32[1,2]{1,0:T(1,128)S(1)}, s32[1,2]{1,0:T(1,128)}, u32[]{:S(2)}) copy-start(s32[1,2]{1,0:T(1,128)} %plan.1) | copy-start | bytes 28
  10.2 42.7 %all-to-all-start = ((bf16[4,32,2176]{2,1,0:T(8,128)(2,1)}), bf16[4,32,2176]{2,1,0:T(8,128)(2,1)S(1)}, u32[]{:S(2)}, u32[]{:S(2)}) async-start(bf16[4,32,2176]{2,1,0:T(8,128)(2,1)} %shard_map.77), calls=%async_computation | async-start | bytes 1114112 | tf_op jit(solution)/shard_map/all_to_all | solution.py:52
  25.8 108.9 %all-gather.3.cloned.1.call-start = ((), (), s32[]{:S(2)}) async-start(), calls=%async_computation.6 | async-start | bytes 2621440 | tf_op jit(solution)/shard_map/all_gather | solution.py:252
  25.8 10.5 %collective-permute-start = (bf16[32,2048]{1,0:T(8,128)(2,1)S(1)}, bf16[32,2048]{1,0:T(8,128)(2,1)S(1)}, u32[]{:S(2)}, u32[]{:S(2)}) collective-permute-start(bf16[32,2048]{1,0:T(8,128)(2,1)S(1)} %bitcast.18), channel_id=1, source_target_pairs={{16,0},{20,4},{24,8},{28,12},{32,16},{36,20},{40,24},{44,28},{48,3... | collective-permute-start | bytes 393224 | tf_op jit(solution)/shard_map/ppermute | solution.py:31
  30.5 7.5 %collective-permute-start.1 = (bf16[32,2048]{1,0:T(8,128)(2,1)S(1)}, bf16[32,2048]{1,0:T(8,128)(2,1)S(1)}, u32[]{:S(2)}, u32[]{:S(2)}) collective-permute-start(bf16[32,2048]{1,0:T(8,128)(2,1)S(1)} %bitcast.19), channel_id=1, source_target_pairs={{32,0},{36,4},{40,8},{44,12},{48,16},{52,20},{56,24},{60,28},{0,32... | collective-permute-start | bytes 393224 | tf_op jit(solution)/shard_map/ppermute | solution.py:31
  32.8 8.7 %collective-permute-start.2 = (bf16[32,2048]{1,0:T(8,128)(2,1)S(1)}, bf16[32,2048]{1,0:T(8,128)(2,1)S(1)}, u32[]{:S(2)}, u32[]{:S(2)}) collective-permute-start(bf16[32,2048]{1,0:T(8,128)(2,1)S(1)} %bitcast.20), channel_id=1, source_target_pairs={{48,0},{52,4},{56,8},{60,12},{0,16},{4,20},{8,24},{12,28},{16,32},... | collective-permute-start | bytes 393224 | tf_op jit(solution)/shard_map/ppermute | solution.py:31
  52.9 91.1 %reduce-scatter.2.cloned.1.call-start = ((), (), s32[]{:S(2)}) async-start(), calls=%async_computation.5 | async-start | bytes 2621440 | tf_op jit(solution)/shard_map/reduce_scatter | solution.py:289
  53.8 24.7 %copy-start = (bf16[2,256,512]{2,1,0:T(8,128)(2,1)S(1)}, bf16[2,256,512]{2,1,0:T(8,128)(2,1)}, u32[]{:S(2)}) copy-start(bf16[2,256,512]{2,1,0:T(8,128)(2,1)} %reverse_select_fusion.saved) | copy-start | bytes 1572868
  53.8 24.7 %copy-start.1 = (bf16[1,512,2048]{2,1,0:T(8,128)(2,1)S(1)}, bf16[1,512,2048]{2,1,0:T(8,128)(2,1)}, u32[]{:S(2)}) copy-start(bf16[1,512,2048]{2,1,0:T(8,128)(2,1)} %param.9) | copy-start | bytes 6291460
  53.8 24.7 %copy-start.5 = (bf16[1,512]{1,0:T(2,128)(2,1)S(1)}, bf16[1,512]{1,0:T(2,128)(2,1)}, u32[]{:S(2)}) copy-start(bf16[1,512]{1,0:T(2,128)(2,1)} %gains.3) | copy-start | bytes 3076
  84.5 5.6 %collective-permute-start.3 = (bf16[512,512]{1,0:T(8,128)(2,1)S(1)}, bf16[512,512]{1,0:T(8,128)(2,1)S(1)}, u32[]{:S(2)}, u32[]{:S(2)}) collective-permute-start(bf16[512,512]{1,0:T(8,128)(2,1)S(1)} %get-tuple-element.32), channel_id=1, source_target_pairs={{0,64},{64,0},{128,192},{192,128},{256,320},{320,256},{384,448},{4... | collective-permute-start | bytes 1572872 | tf_op jit(solution)/shard_map/ppermute | solution.py:40
  90.7 51.7 %copy-start.4 = (bf16[2,256,512]{2,1,0:T(8,128)(2,1)S(1)}, bf16[2,256,512]{2,1,0:T(8,128)(2,1)}, u32[]{:S(2)}) copy-start(bf16[2,256,512]{2,1,0:T(8,128)(2,1)} %top.1) | copy-start | bytes 1572868
  90.7 20.7 %collective-permute-start.4 = (bf16[256,512]{1,0:T(8,128)(2,1)S(1)}, bf16[256,512]{1,0:T(8,128)(2,1)S(1)}, u32[]{:S(2)}, u32[]{:S(2)}) collective-permute-start(bf16[256,512]{1,0:T(8,128)(2,1)S(1)} %shard_map.80), channel_id=1, source_target_pairs={{128,0},{192,64},{256,128},{320,192},{384,256},{448,320},{129,1},{... | collective-permute-start | bytes 786440 | tf_op jit(solution)/shard_map/ppermute | solution.py:44
  111.4 23.3 %collective-permute-start.5 = (bf16[256,512]{1,0:T(8,128)(2,1)S(1)}, bf16[256,512]{1,0:T(8,128)(2,1)S(1)}, u32[]{:S(2)}, u32[]{:S(2)}) collective-permute-start(bf16[256,512]{1,0:T(8,128)(2,1)S(1)} %add_convert_fusion), channel_id=1, source_target_pairs={{256,0},{320,64},{384,128},{448,192},{257,1},{321,65},{385,129},{4... | collective-permute-start | bytes 786440 | tf_op jit(solution)/shard_map/ppermute | solution.py:44
  134.7 1.6 %copy-start.2 = (bf16[8,256,512]{2,1,0:T(8,128)(2,1)S(1)}, bf16[8,256,512]{2,1,0:T(8,128)(2,1)}, u32[]{:S(2)}) copy-start(bf16[8,256,512]{2,1,0:T(8,128)(2,1)} %all-gather.3.cloned.1.call-done) | copy-start | bytes 6291460
  137.7 4.8 %collective-permute-start.6 = (bf16[2,256,512]{2,1,0:T(8,128)(2,1)S(1)}, bf16[2,256,512]{2,1,0:T(8,128)(2,1)S(1)}, u32[]{:S(2)}, u32[]{:S(2)}) collective-permute-start(bf16[2,256,512]{2,1,0:T(8,128)(2,1)S(1)} %get-tuple-element.40), channel_id=1, source_target_pairs={{0,64},{64,0},{128,192},{192,128},{256,320},{320,256},{384,448},{4... | collective-permute-start | bytes 1572872 | tf_op jit(solution)/shard_map/ppermute | solution.py:40
Sparse Core Ops, SparseCore 0:
  53.1 60.3 all-gather.2
Sparse Core Ops, SparseCore 1:
  84.6 35.6 reduce-scatter.1

commit v10 on v9

--- a/solution.py
+++ b/solution.py
@@ -275,8 +275,8 @@
     chip, above1, aligned = lax.optimization_barrier((chip, above1, aligned))
     pair = (chip.astype(F32) + above1.astype(F32)).astype(BF16)
     above2 = from_chips_above(pair, 2)
+    aligned, saved = lax.optimization_barrier((aligned, saved))
     parts = section_y_exchange(jnp.broadcast_to(aligned, (NS // 2 * NY,) + aligned.shape))
-    parts, saved = lax.optimization_barrier((parts, saved))
 
     local = call(
         outer_body,

time: 152 us -> 152 us (level)
  blocking collectives: 64.5 us -> 42.6 us
  starting transfers between devices: 35.2 us -> 46.1 us
  waiting for transfers between devices: 21 us -> 31.4 us
    all_to_all x1 -> x0, blocking collectives: 21.9 us -> none  [section_y_exchange(): lax.all_to_all(spread, ('section', 'tensor'), 0, 0, axis_index_groups=gro...]
    all_to_all x0 -> x1, starting transfers between devices: none -> 10.9 us  [section_y_exchange(): lax.all_to_all(spread, ('section', 'tensor'), 0, 0, axis_index_groups=gro...]
    ppermute x2, waiting for transfers between devices: 1.34 us -> 7.84 us  [from_chips_above(): lax.ppermute(value, 'section', [(s, s - 2 * chips) for s in range(2 * chi...]
    all_to_all x0 -> x1, waiting for transfers between devices: none -> 3.21 us  [section_y_exchange(): lax.all_to_all(spread, ('section', 'tensor'), 0, 0, axis_index_groups=gro...]
  transfers between devices with their start and end apart: 10 -> 11, of which waited for: 6 -> 9; matrix products, arithmetic and copies ran while one was open for 1% -> 1% of each run, Pallas kernels for 7% -> 7%
where the time goes in v10:
time: 152 us; the launch traced here: 151 us
  starting transfers between devices  46.1 us (30%)
  blocking collectives  42.6 us (28%)
  waiting for transfers between devices  31.4 us (21%)
  between operations  15.7 us (10%)
  Pallas kernels  12.4 us (8%)
  local copies, waits for them, and re-layouts  2.25 us (1%)
    all_to_all x1, blocking collectives, y_exchange(): return lax.all_to_all(spread, 'tensor', 0, 0, axis_index_groups=y_groups())  24.7 us
    all_to_all x1, blocking collectives, z_exchange(): return lax.all_to_all(spread, 'tensor', 0, 0, axis_index_groups=z_groups())  17.9 us
    all_to_all x1, starting transfers between devices, z_exchange(): return lax.all_to_all(spread, 'tensor', 0, 0, axis_index_groups=z_groups())  15.6 us
    pallas_call x7, Pallas kernels, call(): pl.pallas_call(body, out_shape=out_shape, in_specs=specs, out_specs=jax.t...  12.4 us
    all_to_all x1, waiting for transfers between devices, z_exchange(): return lax.all_to_all(spread, 'tensor', 0, 0, axis_index_groups=z_groups())  11.4 us
    all_to_all x1, starting transfers between devices, section_y_exchange(): lax.all_to_all(spread, ('section', 'tensor'), 0, 0, axis_index_groups=gro...  10.9 us
    ppermute x3, starting transfers between devices, from_y(): return lax.ppermute(value, 'tensor', perm)  9.5 us
    ppermute x2, waiting for transfers between devices, from_chips_above(): lax.ppermute(value, 'section', [(s, s - 2 * chips) for s in range(2 * chi...  7.84 us
  transfers between devices with their start and end apart: 11, of which 9 were waited for; matrix products, arithmetic and copies ran while one was open for 1% of the time, Pallas kernels for 7%

profile of v10, /device:TPU:1, one launch (start us, length us, event | category | flops | bytes accessed | tf_op | source)
XLA Modules:
  0.0 151.5 jit_solution(11701522418215057175)
XLA Ops:
  8.0 0.0 copy-start.3
  8.0 0.0 copy-start.6
  8.0 0.0 copy-start.7
  8.0 2.2 %shard_map.77 = bf16[4,32,2176]{2,1,0:T(8,128)(2,1)} custom-call(s32[1,2]{1,0:T(1,128)} %plan.1, bf16[32,2048]{1,0:T(8,128)(2,1)} %bitcast.17, bf16[2,256,512]{2,1,0:T(8,128)(2,1)} %bitcast.23), custom_call_target="tpu_custom_call" | custom-call | tf_op jit(solution)/shard_map/pallas_call | solution.py:65
  10.2 15.6 %all-to-all-start = ((bf16[4,32,2176]{2,1,0:T(8,128)(2,1)}), bf16[4,32,2176]{2,1,0:T(8,128)(2,1)S(1)}, u32[]{:S(2)}, u32[]{:S(2)}) async-start(bf16[4,32,2176]{2,1,0:T(8,128)(2,1)} %shard_map.77), calls=%async_computation | async-start | bytes 1114112 | tf_op jit(solution)/shard_map/all_to_all | solution.py:52
  25.8 0.0 all-gather.3.cloned.1.call-start
  25.8 0.0 copy-done.3
  25.8 4.6 %collective-permute-start = (bf16[32,2048]{1,0:T(8,128)(2,1)S(1)}, bf16[32,2048]{1,0:T(8,128)(2,1)S(1)}, u32[]{:S(2)}, u32[]{:S(2)}) collective-permute-start(bf16[32,2048]{1,0:T(8,128)(2,1)S(1)} %bitcast.18), channel_id=1, source_target_pairs={{16,0},{20,4},{24,8},{28,12},{32,16},{36,20},{40,24},{44,28},{48,3... | collective-permute-start | bytes 393224 | tf_op jit(solution)/shard_map/ppermute | solution.py:31
  30.5 2.3 %collective-permute-start.1 = (bf16[32,2048]{1,0:T(8,128)(2,1)S(1)}, bf16[32,2048]{1,0:T(8,128)(2,1)S(1)}, u32[]{:S(2)}, u32[]{:S(2)}) collective-permute-start(bf16[32,2048]{1,0:T(8,128)(2,1)S(1)} %bitcast.19), channel_id=1, source_target_pairs={{32,0},{36,4},{40,8},{44,12},{48,16},{52,20},{56,24},{60,28},{0,32... | collective-permute-start | bytes 393224 | tf_op jit(solution)/shard_map/ppermute | solution.py:31
  32.8 2.6 %collective-permute-start.2 = (bf16[32,2048]{1,0:T(8,128)(2,1)S(1)}, bf16[32,2048]{1,0:T(8,128)(2,1)S(1)}, u32[]{:S(2)}, u32[]{:S(2)}) collective-permute-start(bf16[32,2048]{1,0:T(8,128)(2,1)S(1)} %bitcast.20), channel_id=1, source_target_pairs={{48,0},{52,4},{56,8},{60,12},{0,16},{4,20},{8,24},{12,28},{16,32},... | collective-permute-start | bytes 393224 | tf_op jit(solution)/shard_map/ppermute | solution.py:31
  35.4 0.0 copy-done.7
  35.4 0.0 copy-done.6
  35.4 0.9 reverse_select_fusion.saved
  36.3 0.0 collective-permute-done.own1
  36.3 1.7 %collective-permute-done.1.own2 = bf16[32,2048]{1,0:T(8,128)(2,1)S(1)} collective-permute-done((bf16[32,2048]{1,0:T(8,128)(2,1)S(1)}, bf16[32,2048]{1,0:T(8,128)(2,1)S(1)}, u32[]{:S(2)}, u32[]{:S(2)}) %collective-permute-start.1) | collective-permute-done | bytes 131104 | tf_op jit(solution)/shard_map/ppermute | solution.py:31
  38.0 3.5 %collective-permute-done.2.own3 = bf16[32,2048]{1,0:T(8,128)(2,1)S(1)} collective-permute-done((bf16[32,2048]{1,0:T(8,128)(2,1)S(1)}, bf16[32,2048]{1,0:T(8,128)(2,1)S(1)}, u32[]{:S(2)}, u32[]{:S(2)}) %collective-permute-start.2) | collective-permute-done | bytes 131104 | tf_op jit(solution)/shard_map/ppermute | solution.py:31
  41.5 11.4 %all-to-all-done.kv_ref = bf16[4,32,2176]{2,1,0:T(8,128)(2,1)S(1)} async-done(((bf16[4,32,2176]{2,1,0:T(8,128)(2,1)}), bf16[4,32,2176]{2,1,0:T(8,128)(2,1)S(1)}, u32[]{:S(2)}, u32[]{:S(2)}) %all-to-all-start) | async-done | bytes 557088 | tf_op jit(solution)/shard_map/all_to_all | solution.py:52
  52.9 0.0 all-gather.3.cloned.1.call-update
  52.9 0.0 reduce-scatter.2.cloned.1.call-start
  53.0 0.1 pad_add_fusion.place
  53.1 0.7 shard_map.78
  53.8 0.0 copy-start
  53.8 0.0 copy-start.1
  53.8 0.0 copy-start.5
  53.8 24.7 %all_to_all.20.others = bf16[4,96,2176]{2,1,0:T(8,128)(2,1)S(1)} all-to-all(bf16[4,96,2176]{2,1,0:T(8,128)(2,1)S(1)} %shard_map.78), channel_id=1, replica_groups={{0,16,32,48},{4,20,36,52},{8,24,40,56},{12,28,44,60},{1,17,33,49},{5,21..., dimensions={0} | all-to-all | bytes 3342336 | tf_op jit(solution)/shard_map/all_to_all | solution.py:48
  78.5 2.6 %shard_map.79 = (f32[512,512]{1,0:T(8,128)S(1)}, bf16[512,512]{1,0:T(8,128)(2,1)S(1)}, f32[4,4,128]{2,1,0:T(4,128)S(1)}, f32[4,128]{1,0:T(4,128)S(1)}) custom-call(s32[4]{0:T(128)S(1)} %pad_add_fusion.place, bf16[32,2048]{1,0:T(8,128)(2,1)S(1)} %bitcast.21, bf16[32,2048]{1,0:T(8,128)(2,1)S(1)} %collective-permute-done.own1, ...), custom_call_target="tpu_custom_call" | custom-call | flops 1073741824 | bytes 6291456 | tf_op jit(solution)/shard_map/pallas_call | solution.py:65
  81.1 3.4 %shard_map.83 = bf16[4,512,512]{2,1,0:T(8,128)(2,1)} custom-call(s32[4]{0:T(128)S(1)} %pad_add_fusion.place, bf16[32,2048]{1,0:T(8,128)(2,1)S(1)} %bitcast.22, bf16[32,2048]{1,0:T(8,128)(2,1)S(1)} %collective-permute-done.own1, bf16[32,2048]{1,0:T(8,128)(2,1)S(1)} %collective-permute-done.1.own2, bf16[32,2048]{1,0:T(8,128)(2,1)S(1)} %collective-permute-done.2.own3, ...), custom_call_target="tpu_custom_call" | custom-call | flops 1073741824 | bytes 6291456 | tf_op jit(solution)/shard_map/pallas_call | solution.py:65
  84.5 0.0 reduce-scatter.2.cloned.1.call-update
  84.5 4.1 %collective-permute-start.3 = (bf16[512,512]{1,0:T(8,128)(2,1)S(1)}, bf16[512,512]{1,0:T(8,128)(2,1)S(1)}, u32[]{:S(2)}, u32[]{:S(2)}) collective-permute-start(bf16[512,512]{1,0:T(8,128)(2,1)S(1)} %get-tuple-element.32), channel_id=1, source_target_pairs={{0,64},{64,0},{128,192},{192,128},{256,320},{320,256},{384,448},{4... | collective-permute-start | bytes 1572872 | tf_op jit(solution)/shard_map/ppermute | solution.py:40
  88.6 1.5 collective-permute-done.3.other
  90.1 0.6 shard_map.80
  90.7 0.0 copy-start.4
  90.7 1.4 collective-permute-start.4
  92.1 17.9 %all_to_all.21 = f32[4,4,128]{2,1,0:T(4,128)S(1)} all-to-all(f32[4,4,128]{2,1,0:T(4,128)S(1)} %get-tuple-element.33), channel_id=1, replica_groups={{0,4,8,12},{16,20,24,28},{32,36,40,44},{48,52,56,60},{1,5,9,13},{17,21,..., dimensions={0} | all-to-all | bytes 16384 | tf_op jit(solution)/shard_map/all_to_all | solution.py:52
  110.0 1.3 collective-permute-done.4.above1
  111.4 0.1 add_convert_fusion
  111.4 1.3 collective-permute-start.5
  112.7 0.7 all-gather.3.cloned.1.call-done
  113.4 0.6 broadcast_in_dim.6
  114.1 10.9 %all-to-all-start.3 = ((f32[16,4,128]{2,1,0:T(4,128)}), f32[16,4,128]{2,1,0:T(4,128)S(1)}, u32[]{:S(2)}, u32[]{:S(2)}) async-start(f32[16,4,128]{2,1,0:T(4,128)} %broadcast_in_dim.6), calls=%async_computation.3 | async-start | bytes 65536 | tf_op jit(solution)/shard_map/all_to_all | solution.py:61
  125.0 6.5 %collective-permute-done.5.above2 = bf16[256,512]{1,0:T(8,128)(2,1)S(1)} collective-permute-done((bf16[256,512]{1,0:T(8,128)(2,1)S(1)}, bf16[256,512]{1,0:T(8,128)(2,1)S(1)}, u32[]{:S(2)}, u32[]{:S(2)}) %collective-permute-start.5) | collective-permute-done | bytes 262176 | tf_op jit(solution)/shard_map/ppermute | solution.py:44
  131.5 3.2 %all-to-all-done.3.parts = f32[16,4,128]{2,1,0:T(4,128)S(1)} async-done(((f32[16,4,128]{2,1,0:T(4,128)}), f32[16,4,128]{2,1,0:T(4,128)S(1)}, u32[]{:S(2)}, u32[]{:S(2)}) %all-to-all-start.3) | async-done | bytes 32800 | tf_op jit(solution)/shard_map/all_to_all | solution.py:61
  134.7 1.6 %copy-done.2 = bf16[8,256,512]{2,1,0:T(8,128)(2,1)S(1)} copy-done((bf16[8,256,512]{2,1,0:T(8,128)(2,1)S(1)}, bf16[8,256,512]{2,1,0:T(8,128)(2,1)}, u32[]{:S(2)}) %copy-start.2) | copy-done | bytes 2097176
  136.3 1.3 shard_map.81
  137.6 3.2 %collective-permute-start.6 = (bf16[2,256,512]{2,1,0:T(8,128)(2,1)S(1)}, bf16[2,256,512]{2,1,0:T(8,128)(2,1)S(1)}, u32[]{:S(2)}, u32[]{:S(2)}) collective-permute-start(bf16[2,256,512]{2,1,0:T(8,128)(2,1)S(1)} %get-tuple-element.40), channel_id=1, source_target_pairs={{0,64},{64,0},{128,192},{192,128},{256,320},{320,256},{384,448},{4... | collective-permute-start | bytes 1572872 | tf_op jit(solution)/shard_map/ppermute | solution.py:40
  140.9 1.5 collective-permute-done.6.got
  142.4 0.0 copy-done.4
  142.4 1.6 %shard_map.82 = bf16[2,256,512]{2,1,0:T(8,128)(2,1)} custom-call(s32[4]{0:T(128)S(1)} %pad_add_fusion.place, f32[2,256,512]{2,1,0:T(8,128)S(1)} %get-tuple-element.39.kept, bf16[2,256,512]{2,1,0:T(8,128)(2,1)S(1)} %collective-permute-done.6.got, f32[2,256,512]{2,1,0:T(8,128)S(1)} %bitcast.13, bf16[2,256,512]{2,1,0:T(8,128)(2,1)S(1)} %bitcast.16, ...), custom_call_target="tpu_custom_call" | custom-call | tf_op jit(solution)/shard_map/pallas_call | solution.py:65
  (6 shorter events, 0.0 us)
Async XLA Ops:
  8.0 17.8 %copy-start.3 = (bf16[1,2,16,2048]{3,2,1,0:T(8,128)(2,1)S(1)}, bf16[1,2,16,2048]{3,2,1,0:T(8,128)(2,1)}, u32[]{:S(2)}) copy-start(bf16[1,2,16,2048]{3,2,1,0:T(8,128)(2,1)} %param.10) | copy-start | bytes 393220
  8.0 27.4 %copy-start.6 = (bf16[1,2,256,512]{3,2,1,0:T(8,128)(2,1)S(1)}, bf16[1,2,256,512]{3,2,1,0:T(8,128)(2,1)}, u32[]{:S(2)}) copy-start(bf16[1,2,256,512]{3,2,1,0:T(8,128)(2,1)} %param.7) | copy-start | bytes 1572868
  8.0 27.3 %copy-start.7 = (s32[1,2]{1,0:T(1,128)S(1)}, s32[1,2]{1,0:T(1,128)}, u32[]{:S(2)}) copy-start(s32[1,2]{1,0:T(1,128)} %plan.1) | copy-start | bytes 28
  10.2 42.7 %all-to-all-start = ((bf16[4,32,2176]{2,1,0:T(8,128)(2,1)}), bf16[4,32,2176]{2,1,0:T(8,128)(2,1)S(1)}, u32[]{:S(2)}, u32[]{:S(2)}) async-start(bf16[4,32,2176]{2,1,0:T(8,128)(2,1)} %shard_map.77), calls=%async_computation | async-start | bytes 1114112 | tf_op jit(solution)/shard_map/all_to_all | solution.py:52
  25.8 87.6 %all-gather.3.cloned.1.call-start = ((), (), s32[]{:S(2)}) async-start(), calls=%async_computation.6 | async-start | bytes 2621440 | tf_op jit(solution)/shard_map/all_gather | solution.py:252
  25.8 10.5 %collective-permute-start = (bf16[32,2048]{1,0:T(8,128)(2,1)S(1)}, bf16[32,2048]{1,0:T(8,128)(2,1)S(1)}, u32[]{:S(2)}, u32[]{:S(2)}) collective-permute-start(bf16[32,2048]{1,0:T(8,128)(2,1)S(1)} %bitcast.18), channel_id=1, source_target_pairs={{16,0},{20,4},{24,8},{28,12},{32,16},{36,20},{40,24},{44,28},{48,3... | collective-permute-start | bytes 393224 | tf_op jit(solution)/shard_map/ppermute | solution.py:31
  30.5 7.5 %collective-permute-start.1 = (bf16[32,2048]{1,0:T(8,128)(2,1)S(1)}, bf16[32,2048]{1,0:T(8,128)(2,1)S(1)}, u32[]{:S(2)}, u32[]{:S(2)}) collective-permute-start(bf16[32,2048]{1,0:T(8,128)(2,1)S(1)} %bitcast.19), channel_id=1, source_target_pairs={{32,0},{36,4},{40,8},{44,12},{48,16},{52,20},{56,24},{60,28},{0,32... | collective-permute-start | bytes 393224 | tf_op jit(solution)/shard_map/ppermute | solution.py:31
  32.8 8.7 %collective-permute-start.2 = (bf16[32,2048]{1,0:T(8,128)(2,1)S(1)}, bf16[32,2048]{1,0:T(8,128)(2,1)S(1)}, u32[]{:S(2)}, u32[]{:S(2)}) collective-permute-start(bf16[32,2048]{1,0:T(8,128)(2,1)S(1)} %bitcast.20), channel_id=1, source_target_pairs={{48,0},{52,4},{56,8},{60,12},{0,16},{4,20},{8,24},{12,28},{16,32},... | collective-permute-start | bytes 393224 | tf_op jit(solution)/shard_map/ppermute | solution.py:31
  52.9 91.1 %reduce-scatter.2.cloned.1.call-start = ((), (), s32[]{:S(2)}) async-start(), calls=%async_computation.5 | async-start | bytes 2621440 | tf_op jit(solution)/shard_map/reduce_scatter | solution.py:289
  53.8 24.7 %copy-start = (bf16[2,256,512]{2,1,0:T(8,128)(2,1)S(1)}, bf16[2,256,512]{2,1,0:T(8,128)(2,1)}, u32[]{:S(2)}) copy-start(bf16[2,256,512]{2,1,0:T(8,128)(2,1)} %reverse_select_fusion.saved) | copy-start | bytes 1572868
  53.8 24.7 %copy-start.1 = (bf16[1,512,2048]{2,1,0:T(8,128)(2,1)S(1)}, bf16[1,512,2048]{2,1,0:T(8,128)(2,1)}, u32[]{:S(2)}) copy-start(bf16[1,512,2048]{2,1,0:T(8,128)(2,1)} %param.9) | copy-start | bytes 6291460
  53.8 24.7 %copy-start.5 = (bf16[1,512]{1,0:T(2,128)(2,1)S(1)}, bf16[1,512]{1,0:T(2,128)(2,1)}, u32[]{:S(2)}) copy-start(bf16[1,512]{1,0:T(2,128)(2,1)} %gains.3) | copy-start | bytes 3076
  84.5 5.6 %collective-permute-start.3 = (bf16[512,512]{1,0:T(8,128)(2,1)S(1)}, bf16[512,512]{1,0:T(8,128)(2,1)S(1)}, u32[]{:S(2)}, u32[]{:S(2)}) collective-permute-start(bf16[512,512]{1,0:T(8,128)(2,1)S(1)} %get-tuple-element.32), channel_id=1, source_target_pairs={{0,64},{64,0},{128,192},{192,128},{256,320},{320,256},{384,448},{4... | collective-permute-start | bytes 1572872 | tf_op jit(solution)/shard_map/ppermute | solution.py:40
  90.7 51.7 %copy-start.4 = (bf16[2,256,512]{2,1,0:T(8,128)(2,1)S(1)}, bf16[2,256,512]{2,1,0:T(8,128)(2,1)}, u32[]{:S(2)}) copy-start(bf16[2,256,512]{2,1,0:T(8,128)(2,1)} %top.1) | copy-start | bytes 1572868
  90.7 20.7 %collective-permute-start.4 = (bf16[256,512]{1,0:T(8,128)(2,1)S(1)}, bf16[256,512]{1,0:T(8,128)(2,1)S(1)}, u32[]{:S(2)}, u32[]{:S(2)}) collective-permute-start(bf16[256,512]{1,0:T(8,128)(2,1)S(1)} %shard_map.80), channel_id=1, source_target_pairs={{128,0},{192,64},{256,128},{320,192},{384,256},{448,320},{129,1},{... | collective-permute-start | bytes 786440 | tf_op jit(solution)/shard_map/ppermute | solution.py:44
  111.4 20.0 %collective-permute-start.5 = (bf16[256,512]{1,0:T(8,128)(2,1)S(1)}, bf16[256,512]{1,0:T(8,128)(2,1)S(1)}, u32[]{:S(2)}, u32[]{:S(2)}) collective-permute-start(bf16[256,512]{1,0:T(8,128)(2,1)S(1)} %add_convert_fusion), channel_id=1, source_target_pairs={{256,0},{320,64},{384,128},{448,192},{257,1},{321,65},{385,129},{4... | collective-permute-start | bytes 786440 | tf_op jit(solution)/shard_map/ppermute | solution.py:44
  114.1 20.6 %all-to-all-start.3 = ((f32[16,4,128]{2,1,0:T(4,128)}), f32[16,4,128]{2,1,0:T(4,128)S(1)}, u32[]{:S(2)}, u32[]{:S(2)}) async-start(f32[16,4,128]{2,1,0:T(4,128)} %broadcast_in_dim.6), calls=%async_computation.3 | async-start | bytes 65536 | tf_op jit(solution)/shard_map/all_to_all | solution.py:61
  134.7 1.6 %copy-start.2 = (bf16[8,256,512]{2,1,0:T(8,128)(2,1)S(1)}, bf16[8,256,512]{2,1,0:T(8,128)(2,1)}, u32[]{:S(2)}) copy-start(bf16[8,256,512]{2,1,0:T(8,128)(2,1)} %all-gather.3.cloned.1.call-done) | copy-start | bytes 6291460
  137.6 4.8 %collective-permute-start.6 = (bf16[2,256,512]{2,1,0:T(8,128)(2,1)S(1)}, bf16[2,256,512]{2,1,0:T(8,128)(2,1)S(1)}, u32[]{:S(2)}, u32[]{:S(2)}) collective-permute-start(bf16[2,256,512]{2,1,0:T(8,128)(2,1)S(1)} %get-tuple-element.40), channel_id=1, source_target_pairs={{0,64},{64,0},{128,192},{192,128},{256,320},{320,256},{384,448},{4... | collective-permute-start | bytes 1572872 | tf_op jit(solution)/shard_map/ppermute | solution.py:40
Sparse Core Ops, SparseCore 0:
  53.1 60.3 all-gather.2
Sparse Core Ops, SparseCore 1:
  84.6 35.6 reduce-scatter.1

commit v11 on v10

--- a/solution.py
+++ b/solution.py
@@ -191,11 +191,16 @@
         out_ref[x] = (product / (MICRO * NX)).astype(BF16)
 
 
+def order_body(place, saved, out_ref):
+    chip, chips = place[3] // 2, saved.shape[0]
+    for d in range(chips):
+        out_ref[d] = saved[jnp.minimum(chip + d, chips - 1)]
+
+
 def fix_body(place, saved, parts, above1, above2, kept, sent):
     section, core = place[3], place[2]
     chips = NS // 2
     chip = section // 2
-    chip_at = [jnp.minimum(chip + d, chips - 1) for d in range(chips)]
     step = 2 * ROWS
     for m in range(MICRO):
         for first in range(0, HALF, LANES):
@@ -213,8 +218,8 @@
                 above = above1[at].astype(F32) + above2[at].astype(F32)
                 value = jnp.where(core == m, above, 0.0)
                 for d in range(1, chips):
-                    value = value - saved[chip_at[d], m, at].astype(F32) * scale[here, d : d + 1]
-                whole = value - saved[chip, m, at].astype(F32) * scale[here, :1]
+                    value = value - saved[d, m, at].astype(F32) * scale[here, d : d + 1]
+                whole = value - saved[0, m, at].astype(F32) * scale[here, :1]
                 kept[m, at] = whole
                 sent[m, at] = jnp.where(core == 1, whole, value).astype(BF16)
 
@@ -289,6 +294,7 @@
     weight_grads = lax.psum_scatter(local, "dp", scatter_dimension=0)[None]
 
     by_micro = (MICRO, tokens // MICRO, width)
+    saved = call(order_body, jax.ShapeDtypeStruct(saved.shape, BF16), [SMEM, VMEM], (place, saved))
     kept, sent = call(
         fix_body,
         (jax.ShapeDtypeStruct(by_micro, F32), jax.ShapeDtypeStruct(by_micro, BF16)),

time: 152 us -> 152 us (level)
  waiting for transfers between devices: 31.4 us -> 27.2 us
  starting transfers between devices: 46.1 us -> 48.2 us
    ppermute x2, waiting for transfers between devices: 7.84 us -> 4.13 us  [from_chips_above(): lax.ppermute(value, 'section', [(s, s - 2 * chips) for s in range(2 * chi...]
    all_to_all x1, starting transfers between devices: 10.9 us -> 12.6 us  [section_y_exchange(): lax.all_to_all(spread, ('section', 'tensor'), 0, 0, axis_index_groups=gro...]
    pallas_call x7 -> x8, Pallas kernels: 12.4 us -> 13.6 us  [call(): pl.pallas_call(body, out_shape=out_shape, in_specs=specs, out_specs=jax.t...]
  transfers between devices with their start and end apart: 11 -> 11, of which waited for: 9 -> 9; matrix products, arithmetic and copies ran while one was open for 1% -> 2% of each run, Pallas kernels for 7% -> 8%
where the time goes in v11:
time: 152 us
  starting transfers between devices  48.2 us (32%)
  blocking collectives  42.4 us (28%)
  waiting for transfers between devices  27.2 us (18%)
  between operations  15.7 us (10%)
  Pallas kernels  13.6 us (9%)
  local copies, waits for them, and re-layouts  3.04 us (2%)
  other arithmetic  1.74 us (1%)
    all_to_all x1, blocking collectives, y_exchange(): return lax.all_to_all(spread, 'tensor', 0, 0, axis_index_groups=y_groups())  24.7 us
    all_to_all x1, blocking collectives, z_exchange(): return lax.all_to_all(spread, 'tensor', 0, 0, axis_index_groups=z_groups())  17.8 us
    all_to_all x1, starting transfers between devices, z_exchange(): return lax.all_to_all(spread, 'tensor', 0, 0, axis_index_groups=z_groups())  15.6 us
    pallas_call x8, Pallas kernels, call(): pl.pallas_call(body, out_shape=out_shape, in_specs=specs, out_specs=jax.t...  13.6 us
    all_to_all x1, starting transfers between devices, section_y_exchange(): lax.all_to_all(spread, ('section', 'tensor'), 0, 0, axis_index_groups=gro...  12.6 us
    all_to_all x1, waiting for transfers between devices, z_exchange(): return lax.all_to_all(spread, 'tensor', 0, 0, axis_index_groups=z_groups())  11.4 us
    ppermute x3, starting transfers between devices, from_y(): return lax.ppermute(value, 'tensor', perm)  9.5 us
    ppermute x2, starting transfers between devices, from_other_core(): return lax.ppermute(value, 'section', [(s, s ^ 1) for s in range(NS)])  7.88 us
  transfers between devices with their start and end apart: 11, of which 9 were waited for; matrix products, arithmetic and copies ran while one was open for 2% of the time, Pallas kernels for 8%

profile of v11, /device:TPU:1, one launch (start us, length us, event | category | flops | bytes accessed | tf_op | source)
XLA Modules:
  0.0 151.9 jit_solution(7601085378085587890)
XLA Ops:
  8.0 0.0 copy-start.5
  8.0 0.0 copy-start.8
  8.0 0.0 copy-start.9
  8.0 2.2 %shard_map.77 = bf16[4,32,2176]{2,1,0:T(8,128)(2,1)} custom-call(s32[1,2]{1,0:T(1,128)} %plan.1, bf16[32,2048]{1,0:T(8,128)(2,1)} %bitcast.17, bf16[2,256,512]{2,1,0:T(8,128)(2,1)} %bitcast.23), custom_call_target="tpu_custom_call" | custom-call | tf_op jit(solution)/shard_map/pallas_call | solution.py:65
  10.2 15.6 %all-to-all-start = ((bf16[4,32,2176]{2,1,0:T(8,128)(2,1)}), bf16[4,32,2176]{2,1,0:T(8,128)(2,1)S(1)}, u32[]{:S(2)}, u32[]{:S(2)}) async-start(bf16[4,32,2176]{2,1,0:T(8,128)(2,1)} %shard_map.77), calls=%async_computation | async-start | bytes 1114112 | tf_op jit(solution)/shard_map/all_to_all | solution.py:52
  25.8 0.0 copy-done.5
  25.8 4.6 %collective-permute-start = (bf16[32,2048]{1,0:T(8,128)(2,1)S(1)}, bf16[32,2048]{1,0:T(8,128)(2,1)S(1)}, u32[]{:S(2)}, u32[]{:S(2)}) collective-permute-start(bf16[32,2048]{1,0:T(8,128)(2,1)S(1)} %bitcast.18), channel_id=1, source_target_pairs={{16,0},{20,4},{24,8},{28,12},{32,16},{36,20},{40,24},{44,28},{48,3... | collective-permute-start | bytes 393224 | tf_op jit(solution)/shard_map/ppermute | solution.py:31
  30.5 2.3 %collective-permute-start.1 = (bf16[32,2048]{1,0:T(8,128)(2,1)S(1)}, bf16[32,2048]{1,0:T(8,128)(2,1)S(1)}, u32[]{:S(2)}, u32[]{:S(2)}) collective-permute-start(bf16[32,2048]{1,0:T(8,128)(2,1)S(1)} %bitcast.19), channel_id=1, source_target_pairs={{32,0},{36,4},{40,8},{44,12},{48,16},{52,20},{56,24},{60,28},{0,32... | collective-permute-start | bytes 393224 | tf_op jit(solution)/shard_map/ppermute | solution.py:31
  32.8 2.6 %collective-permute-start.2 = (bf16[32,2048]{1,0:T(8,128)(2,1)S(1)}, bf16[32,2048]{1,0:T(8,128)(2,1)S(1)}, u32[]{:S(2)}, u32[]{:S(2)}) collective-permute-start(bf16[32,2048]{1,0:T(8,128)(2,1)S(1)} %bitcast.20), channel_id=1, source_target_pairs={{48,0},{52,4},{56,8},{60,12},{0,16},{4,20},{8,24},{12,28},{16,32},... | collective-permute-start | bytes 393224 | tf_op jit(solution)/shard_map/ppermute | solution.py:31
  35.4 0.0 copy-done.9
  35.4 0.9 reverse_select_fusion.saved
  36.3 0.0 collective-permute-done.own1
  36.3 1.7 %collective-permute-done.1.own2 = bf16[32,2048]{1,0:T(8,128)(2,1)S(1)} collective-permute-done((bf16[32,2048]{1,0:T(8,128)(2,1)S(1)}, bf16[32,2048]{1,0:T(8,128)(2,1)S(1)}, u32[]{:S(2)}, u32[]{:S(2)}) %collective-permute-start.1) | collective-permute-done | bytes 131104 | tf_op jit(solution)/shard_map/ppermute | solution.py:31
  38.0 3.5 %collective-permute-done.2.own3 = bf16[32,2048]{1,0:T(8,128)(2,1)S(1)} collective-permute-done((bf16[32,2048]{1,0:T(8,128)(2,1)S(1)}, bf16[32,2048]{1,0:T(8,128)(2,1)S(1)}, u32[]{:S(2)}, u32[]{:S(2)}) %collective-permute-start.2) | collective-permute-done | bytes 131104 | tf_op jit(solution)/shard_map/ppermute | solution.py:31
  41.5 11.4 %all-to-all-done.kv_ref = bf16[4,32,2176]{2,1,0:T(8,128)(2,1)S(1)} async-done(((bf16[4,32,2176]{2,1,0:T(8,128)(2,1)}), bf16[4,32,2176]{2,1,0:T(8,128)(2,1)S(1)}, u32[]{:S(2)}, u32[]{:S(2)}) %all-to-all-start) | async-done | bytes 557088 | tf_op jit(solution)/shard_map/all_to_all | solution.py:52
  52.9 0.0 all-gather.3.cloned.1.call-update
  52.9 0.0 reduce-scatter.2.cloned.1.call-start
  53.0 0.1 pad_add_fusion.place
  53.1 0.7 shard_map.78
  53.8 0.0 copy-start
  53.8 0.0 copy-start.1
  53.8 0.0 copy-start.7
  53.8 24.7 %all_to_all.20.others = bf16[4,96,2176]{2,1,0:T(8,128)(2,1)S(1)} all-to-all(bf16[4,96,2176]{2,1,0:T(8,128)(2,1)S(1)} %shard_map.78), channel_id=1, replica_groups={{0,16,32,48},{4,20,36,52},{8,24,40,56},{12,28,44,60},{1,17,33,49},{5,21..., dimensions={0} | all-to-all | bytes 3342336 | tf_op jit(solution)/shard_map/all_to_all | solution.py:48
  78.5 0.0 copy-done.1
  78.5 2.6 %shard_map.79 = (f32[512,512]{1,0:T(8,128)S(1)}, bf16[512,512]{1,0:T(8,128)(2,1)S(1)}, f32[4,4,128]{2,1,0:T(4,128)S(1)}, f32[4,128]{1,0:T(4,128)S(1)}) custom-call(s32[4]{0:T(128)S(1)} %pad_add_fusion.place, bf16[32,2048]{1,0:T(8,128)(2,1)S(1)} %bitcast.21, bf16[32,2048]{1,0:T(8,128)(2,1)S(1)} %collective-permute-done.own1, ...), custom_call_target="tpu_custom_call" | custom-call | flops 1073741824 | bytes 6291456 | tf_op jit(solution)/shard_map/pallas_call | solution.py:65
  81.1 3.4 %shard_map.84 = bf16[4,512,512]{2,1,0:T(8,128)(2,1)} custom-call(s32[4]{0:T(128)S(1)} %pad_add_fusion.place, bf16[32,2048]{1,0:T(8,128)(2,1)S(1)} %bitcast.22, bf16[32,2048]{1,0:T(8,128)(2,1)S(1)} %collective-permute-done.own1, bf16[32,2048]{1,0:T(8,128)(2,1)S(1)} %collective-permute-done.1.own2, bf16[32,2048]{1,0:T(8,128)(2,1)S(1)} %collective-permute-done.2.own3, ...), custom_call_target="tpu_custom_call" | custom-call | flops 1073741824 | bytes 6291456 | tf_op jit(solution)/shard_map/pallas_call | solution.py:65
  84.5 0.0 reduce-scatter.2.cloned.1.call-update
  84.5 4.1 %collective-permute-start.3 = (bf16[512,512]{1,0:T(8,128)(2,1)S(1)}, bf16[512,512]{1,0:T(8,128)(2,1)S(1)}, u32[]{:S(2)}, u32[]{:S(2)}) collective-permute-start(bf16[512,512]{1,0:T(8,128)(2,1)S(1)} %get-tuple-element.32), channel_id=1, source_target_pairs={{0,64},{64,0},{128,192},{192,128},{256,320},{320,256},{384,448},{4... | collective-permute-start | bytes 1572872 | tf_op jit(solution)/shard_map/ppermute | solution.py:40
  88.6 1.5 collective-permute-done.3.other
  90.1 0.6 shard_map.80
  90.7 0.8 copy-done.3
  91.5 1.3 collective-permute-start.4
  92.8 17.8 %all_to_all.21 = f32[4,4,128]{2,1,0:T(4,128)S(1)} all-to-all(f32[4,4,128]{2,1,0:T(4,128)S(1)} %get-tuple-element.33), channel_id=1, replica_groups={{0,4,8,12},{16,20,24,28},{32,36,40,44},{48,52,56,60},{1,5,9,13},{17,21,..., dimensions={0} | all-to-all | bytes 16384 | tf_op jit(solution)/shard_map/all_to_all | solution.py:52
  110.6 0.7 collective-permute-done.4.above1
  111.2 0.8 add_convert_fusion
  112.0 1.3 collective-permute-start.5
  113.3 0.1 all-gather.3.cloned.1.call-done
  113.4 0.6 broadcast_in_dim.6
  114.1 12.6 %all-to-all-start.3 = ((f32[16,4,128]{2,1,0:T(4,128)}), f32[16,4,128]{2,1,0:T(4,128)S(1)}, u32[]{:S(2)}, u32[]{:S(2)}) async-start(f32[16,4,128]{2,1,0:T(4,128)} %broadcast_in_dim.6), calls=%async_computation.3 | async-start | bytes 65536 | tf_op jit(solution)/shard_map/all_to_all | solution.py:61
  126.6 1.6 %copy-done.2 = bf16[8,256,512]{2,1,0:T(8,128)(2,1)S(1)} copy-done((bf16[8,256,512]{2,1,0:T(8,128)(2,1)S(1)}, bf16[8,256,512]{2,1,0:T(8,128)(2,1)}, u32[]{:S(2)}) %copy-start.2) | copy-done | bytes 2097176
  128.2 0.7 shard_map.81.saved
  128.9 3.5 %collective-permute-done.5.above2 = bf16[256,512]{1,0:T(8,128)(2,1)} collective-permute-done((bf16[256,512]{1,0:T(8,128)(2,1)}, bf16[256,512]{1,0:T(8,128)(2,1)}, u32[]{:S(2)}, u32[]{:S(2)}) %collective-permute-start.5) | collective-permute-done | bytes 262176 | tf_op jit(solution)/shard_map/ppermute | solution.py:44
  132.4 3.2 %all-to-all-done.3.parts = f32[16,4,128]{2,1,0:T(4,128)S(1)} async-done(((f32[16,4,128]{2,1,0:T(4,128)}), f32[16,4,128]{2,1,0:T(4,128)S(1)}, u32[]{:S(2)}, u32[]{:S(2)}) %all-to-all-start.3) | async-done | bytes 32800 | tf_op jit(solution)/shard_map/all_to_all | solution.py:61
  135.6 1.8 %shard_map.82 = (f32[2,256,512]{2,1,0:T(8,128)S(1)}, bf16[2,256,512]{2,1,0:T(8,128)(2,1)S(1)}) custom-call(s32[4]{0:T(128)S(1)} %pad_add_fusion.place, bf16[4,2,256,512]{3,2,1,0:T(8,128)(2,1)S(1)} %shard_map.81.saved, f32[16,4,128]{2,1,0:T(4,128)S(1)} %all-to-all-done.3.parts, bf16[256,512]{1,0:T(8,128)(2,1)S(1)} %collective-permute-done.4.above1, ...), custom_call_target="tpu_custom_call" | custom-call | tf_op jit(solution)/shard_map/pallas_call | solution.py:65
  137.5 3.8 %collective-permute-start.6 = (bf16[2,256,512]{2,1,0:T(8,128)(2,1)S(1)}, bf16[2,256,512]{2,1,0:T(8,128)(2,1)S(1)}, u32[]{:S(2)}, u32[]{:S(2)}) collective-permute-start(bf16[2,256,512]{2,1,0:T(8,128)(2,1)S(1)} %get-tuple-element.40), channel_id=1, source_target_pairs={{0,64},{64,0},{128,192},{192,128},{256,320},{320,256},{384,448},{4... | collective-permute-start | bytes 1572872 | tf_op jit(solution)/shard_map/ppermute | solution.py:40
  141.3 1.5 collective-permute-done.6.got
  142.8 0.0 copy-done.4
  142.8 1.6 %shard_map.83 = bf16[2,256,512]{2,1,0:T(8,128)(2,1)} custom-call(s32[4]{0:T(128)S(1)} %pad_add_fusion.place, f32[2,256,512]{2,1,0:T(8,128)S(1)} %get-tuple-element.39.kept, bf16[2,256,512]{2,1,0:T(8,128)(2,1)S(1)} %collective-permute-done.6.got, f32[2,256,512]{2,1,0:T(8,128)S(1)} %bitcast.13, bf16[2,256,512]{2,1,0:T(8,128)(2,1)S(1)} %bitcast.16, ...), custom_call_target="tpu_custom_call" | custom-call | tf_op jit(solution)/shard_map/pallas_call | solution.py:65
  (11 shorter events, 0.0 us)
Async XLA Ops:
  8.0 17.8 %copy-start.5 = (bf16[1,2,16,2048]{3,2,1,0:T(8,128)(2,1)S(1)}, bf16[1,2,16,2048]{3,2,1,0:T(8,128)(2,1)}, u32[]{:S(2)}) copy-start(bf16[1,2,16,2048]{3,2,1,0:T(8,128)(2,1)} %param.10) | copy-start | bytes 393220
  8.0 27.4 %copy-start.8 = (bf16[1,2,256,512]{3,2,1,0:T(8,128)(2,1)S(1)}, bf16[1,2,256,512]{3,2,1,0:T(8,128)(2,1)}, u32[]{:S(2)}) copy-start(bf16[1,2,256,512]{3,2,1,0:T(8,128)(2,1)} %param.7) | copy-start | bytes 1572868
  8.0 27.4 %copy-start.9 = (s32[1,2]{1,0:T(1,128)S(1)}, s32[1,2]{1,0:T(1,128)}, u32[]{:S(2)}) copy-start(s32[1,2]{1,0:T(1,128)} %plan.1) | copy-start | bytes 28
  10.2 42.7 %all-to-all-start = ((bf16[4,32,2176]{2,1,0:T(8,128)(2,1)}), bf16[4,32,2176]{2,1,0:T(8,128)(2,1)S(1)}, u32[]{:S(2)}, u32[]{:S(2)}) async-start(bf16[4,32,2176]{2,1,0:T(8,128)(2,1)} %shard_map.77), calls=%async_computation | async-start | bytes 1114112 | tf_op jit(solution)/shard_map/all_to_all | solution.py:52
  25.8 87.6 %all-gather.3.cloned.1.call-start = ((), (), s32[]{:S(2)}) async-start(), calls=%async_computation.6 | async-start | bytes 2621440 | tf_op jit(solution)/shard_map/all_gather | solution.py:257
  25.8 10.5 %collective-permute-start = (bf16[32,2048]{1,0:T(8,128)(2,1)S(1)}, bf16[32,2048]{1,0:T(8,128)(2,1)S(1)}, u32[]{:S(2)}, u32[]{:S(2)}) collective-permute-start(bf16[32,2048]{1,0:T(8,128)(2,1)S(1)} %bitcast.18), channel_id=1, source_target_pairs={{16,0},{20,4},{24,8},{28,12},{32,16},{36,20},{40,24},{44,28},{48,3... | collective-permute-start | bytes 393224 | tf_op jit(solution)/shard_map/ppermute | solution.py:31
  30.5 7.5 %collective-permute-start.1 = (bf16[32,2048]{1,0:T(8,128)(2,1)S(1)}, bf16[32,2048]{1,0:T(8,128)(2,1)S(1)}, u32[]{:S(2)}, u32[]{:S(2)}) collective-permute-start(bf16[32,2048]{1,0:T(8,128)(2,1)S(1)} %bitcast.19), channel_id=1, source_target_pairs={{32,0},{36,4},{40,8},{44,12},{48,16},{52,20},{56,24},{60,28},{0,32... | collective-permute-start | bytes 393224 | tf_op jit(solution)/shard_map/ppermute | solution.py:31
  32.8 8.7 %collective-permute-start.2 = (bf16[32,2048]{1,0:T(8,128)(2,1)S(1)}, bf16[32,2048]{1,0:T(8,128)(2,1)S(1)}, u32[]{:S(2)}, u32[]{:S(2)}) collective-permute-start(bf16[32,2048]{1,0:T(8,128)(2,1)S(1)} %bitcast.20), channel_id=1, source_target_pairs={{48,0},{52,4},{56,8},{60,12},{0,16},{4,20},{8,24},{12,28},{16,32},... | collective-permute-start | bytes 393224 | tf_op jit(solution)/shard_map/ppermute | solution.py:31
  52.9 91.5 %reduce-scatter.2.cloned.1.call-start = ((), (), s32[]{:S(2)}) async-start(), calls=%async_computation.5 | async-start | bytes 2621440 | tf_op jit(solution)/shard_map/reduce_scatter | solution.py:294
  53.8 24.7 %copy-start = (bf16[2,256,512]{2,1,0:T(8,128)(2,1)S(1)}, bf16[2,256,512]{2,1,0:T(8,128)(2,1)}, u32[]{:S(2)}) copy-start(bf16[2,256,512]{2,1,0:T(8,128)(2,1)} %reverse_select_fusion.saved) | copy-start | bytes 1572868
  53.8 24.7 %copy-start.1 = (bf16[1,512,2048]{2,1,0:T(8,128)(2,1)S(1)}, bf16[1,512,2048]{2,1,0:T(8,128)(2,1)}, u32[]{:S(2)}) copy-start(bf16[1,512,2048]{2,1,0:T(8,128)(2,1)} %param.9) | copy-start | bytes 6291460
  53.8 24.7 %copy-start.7 = (bf16[1,512]{1,0:T(2,128)(2,1)S(1)}, bf16[1,512]{1,0:T(2,128)(2,1)}, u32[]{:S(2)}) copy-start(bf16[1,512]{1,0:T(2,128)(2,1)} %gains.3) | copy-start | bytes 3076
  84.5 5.6 %collective-permute-start.3 = (bf16[512,512]{1,0:T(8,128)(2,1)S(1)}, bf16[512,512]{1,0:T(8,128)(2,1)S(1)}, u32[]{:S(2)}, u32[]{:S(2)}) collective-permute-start(bf16[512,512]{1,0:T(8,128)(2,1)S(1)} %get-tuple-element.32), channel_id=1, source_target_pairs={{0,64},{64,0},{128,192},{192,128},{256,320},{320,256},{384,448},{4... | collective-permute-start | bytes 1572872 | tf_op jit(solution)/shard_map/ppermute | solution.py:40
  90.7 0.8 copy-start.3
  91.5 19.7 %collective-permute-start.4 = (bf16[256,512]{1,0:T(8,128)(2,1)S(1)}, bf16[256,512]{1,0:T(8,128)(2,1)S(1)}, u32[]{:S(2)}, u32[]{:S(2)}) collective-permute-start(bf16[256,512]{1,0:T(8,128)(2,1)S(1)} %shard_map.80), channel_id=1, source_target_pairs={{128,0},{192,64},{256,128},{320,192},{384,256},{448,320},{129,1},{... | collective-permute-start | bytes 786440 | tf_op jit(solution)/shard_map/ppermute | solution.py:44
  112.0 20.4 %collective-permute-start.5 = (bf16[256,512]{1,0:T(8,128)(2,1)}, bf16[256,512]{1,0:T(8,128)(2,1)}, u32[]{:S(2)}, u32[]{:S(2)}) collective-permute-start(bf16[256,512]{1,0:T(8,128)(2,1)} %add_convert_fusion), channel_id=1, source_target_pairs={{256,0},{320,64},{384,128},{448,192},{257,1},{321,65},{385,129},{4... | collective-permute-start | bytes 786440 | tf_op jit(solution)/shard_map/ppermute | solution.py:44
  114.1 21.5 %all-to-all-start.3 = ((f32[16,4,128]{2,1,0:T(4,128)}), f32[16,4,128]{2,1,0:T(4,128)S(1)}, u32[]{:S(2)}, u32[]{:S(2)}) async-start(f32[16,4,128]{2,1,0:T(4,128)} %broadcast_in_dim.6), calls=%async_computation.3 | async-start | bytes 65536 | tf_op jit(solution)/shard_map/all_to_all | solution.py:61
  126.6 1.6 %copy-start.2 = (bf16[8,256,512]{2,1,0:T(8,128)(2,1)S(1)}, bf16[8,256,512]{2,1,0:T(8,128)(2,1)}, u32[]{:S(2)}) copy-start(bf16[8,256,512]{2,1,0:T(8,128)(2,1)} %all-gather.3.cloned.1.call-done) | copy-start | bytes 6291460
  135.6 7.2 %copy-start.4 = (bf16[512,512]{1,0:T(8,128)(2,1)S(1)}, bf16[512,512]{1,0:T(8,128)(2,1)}, u32[]{:S(2)}) copy-start(bf16[512,512]{1,0:T(8,128)(2,1)} %copy-done.3) | copy-start | bytes 1572868
  135.6 7.2 %copy-start.6 = (bf16[2,256,512]{2,1,0:T(8,128)(2,1)S(1)}, bf16[2,256,512]{2,1,0:T(8,128)(2,1)}, u32[]{:S(2)}) copy-start(bf16[2,256,512]{2,1,0:T(8,128)(2,1)} %top.1) | copy-start | bytes 1572868
  137.5 5.3 %collective-permute-start.6 = (bf16[2,256,512]{2,1,0:T(8,128)(2,1)S(1)}, bf16[2,256,512]{2,1,0:T(8,128)(2,1)S(1)}, u32[]{:S(2)}, u32[]{:S(2)}) collective-permute-start(bf16[2,256,512]{2,1,0:T(8,128)(2,1)S(1)} %get-tuple-element.40), channel_id=1, source_target_pairs={{0,64},{64,0},{128,192},{192,128},{256,320},{320,256},{384,448},{4... | collective-permute-start | bytes 1572872 | tf_op jit(solution)/shard_map/ppermute | solution.py:40
Sparse Core Ops, SparseCore 0:
  53.1 60.3 all-gather.2
Sparse Core Ops, SparseCore 1:
  84.6 35.6 reduce-scatter.1
